TPU v7x, 32 devices: a whole 2x2x4 slice. The times are simulated.
32 devices in a mesh: section: 4 (over y, x), shard: 8 (over z, core).
Axes of the slice: x: 2, y: 2, z: 4, core: 2. Of those that a mesh axis runs over, the one named last changes fastest.
Arguments:
- voltages: bfloat16 [4, 2, 1024, 32768], P('section', None, 'shard'), may hold values from -30 to 30, as said below
- feed_gains: bfloat16 [2, 1024, 1024], P(None, 'shard'), may hold values from -6 to 6
- grid_index: int32 [1024], replicated, may hold values from 0 to 1023, each once
- decay_rates: float32 [1024], P('shard'), may hold values from 0.3 to 0.95
- delays: int32 [1024, 512], replicated, may hold values from 0 to 4095
Outputs:
- dedispersed: bfloat16 [4, 7, 512, 2, 1024], P('section', None, None, None, 'shard')
Inputs may be any that keep to these rules, and one draw needn't show every extreme that they name: Real sample voltages.
All inputs are finite; a program needn't handle non-finite values.
Results may differ from a plain program's by a relative error of at most 0.009.
Values may be sent and summed in bfloat16 or wider, within the bound.
No kernel may reach another device: no remote copies, remote signals or barrier semaphores. Data moves between devices by JAX's collectives and lax.ppermute only.
A program may use at most 192 MiB of HBM per device.

v0:
```python
import math

import jax
import jax.numpy as jnp
import numpy as np
from jax import lax
from jax.sharding import PartitionSpec as P

POL = 2
GRID_X = 4
GRID_Y = 256
NSAMP = 2048
TDFT = 16
FEEDS = 1024
CHANS = 1024
MODF = 7


def carried_in(part, axis, combine, identity):
    place = lax.axis_index(axis)
    gathered = jax.tree.map(lambda a: lax.all_gather(a, axis), part)
    state = jax.tree.map(lambda a, e: jnp.zeros_like(a) + jnp.asarray(e, a.dtype), part, identity)

    def one(lap, state):
        return combine(
            state, jax.tree.map(lambda a: lax.dynamic_index_in_dim(a, lap, 0, False), gathered)
        )

    return lax.fori_loop(0, place, one, state)


def spectral_constant():
    row_index = np.arange(CHANS, dtype=np.int64)[:, None]
    col_index = np.arange(NSAMP, dtype=np.int64)[None, :]
    angles = np.float32(2.0 * math.pi / NSAMP) * (row_index * col_index % NSAMP).astype(np.float32)
    table = np.concatenate([np.cos(angles), -np.sin(angles)], 0).astype(np.float32)
    return jnp.asarray(table).astype(jnp.bfloat16)


def twiddle_table(length):
    row_index = jnp.arange(length, dtype=jnp.int32)[:, None]
    col_index = jnp.arange(length, dtype=jnp.int32)[None, :]
    angles = 2.0 * math.pi / length * (row_index * col_index % length).astype(jnp.float32)
    cosine = jnp.cos(angles)
    sine_part = jnp.sin(angles)
    return jnp.stack([jnp.stack([cosine, -sine_part], 1), jnp.stack([sine_part, cosine], 1)], 0)


def frame_table():
    frames = jnp.arange(TDFT, dtype=jnp.int32)[:, None]
    freqs = jnp.arange(1, MODF + 1, dtype=jnp.int32)[None, :]
    angles = 2.0 * math.pi / TDFT * (frames * freqs % TDFT).astype(jnp.float32)
    return jnp.concatenate([jnp.cos(angles), -jnp.sin(angles)], 1) / math.sqrt(TDFT)


def form_beams(transposed_block, feed_gains, cell_feed):
    chan_count = transposed_block.shape[1]
    pol_count = transposed_block.shape[2]
    values = transposed_block.reshape(2, chan_count, pol_count, FEEDS, TDFT).astype(jnp.float32)
    gain_values = feed_gains.astype(jnp.float32)[:, :, None, :, None]
    real_part = gain_values[0] * values[0] - gain_values[1] * values[1]
    imag_part = gain_values[0] * values[1] + gain_values[1] * values[0]
    calibrated = jnp.stack([real_part, imag_part]).astype(jnp.bfloat16)
    gridded = jnp.take(calibrated, cell_feed, axis=3).reshape(
        2, chan_count, pol_count, GRID_X, GRID_Y, TDFT
    )
    rows = twiddle_table(GRID_Y).astype(jnp.bfloat16)
    row_beams = jnp.einsum("acpxyn,aybw->bcpxwn", gridded, rows, preferred_element_type=jnp.float32)
    beam_voltage = jnp.einsum(
        "bcpxwn,bxeu->ecpnuw", row_beams, twiddle_table(GRID_X), precision=lax.Precision.HIGHEST
    )
    powers = jnp.sum(beam_voltage * beam_voltage, axis=0)
    return jnp.moveaxis(powers, 1, 0).reshape(pol_count, chan_count, TDFT, FEEDS)


def dedisperse(freq_major, delays):
    residues = delays % TDFT
    contract = (((0,), (0,)), ((), ()))

    def per_frequency(position_index):
        frequency = position_index + 1
        angles = 2.0 * math.pi / TDFT * (frequency * residues % TDFT).astype(jnp.float32)
        cosine_part = jnp.cos(angles).astype(jnp.bfloat16)
        sine_part = jnp.sin(angles).astype(jnp.bfloat16)
        mod_real = freq_major[position_index]
        mod_imag = freq_major[MODF + position_index]
        real_out = lax.dot_general(
            cosine_part, mod_real, contract, preferred_element_type=jnp.float32
        ) + lax.dot_general(sine_part, mod_imag, contract, preferred_element_type=jnp.float32)
        imag_out = lax.dot_general(
            cosine_part, mod_imag, contract, preferred_element_type=jnp.float32
        ) - lax.dot_general(sine_part, mod_real, contract, preferred_element_type=jnp.float32)
        result = jnp.stack([real_out, imag_out], 1) / math.sqrt(CHANS)
        return result.astype(jnp.bfloat16)

    return lax.map(per_frequency, jnp.arange(MODF, dtype=jnp.int32))


def combine(earlier, later):
    return (
        earlier[0] * later[0],
        later[0] * earlier[1] + later[1],
        later[0] * earlier[2] + later[2],
    )


def shards(voltages, feed_gains, grid_index, decay_rates, delays):
    cell_feed = (
        jnp.zeros((FEEDS,), jnp.int32).at[grid_index].set(jnp.arange(FEEDS, dtype=jnp.int32))
    )
    local_feeds = voltages.shape[2]
    samples = voltages[0].reshape(POL * local_feeds * TDFT, NSAMP)
    spectra = lax.dot_general(
        spectral_constant(), samples, (((1,), (1,)), ((), ())), preferred_element_type=jnp.float32
    )
    spectra = (
        (spectra * (1.0 / math.sqrt(NSAMP)))
        .astype(jnp.bfloat16)
        .reshape(2, CHANS, POL, local_feeds * TDFT)
    )
    turned = lax.all_to_all(spectra, "shard", split_axis=1, concat_axis=3, tiled=True)
    per_pol = form_beams(turned, feed_gains, cell_feed)
    beam_power = jnp.sum(per_pol, axis=0)
    levels = jnp.mean(beam_power, axis=(1, 2)) + 1e-06
    unity = jnp.ones_like(levels)
    nothing = jnp.zeros_like(levels)
    prefix = carried_in((decay_rates, levels, unity), "section", combine, (unity, nothing, nothing))
    baseline_level = (decay_rates * prefix[1] + levels) / (decay_rates * prefix[2] + 1.0)
    normalized = beam_power / baseline_level[:, None, None] - 1.0
    modulated = jnp.einsum(
        "cnb,nq->cbq", normalized, frame_table(), precision=lax.Precision.HIGHEST
    ).astype(jnp.bfloat16)
    flattened = modulated.reshape(modulated.shape[0], FEEDS * 2 * MODF)
    moved = lax.all_to_all(flattened, "shard", split_axis=1, concat_axis=0, tiled=True)
    local_beams = FEEDS // lax.axis_size("shard")
    gathered = moved.reshape(CHANS, local_beams, 2 * MODF)
    freq_major = jnp.transpose(gathered, (2, 0, 1))
    return dedisperse(freq_major, delays)[None]


def solution(mesh):
    in_specs = (P("section", None, "shard", None), P(None, "shard", None), P(), P("shard"), P())
    out_specs = P("section", None, None, None, "shard")
    return jax.shard_map(shards, mesh=mesh, in_specs=in_specs, out_specs=out_specs, check_vma=False)
```

profile of v0, /device:TPU:0, one launch (start us, length us, event | category | flops | bytes accessed | tf_op | source)
XLA Modules:
  0.0 1237.8 jit_solution(16668400238170787444)
XLA Ops:
  0.0 25.7 %reshape_squeeze.3 = bf16[4096,2048]{1,0:T(8,128)(2,1)} reshape(bf16[1,2,128,32768]{3,2,1,0:T(8,128)(2,1)} %param.10) | data formatting | bytes 33554432 | tf_op jit(solution)/shard_map/reshape;squeeze | solution.py:112
  25.7 42.1 %multiply_convert_fusion = bf16[2048,4096]{1,0:T(8,128)(2,1)} fusion(bf16[2048,2048]{1,0:T(8,128)(2,1)} %constant.186, bf16[4096,2048]{1,0:T(8,128)(2,1)} %reshape_squeeze.3), kind=kOutput, calls=%fused_computation.40 | convolution fusion | flops 34376515584 | bytes 41943040 | tf_op jit(solution)/shard_map/dot_general | solution.py:113
  67.7 27.8 %reshape.245 = bf16[2,1024,2,2048]{3,2,1,0:T(2,128)(2,1)} reshape(bf16[2048,4096]{1,0:T(8,128)(2,1)} %multiply_convert_fusion) | data formatting | bytes 33554432 | tf_op jit(solution)/shard_map/reshape | solution.py:119
  95.5 20.5 %copy.36 = bf16[2,1024,2,2048]{3,2,0,1:T(2,128)(2,1)} copy(bf16[2,1024,2,2048]{3,2,1,0:T(2,128)(2,1)} %reshape.245) | data formatting | bytes 33554432 | tf_op jit(solution)/shard_map/reshape | solution.py:119
  128.5 9.3 all-gather.2
  142.1 344.3 %all-to-all-done = bf16[2,1024,2,2048]{3,2,0,1:T(2,128)(2,1)} async-done(((bf16[2,1024,2,2048]{3,2,0,1:T(2,128)(2,1)}), bf16[2,1024,2,2048]{3,2,0,1:T(2,128)(2,1)}, u32[]{:S(2)}, u32[]{:S(2)}) %all-to-all-start) | async-done | bytes 16777248 | tf_op jit(solution)/shard_map/all_to_all | solution.py:121
  486.4 12.2 copy.37
  498.5 11.4 convert_bitcast_fusion
  509.9 21.2 %fusion.86 = (f32[1,128,2,8,2048]{4,1,3,2,0:T(8,128)}, f32[1,128,2,8,2048]{4,1,3,2,0:T(8,128)}) fusion(f32[2,128,2,8,2048]{4,1,3,2,0:T(8,128)} %convert_bitcast_fusion), kind=kLoop, calls=%fused_computation.128 | loop fusion | bytes 67108864 | tf_op jit(solution)/shard_map/slice | solution.py:61
  531.0 17.2 %copy.38 = f32[1,128,2,8,2048]{1,4,3,2,0:T(8,128)} copy(f32[1,128,2,8,2048]{4,1,3,2,0:T(8,128)} %get-tuple-element.197) | data formatting | bytes 33554432 | tf_op jit(solution)/shard_map/slice | solution.py:61
  548.3 17.3 %copy.40 = f32[1,128,2,8,2048]{1,4,3,2,0:T(8,128)} copy(f32[1,128,2,8,2048]{4,1,3,2,0:T(8,128)} %get-tuple-element.196) | data formatting | bytes 33554432 | tf_op jit(solution)/shard_map/slice | solution.py:61
  565.5 12.0 subtract_convert_fusion
  584.3 20.3 %gather_fusion = bf16[1024,2,128,2,16]{2,4,3,1,0:T(8,128)(2,1)} fusion(bf16[2,128,2,1024,16]{1,4,3,2,0:T(8,128)(2,1)} %pad_maximum_fusion, s32[1024]{0:T(1024)S(1)} %fusion.69), kind=kCustom, calls=%fused_computation | custom fusion | bytes 33558528 | tf_op jit(solution)/shard_map/jit(_take)/gather | solution.py:64
  604.6 26.3 %copy.41 = bf16[2,128,2,4,256,16]{4,1,0,5,3,2:T(8,128)(2,1)} copy(bf16[2,128,2,4,256,16]{1,5,2,0,4,3:T(8,128)(2,1)} %bitcast.123) | data formatting | bytes 33554432 | tf_op jit(solution)/shard_map/jit(_take)/gather | solution.py:64
  630.9 19.8 %fusion.33 = f32[2,128,2,4,256,16]{1,4,5,3,2,0:T(8,128)} fusion(bf16[2,128,2,4,256,16]{4,1,0,5,3,2:T(8,128)(2,1)} %copy.41, pred[4,256]{1,0:T(4,128)(4,1)S(1)} %copy-done.11, bf16[1,256,2,256]{1,3,0,2:T(8,128)(2,1)S(1)} %copy-done.4, bf16[1,256,2,256]{1,3,0,2:T(8,128)(2,1)S(1)} %copy-done.3), kind=kOutput, calls=%fused_computation.50 | convolution fusion | flops 8599371776 | bytes 50856960 | tf_op jit(solution)/shard_map/acpxyn,aybw->bcpxwn/dot_general | solution.py:68
  650.8 39.2 %copy.42 = f32[2,128,2,4,256,16]{4,3,0,5,2,1:T(4,128)} copy(f32[2,128,2,4,256,16]{1,4,5,3,2,0:T(8,128)} %fusion.33) | data formatting | bytes 67108864 | tf_op jit(solution)/shard_map/acpxyn,aybw->bcpxwn/transpose | solution.py:68
  689.9 87.6 %fusion.27 = (f32[128]{0:T(128)S(1)}, f32[4,128,256,16]{2,0,3,1:T(4,128)}) fusion(f32[2,128,2,4,256,16]{4,3,0,5,2,1:T(4,128)} %copy.42, f32[2,4,2,4,1,1,1]{1,3,0,6,5,4,2:T(4,128)S(1)} %copy-done.5), kind=kOutput, calls=%fused_computation.41 | convolution fusion | flops 828374912 | bytes 41943808 | tf_op jit(solution)/shard_map/bcpxwn,bxeu->ecpnuw/dot_general | solution.py:69
  786.2 11.3 reduce_sum.28
  797.5 11.9 fusion.42
  830.5 80.6 %all-to-all-done.1 = bf16[128,8,1792]{0,2,1:T(8,128)(2,1)} async-done(((bf16[128,8,1792]{0,2,1:T(8,128)(2,1)}), bf16[128,8,1792]{0,2,1:T(8,128)(2,1)}, u32[]{:S(2)}, u32[]{:S(2)}) %all-to-all-start.1) | async-done | bytes 3670048 | tf_op jit(solution)/shard_map/all_to_all | solution.py:134
  911.1 12.2 copy.44
  937.3 300.1 %while.28 = (s32[]{:T(128)}, bf16[7,512,2,128]{3,2,1,0:T(2,128)(2,1)}, s32[7]{0:T(128)S(1)}, s32[1024,512]{1,0:T(8,128)S(1)}, bf16[14,1024,128]{2,1,0:T(8,128)(2...) while((s32[]{:T(128)}, bf16[7,512,2,128]{3,2,1,0:T(2,128)(2,1)}, s32[7]{0:T(128)S(1)}, ...), condition=%wide.region_6.7_spmd, body=%wide.region_5.6_spmd.sunk | while | flops 568852480 | bytes 12321517 | solution.py:96
  961.7 8.7 fusion.107
  971.4 8.8 fusion.108
  980.2 8.7 fusion.105
  988.9 8.8 fusion.106
  1011.2 8.8 fusion.108
  1020.0 8.7 fusion.105
  1028.7 8.8 fusion.106
  1041.2 8.7 fusion.107
  1051.0 8.8 fusion.108
  1059.8 8.7 fusion.105
  1068.5 8.8 fusion.106
  1081.0 8.7 fusion.107
  1090.8 8.8 fusion.108
  1099.5 8.7 fusion.105
  1108.2 8.8 fusion.106
  1120.8 8.7 fusion.107
  1130.6 8.8 fusion.108
  1139.3 8.7 fusion.105
  1148.0 8.8 fusion.106
  1170.3 8.8 fusion.108
  1179.1 8.7 fusion.105
  1187.8 8.8 fusion.106
  1200.3 8.7 fusion.107
  1210.1 8.8 fusion.108
  1218.9 8.7 fusion.105
  1227.6 8.8 fusion.106
  (84 shorter events, 95.5 us)
Async XLA Ops:
  116.0 6.5 copy-start.2
  116.0 370.3 %all-to-all-start = ((bf16[2,1024,2,2048]{3,2,0,1:T(2,128)(2,1)}), bf16[2,1024,2,2048]{3,2,0,1:T(2,128)(2,1)}, u32[]{:S(2)}, u32[]{:S(2)}) async-start(bf16[2,1024,2,2048]{3,2,0,1:T(2,128)(2,1)} %copy.36), calls=%async_computation | async-start | bytes 33554432 | tf_op jit(solution)/shard_map/all_to_all | solution.py:121
  122.5 0.7 copy-start.6
  122.5 6.0 copy-start.9
  604.6 26.3 %copy-start.3 = (bf16[1,256,2,256]{1,3,0,2:T(8,128)(2,1)S(1)}, bf16[1,256,2,256]{1,3,0,2:T(8,128)(2,1)}, u32[]{:S(2)}) copy-start(bf16[1,256,2,256]{1,3,0,2:T(8,128)(2,1)} %get-tuple-element.200) | copy-start | bytes 786436
  604.6 26.3 %copy-start.4 = (bf16[1,256,2,256]{1,3,0,2:T(8,128)(2,1)S(1)}, bf16[1,256,2,256]{1,3,0,2:T(8,128)(2,1)}, u32[]{:S(2)}) copy-start(bf16[1,256,2,256]{1,3,0,2:T(8,128)(2,1)} %get-tuple-element.201) | copy-start | bytes 786436
  604.6 26.3 %copy-start.11 = (pred[4,256]{1,0:T(4,128)(4,1)S(1)}, pred[4,256]{1,0:T(4,128)(4,1)}, u32[]{:S(2)}) copy-start(pred[4,256]{1,0:T(4,128)(4,1)} %broadcast_in_dim.38) | copy-start | bytes 3076
  650.7 39.2 %copy-start.5 = (f32[2,4,2,4,1,1,1]{1,3,0,6,5,4,2:T(4,128)S(1)}, f32[2,4,2,4,1,1,1]{1,3,0,6,5,4,2:T(4,128)}, u32[]{:S(2)}) copy-start(f32[2,4,2,4,1,1,1]{1,3,0,6,5,4,2:T(4,128)} %maximum_bitcast_fusion.5.clone.4) | copy-start | bytes 772
  786.1 11.3 copy-start.10
  786.1 11.3 copy-start.7
  786.1 11.3 copy-start.8
  823.5 4.8 copy-start
  823.5 87.6 %all-to-all-start.1 = ((bf16[128,8,1792]{0,2,1:T(8,128)(2,1)}), bf16[128,8,1792]{0,2,1:T(8,128)(2,1)}, u32[]{:S(2)}, u32[]{:S(2)}) async-start(bf16[128,8,1792]{0,2,1:T(8,128)(2,1)} %all_to_all.20), calls=%async_computation.1 | async-start | bytes 7340032 | tf_op jit(solution)/shard_map/all_to_all | solution.py:134
  930.6 6.7 copy-start.1
where the time goes:
time: 1250 us; the launch traced here: 1240 us
  waiting for transfers between devices  425 us (34%)
  matrix products  406 us (32%)
  local copies, waits for them, and re-layouts  295 us (24%)
  loops' own time  44.9 us (4%)
  other arithmetic  37.1 us (3%)
  blocking collectives  17.9 us (1%)
    all_to_all x1, waiting for transfers between devices, shards(): lax.all_to_all(spectra, 'shard', split_axis=1, concat_axis=3, tiled=True)  344 us
    dot_general x1, matrix products, form_beams(): jnp.einsum('bcpxwn,bxeu->ecpnuw', row_beams, twiddle_table(GRID_X), preci...  87.6 us
    all_to_all x1, waiting for transfers between devices, shards(): lax.all_to_all(flattened, 'shard', split_axis=1, concat_axis=0, tiled=True)  80.6 us
    dot_general x7, matrix products, per_frequency(): lax.dot_general(sine_part, mod_imag, contract, preferred_element_type=jnp...  61.3 us
    dot_general x7, matrix products, per_frequency(): lax.dot_general(sine_part, mod_real, contract, preferred_element_type=jnp...  61.3 us
    dot_general x7, matrix products, per_frequency(): lax.dot_general(cosine_part, mod_imag, contract, preferred_element_type=j...  60.8 us
    dot_general x7, matrix products, per_frequency(): lax.dot_general(cosine_part, mod_real, contract, preferred_element_type=j...  60.8 us
    slice x3, local copies, waits for them, and re-layouts, form_beams(): real_part = gain_values[0] * values[0] - gain_values[1] * values[1]  55.6 us
  transfers between devices with their start and end apart: 2, of which 2 were waited for; matrix products, arithmetic and copies ran while one was open for 1% of the time, Pallas kernels for 0%

commit v1 on v0

v1 whole, which is shorter than its diff:
```python
import functools
import math

import jax
import jax.numpy as jnp
import numpy as np
from jax import lax
from jax.experimental import pallas as pl
from jax.experimental.pallas import tpu as pltpu
from jax.sharding import PartitionSpec as P

POL = 2
GRID_X = 4
GRID_Y = 256
NSAMP = 2048
MODF = 7
LANES = 128
ROWS = 16


def spectral_constant(chans):
    row_index = np.arange(chans, dtype=np.int64)[:, None]
    col_index = np.arange(NSAMP, dtype=np.int64)[None, :]
    angles = np.float32(2.0 * math.pi / NSAMP) * (row_index * col_index % NSAMP).astype(np.float32)
    return np.stack([np.cos(angles), -np.sin(angles)], 0).astype(np.float32).astype(jnp.bfloat16)


def cosine_of(index, period):
    half, quarter = period // 2, period // 4
    folded = jnp.abs(((index + half) & (period - 1)) - half) - quarter
    x = folded.astype(jnp.float32) * np.float32(2.0 * math.pi / period)
    x2 = x * x
    series = np.float32(-1.0 / math.factorial(11))
    for order in (9, 7, 5, 3, 1):
        sign = 1.0 if order % 4 == 1 else -1.0
        series = series * x2 + np.float32(sign / math.factorial(order))
    return -x * series


def beam_table(grid_index):
    feeds = grid_index.shape[0]
    cell = jnp.concatenate([grid_index, grid_index])[:, None]
    part = lax.broadcasted_iota(jnp.int32, (2 * feeds, 1), 0) // feeds
    column = lax.broadcasted_iota(jnp.int32, (1, 2 * feeds), 1)
    end = (column // LANES) % 2
    beam = column // (2 * LANES) * LANES + column % LANES
    x, y = cell // GRID_Y, cell % GRID_Y
    u, w = beam // GRID_Y, beam % GRID_Y
    turn = y * w + (GRID_Y // GRID_X) * (x * u) + (GRID_Y // 4) * (end - part)
    return cosine_of(turn, GRID_Y).astype(jnp.bfloat16)


def frame_sums(frames):
    even = [frames[n] + frames[n + 8] for n in range(8)]
    odd = [frames[n] - frames[n + 8] for n in range(8)]
    ee = [even[n] + even[n + 4] for n in range(4)]
    ed = [even[n] - even[n + 4] for n in range(4)]
    real, imag = [None] * 8, [None] * 8
    real[4] = ee[0] - ee[2]
    imag[4] = ee[3] - ee[1]
    root = np.float32(math.sqrt(0.5))
    diff, total = root * (ed[1] - ed[3]), root * (ed[1] + ed[3])
    real[2], imag[2] = ed[0] + diff, -ed[2] - total
    real[6], imag[6] = ed[0] - diff, ed[2] - total
    minus = [None] + [odd[n] - odd[8 - n] for n in (1, 2, 3)]
    plus = [None] + [odd[n] + odd[8 - n] for n in (1, 2, 3)]
    for f in (1, 3, 5, 7):
        c = [np.float32(math.cos(math.pi * f * n / 8)) for n in range(4)]
        s = [np.float32(math.sin(math.pi * f * n / 8)) for n in range(5)]
        real[f] = odd[0] + (c[1] * minus[1] + c[2] * minus[2] + c[3] * minus[3])
        last = odd[4] if s[4] > 0 else -odd[4]
        imag[f] = -(last + (s[1] * plus[1] + s[2] * plus[2] + s[3] * plus[3]))
    return [np.float32(0.25) * v for v in real[1:] + imag[1:]]


def channelize_kernel(shards, size, frames, n_after, place, table, volts, *rest):
    outs, (held,) = rest[n_after : n_after + shards], rest[n_after + shards + 1 :]
    rest[n_after + shards][...] = jnp.zeros((8, LANES), jnp.int32)
    for n in range(frames):
        samples = volts[0, :, :, n * NSAMP : (n + 1) * NSAMP].reshape(-1, NSAMP)
        product = lax.dot_general(
            table[...], samples, (((1,), (1,)), ((), ())), preferred_element_type=jnp.float32
        )
        held[...] = (product * np.float32(1.0 / math.sqrt(NSAMP))).reshape(held.shape)
        for m in range(shards):
            mine = held[place[0] ^ m].astype(jnp.bfloat16)
            for a in range(2):
                for p in range(POL):
                    outs[m][a, p, n] = mine[a * size : (a + 1) * size, p * LANES : (p + 1) * LANES]


def channelize(place, table, voltages, size, shards, after):
    total = voltages.shape[3] // NSAMP
    frames = 2 if size < 32 else 4
    shape = (2, POL, total, size, LANES)
    block = (2, POL, frames, size, LANES)
    outs = pl.pallas_call(
        functools.partial(channelize_kernel, shards, size, frames, len(after)),
        grid_spec=pltpu.PrefetchScalarGridSpec(
            num_scalar_prefetch=1,
            grid=(total // frames,),
            in_specs=[
                pl.BlockSpec(table.shape, lambda n, _: (0, 0)),
                pl.BlockSpec((1, POL, LANES, frames * NSAMP), lambda n, _: (0, 0, 0, n)),
            ]
            + [pl.BlockSpec(memory_space=pl.ANY)] * len(after),
            out_specs=[pl.BlockSpec(block, lambda n, _: (0, 0, n, 0, 0))] * shards
            + [pl.BlockSpec((8, LANES), lambda n, _: (0, 0))],
            scratch_shapes=[pltpu.VMEM((shards, 2 * size, POL * LANES), jnp.float32)],
        ),
        out_shape=[jax.ShapeDtypeStruct(shape, jnp.bfloat16)] * shards
        + [jax.ShapeDtypeStruct((8, LANES), jnp.int32)],
        compiler_params=pltpu.CompilerParams(vmem_limit_bytes=40 << 20),
        cost_estimate=pl.CostEstimate(
            flops=2 * table.shape[0] * NSAMP * POL * LANES * total,
            bytes_accessed=voltages.size * 2 + table.size * 4,
            transcendentals=0,
        ),
        name="channelize",
    )(place, table, voltages, *after)
    return outs[:shards], outs[shards]


def beam_kernel(shards, frames, place, gains, table, *rest):
    spectra, outs, level, held = rest[:shards], rest[shards : 2 * shards], rest[-2], rest[-1]
    feeds = shards * LANES
    rows = POL * frames * ROWS
    for m in range(shards):
        at = pl.multiple_of((place[0] ^ m) * LANES, LANES)
        gain_real = gains[0, :, pl.ds(at, LANES)].astype(jnp.float32)
        gain_imag = gains[1, :, pl.ds(at, LANES)].astype(jnp.float32)
        real = spectra[m][0].astype(jnp.float32)
        imag = spectra[m][1].astype(jnp.float32)
        cal_real = (gain_real * real - gain_imag * imag).astype(jnp.bfloat16)
        cal_imag = (gain_real * imag + gain_imag * real).astype(jnp.bfloat16)
        held[:, pl.ds(at, LANES)] = cal_real.reshape(rows, LANES)
        held[:, pl.ds(pl.multiple_of(at + feeds, LANES), LANES)] = cal_imag.reshape(rows, LANES)
    sums = jnp.zeros((ROWS, LANES), jnp.float32)
    for m in range(shards):
        at = pl.multiple_of((place[0] ^ m) * (2 * LANES), 2 * LANES)
        beams = jnp.dot(held[...], table[:, pl.ds(at, 2 * LANES)], preferred_element_type=jnp.float32)
        squares = beams * beams
        power = squares[:, :LANES] + squares[:, LANES:]
        power = (power[: rows // 2] + power[rows // 2 :]).reshape(frames, ROWS, LANES)
        sums = sums + jnp.sum(power, axis=0)
        for q, value in enumerate(frame_sums(power)):
            outs[m][q] = value
    level[...] = sums


def form_beams(place, gains, table, spectra, start, size, frames):
    shards = len(spectra)
    outs = pl.pallas_call(
        functools.partial(beam_kernel, shards, frames),
        grid_spec=pltpu.PrefetchScalarGridSpec(
            num_scalar_prefetch=1,
            grid=(size // ROWS,),
            in_specs=[
                pl.BlockSpec((2, ROWS, gains.shape[2]), lambda g, _: (0, start // ROWS + g, 0)),
                pl.BlockSpec(table.shape, lambda g, _: (0, 0), pipeline_mode=pl.Buffered(1)),
            ]
            + [pl.BlockSpec((2, POL, frames, ROWS, LANES), lambda g, _: (0, 0, 0, g, 0))] * shards,
            out_specs=[pl.BlockSpec((2 * MODF, ROWS, LANES), lambda g, _: (0, g, 0))] * shards
            + [pl.BlockSpec((ROWS, LANES), lambda g, _: (g, 0))],
            scratch_shapes=[pltpu.VMEM((POL * frames * ROWS, table.shape[0]), jnp.bfloat16)],
        ),
        out_shape=[jax.ShapeDtypeStruct((2 * MODF, size, LANES), jnp.float32)] * shards
        + [jax.ShapeDtypeStruct((size, LANES), jnp.float32)],
        compiler_params=pltpu.CompilerParams(vmem_limit_bytes=46 << 20),
        cost_estimate=pl.CostEstimate(
            flops=2 * POL * frames * size * table.size,
            bytes_accessed=table.size * 2 + 8 * size * frames * gains.shape[2],
            transcendentals=0,
        ),
        name="form_beams",
    )(place, gains, table, *spectra)
    return outs[:shards], outs[shards]


def normalise_kernel(count, scale, section, levels, decay, *rest):
    shards = (len(rest)) // 2
    rate = decay[...]
    dividend, divisor = jnp.zeros_like(rate), jnp.zeros_like(rate)
    for block in range(count):
        mean = jnp.sum(levels[block], axis=1, keepdims=True) * scale + np.float32(1e-6)
        later = block <= section[0]
        dividend = jnp.where(later, rate * dividend + mean, dividend)
        divisor = jnp.where(later, rate * divisor + 1.0, divisor)
    inverse = divisor / dividend
    for m in range(shards):
        rest[shards + m][...] = (rest[m][...] * inverse).astype(jnp.bfloat16)


def normalise(section, levels, decay, sums, scale):
    spec = pl.BlockSpec(memory_space=pltpu.VMEM)
    return pl.pallas_call(
        functools.partial(normalise_kernel, levels.shape[0], scale),
        in_specs=[pl.BlockSpec(memory_space=pltpu.SMEM)] + [spec] * (2 + len(sums)),
        out_specs=[spec] * len(sums),
        out_shape=[jax.ShapeDtypeStruct(s.shape, jnp.bfloat16) for s in sums],
        compiler_params=pltpu.CompilerParams(vmem_limit_bytes=24 << 20),
        name="normalise",
    )(section, levels, decay, *sums)


def dedisperse_kernel(shards, size, last, first, scale, place, cosine, sine, *rest):
    parts = rest[:shards]
    total = None if first else rest[shards]
    out, real, imag = rest[-3:]
    f = pl.program_id(0)
    for m in range(shards):
        at = pl.multiple_of((place[0] ^ m) * size, size)
        real[pl.ds(at, size), :] = parts[m][f]
        imag[pl.ds(at, size), :] = parts[m][f + MODF]
    value = jnp.dot(cosine[0], real[...], preferred_element_type=jnp.float32) + jnp.dot(
        sine[0], imag[...], preferred_element_type=jnp.float32
    )
    if total is not None:
        value = value + total[0]
    out[0] = (value * scale).astype(out.dtype) if last else value


def dedisperse(place, cosine, sine, parts, total, last, scale):
    shards, (_, size, _) = len(parts), parts[0].shape
    rows, depth = cosine.shape[1:]
    each = lambda f, _: (f, 0, 0)
    whole = pl.BlockSpec(parts[0].shape, lambda f, _: (0, 0, 0))
    sums = [] if total is None else [total]
    return pl.pallas_call(
        functools.partial(dedisperse_kernel, shards, size, last, total is None, scale),
        grid_spec=pltpu.PrefetchScalarGridSpec(
            num_scalar_prefetch=1,
            grid=(MODF,),
            in_specs=[pl.BlockSpec((1, rows, depth), each)] * 2
            + [whole] * shards
            + [pl.BlockSpec((1, rows, LANES), each)] * len(sums),
            out_specs=pl.BlockSpec((1, rows, LANES), each),
            scratch_shapes=[pltpu.VMEM((depth, LANES), jnp.bfloat16)] * 2,
        ),
        out_shape=jax.ShapeDtypeStruct((MODF, rows, LANES), jnp.bfloat16 if last else jnp.float32),
        compiler_params=pltpu.CompilerParams(vmem_limit_bytes=32 << 20),
        cost_estimate=pl.CostEstimate(
            flops=4 * MODF * rows * depth * LANES,
            bytes_accessed=4 * MODF * rows * (depth + LANES),
            transcendentals=0,
        ),
        name="dedisperse",
    )(place, cosine, sine, *parts, *sums)


def phase_tables(turns, frames):
    delay, quarter = turns
    f = jnp.arange(1, MODF + 1, dtype=jnp.int32)[:, None, None]
    turn = f * delay[None] + quarter[None]
    cosine = cosine_of(turn, frames).astype(jnp.bfloat16)
    sine = cosine_of(turn - frames // 4, frames).astype(jnp.bfloat16)
    return cosine, sine


def chunk_sizes(channels):
    edge, inner = ROWS, 2 * ROWS
    if channels < 2 * edge + inner:
        return [ROWS] * (channels // ROWS)
    left = channels - 2 * edge
    sizes = [edge] + [inner] * (left // inner) + ([left % inner] if left % inner else []) + [edge]
    return sizes


def pipelined(voltages, feed_gains, grid_index, decay_rates, delays):
    shards, blocks = lax.axis_size("shard"), lax.axis_size("section")
    frames = voltages.shape[3] // NSAMP
    chans, trials = delays.shape
    feeds = grid_index.shape[0]
    local = chans // shards
    place = lax.axis_index("shard").reshape(1)
    section = lax.axis_index("section").reshape(1)
    sizes = chunk_sizes(local)
    starts = [sum(sizes[:c]) for c in range(len(sizes))]
    rows = spectral_constant(chans).reshape(2, shards, local, NSAMP)
    scale = np.float32(1.0 / (frames * feeds))

    def exchange(parts):
        got = [parts[0]] + [None] * (shards - 1)
        order = [m for m in range(shards - 1, 0, -1)]
        for m in order:
            got[m] = lax.ppermute(parts[m], "shard", [(j, j ^ m) for j in range(shards)])
        return got

    def send_spectra(c, after):
        table = np.ascontiguousarray(rows[:, :, starts[c] : starts[c] + sizes[c]].transpose(1, 0, 2, 3))
        table = jnp.asarray(table.reshape(-1, NSAMP))
        parts, zero = channelize(place, table, voltages, sizes[c], shards, after)
        return exchange(parts), zero

    received, zero = {}, None
    received[0], zero = send_spectra(0, [])
    received[1], _ = send_spectra(1, [])

    zero = zero[0, 0]
    table = beam_table(grid_index + zero)
    by_trial = jnp.transpose((delays + zero) & (frames - 1)).reshape(trials, shards, local)
    by_trial = jnp.repeat(by_trial, 2, axis=0)
    quarter = (lax.broadcasted_iota(jnp.int32, (2 * trials, 1), 0) % 2) * (frames // 4)

    total = None
    pending = None
    for c in range(len(sizes)):
        start, size = starts[c], sizes[c]
        if c + 2 < len(sizes):
            received[c + 2], _ = send_spectra(c + 2, received[c][1:])
        sums, level = form_beams(place, feed_gains, table, received[c], start, size, frames)
        levels = lax.all_gather(level, "section")
        decay = decay_rates[start : start + size].reshape(size, 1)
        modulated = exchange(normalise(section, levels, decay, sums, scale))
        chosen = by_trial[:, :, start : start + size].reshape(2 * trials, shards * size)
        cosine, sine = phase_tables((chosen, quarter), frames)
        total = dedisperse(
            place, cosine, sine, modulated, total, c + 1 == len(sizes), np.float32(1.0 / math.sqrt(chans))
        )
    return total.reshape(1, MODF, trials, 2, feeds // shards)


def plain(voltages, feed_gains, grid_index, decay_rates, delays):
    shards = lax.axis_size("shard")
    chans, trials = delays.shape
    feeds, local_feeds = grid_index.shape[0], voltages.shape[2]
    frames = voltages.shape[3] // NSAMP
    samples = voltages[0].reshape(POL * local_feeds * frames, NSAMP)
    rows = jnp.asarray(spectral_constant(chans).reshape(2 * chans, NSAMP))
    spectra = lax.dot_general(rows, samples, (((1,), (1,)), ((), ())), preferred_element_type=jnp.float32)
    spectra = (spectra * (1.0 / math.sqrt(NSAMP))).astype(jnp.bfloat16)
    spectra = spectra.reshape(2, chans, POL, local_feeds, frames)
    turned = lax.all_to_all(spectra, "shard", split_axis=1, concat_axis=3, tiled=True)
    values = turned.astype(jnp.float32)
    gain = feed_gains.astype(jnp.float32)[:, :, None, :, None]
    calibrated = jnp.stack(
        [gain[0] * values[0] - gain[1] * values[1], gain[0] * values[1] + gain[1] * values[0]]
    ).astype(jnp.bfloat16)
    table = beam_table(grid_index).reshape(2, feeds, feeds // LANES, 2, LANES)
    beams = jnp.einsum("akpfn,afdel->eknpdl", calibrated, table, preferred_element_type=jnp.float32)
    power = jnp.sum(beams * beams, axis=(0, 3)).reshape(-1, frames, feeds)
    levels = jnp.mean(power, axis=(1, 2)) + 1e-06
    gathered = lax.all_gather(levels, "section")
    dividend, divisor = jnp.zeros_like(levels), jnp.zeros_like(levels)
    for block in range(gathered.shape[0]):
        later = block <= lax.axis_index("section")
        dividend = jnp.where(later, decay_rates * dividend + gathered[block], dividend)
        divisor = jnp.where(later, decay_rates * divisor + 1.0, divisor)
    power = power * (divisor / dividend)[:, None, None]
    sums = jnp.stack(frame_sums([power[:, n] for n in range(frames)])).astype(jnp.bfloat16)
    moved = lax.all_to_all(sums, "shard", split_axis=2, concat_axis=1, tiled=True)
    turn = jnp.arange(1, MODF + 1, dtype=jnp.int32)[:, None, None] * (delays & (frames - 1))[None]
    cosine = cosine_of(turn, frames).astype(jnp.bfloat16)
    sine = cosine_of(turn - frames // 4, frames).astype(jnp.bfloat16)
    dot = functools.partial(jnp.einsum, "fkt,fkb->ftb", preferred_element_type=jnp.float32)
    real, imag = moved[:MODF], moved[MODF:]
    result = jnp.stack(
        [dot(cosine, real) + dot(sine, imag), dot(cosine, imag) - dot(sine, real)], 2
    ) * (1.0 / math.sqrt(chans))
    return result.astype(jnp.bfloat16)[None]


def solution(mesh):
    def shards(voltages, feed_gains, grid_index, decay_rates, delays):
        count = lax.axis_size("shard")
        fits = (
            voltages.shape[2] == LANES
            and grid_index.shape[0] == count * LANES
            and delays.shape[0] % (count * ROWS) == 0
            and voltages.shape[3] == ROWS * NSAMP
            and count & (count - 1) == 0
            and delays.shape[0] // count >= 2 * ROWS
        )
        form = pipelined if fits else plain
        return form(voltages, feed_gains, grid_index, decay_rates, delays)

    in_specs = (P("section", None, "shard", None), P(None, "shard", None), P(), P("shard"), P())
    out_specs = P("section", None, None, None, "shard")
    return jax.shard_map(shards, mesh=mesh, in_specs=in_specs, out_specs=out_specs, check_vma=False)
```

time: 1250 us -> 639 us (0.51)
  matrix products: 406 us -> 0 us
  waiting for transfers between devices: 425 us -> 137 us
  local copies, waits for them, and re-layouts: 295 us -> 76.2 us
  Pallas kernels: 0 us -> 152 us
  starting transfers between devices: 11.3 us -> 154 us
  loops' own time: 44.9 us -> 0 us
  other arithmetic: 37.1 us -> 69.8 us
  blocking collectives: 17.9 us -> 39.2 us
    all_to_all x2 -> x0, waiting for transfers between devices: 425 us -> none  [the longest x1 344 us: shards(): lax.all_to_all(spectra, 'shard', split_axis=1, concat_axis=3, tiled=True)]
    dot_general x32 -> x0, matrix products: 406 us -> none  [the longest x1 87.6 us: form_beams(): jnp.einsum('bcpxwn,bxeu->ecpnuw', row_beams, twiddle_table(GRID_X), preci...]
    ppermute x0 -> x70, starting transfers between devices: none -> 154 us  [exchange(): lax.ppermute(parts[m], 'shard', [(j, j ^ m) for j in range(shards)])]
    pallas_call x0 -> x20, Pallas kernels: none -> 152 us  [the longest x5 69.7 us: form_beams(): pl.pallas_call(functools.partial(beam_kernel, shards, frames), grid_spec=...]
    ppermute x0 -> x70, waiting for transfers between devices: none -> 137 us  [exchange(): lax.ppermute(parts[m], 'shard', [(j, j ^ m) for j in range(shards)])]
    convert_element_type x9 -> x3, other arithmetic: 11.8 us -> 66.9 us  [the longest x2 48.4 us: phase_tables(): sine = cosine_of(turn - frames // 4, frames).astype(jnp.bfloat16)]
    reshape x3 -> x8, local copies, waits for them, and re-layouts: 55.6 us -> 3.52 us  [the longest x1 2.95 us: pipelined(): jnp.transpose(delays + zero & frames - 1).reshape(trials, shards, local)]
    gather x2 -> x0, local copies, waits for them, and re-layouts: 46.6 us -> none  [form_beams(): jnp.take(calibrated, cell_feed, axis=3)]
  transfers between devices with their start and end apart: 2 -> 70, of which waited for: 2 -> 9; matrix products, arithmetic and copies ran while one was open for 1% -> 20% of each run, Pallas kernels for 0% -> 22%
where the time goes in v1:
time: 639 us; the launch traced here: 629 us
  starting transfers between devices  154 us (24%)
  Pallas kernels  152 us (24%)
  waiting for transfers between devices  137 us (21%)
  local copies, waits for them, and re-layouts  76.2 us (12%)
  other arithmetic  69.8 us (11%)
  blocking collectives  39.2 us (6%)
    ppermute x70, starting transfers between devices, exchange(): lax.ppermute(parts[m], 'shard', [(j, j ^ m) for j in range(shards)])  154 us
    ppermute x70, waiting for transfers between devices, exchange(): lax.ppermute(parts[m], 'shard', [(j, j ^ m) for j in range(shards)])  137 us
    pallas_call x5, Pallas kernels, form_beams(): pl.pallas_call(functools.partial(beam_kernel, shards, frames), grid_spec=...  69.7 us
    pallas_call x5, Pallas kernels, channelize(): pl.pallas_call(functools.partial(channelize_kernel, shards, size, frames,...  63.9 us
    convert_element_type x2, other arithmetic, phase_tables(): sine = cosine_of(turn - frames // 4, frames).astype(jnp.bfloat16)  48.4 us
    all_gather x5, blocking collectives, pipelined(): levels = lax.all_gather(level, 'section')  39.2 us
    slice x7, local copies, waits for them, and re-layouts, pipelined(): by_trial[:, :, start:start + size].reshape(2 * trials, shards * size)  39 us
    unnamed x156, local copies, waits for them, and re-layouts  19.1 us
  transfers between devices with their start and end apart: 70, of which 9 were waited for; matrix products, arithmetic and copies ran while one was open for 20% of the time, Pallas kernels for 22%

profile of v1, /device:TPU:0, one launch (start us, length us, event | category | flops | bytes accessed | tf_op | source)
XLA Modules:
  0.0 628.7 jit_solution(8106484977699933547)
XLA Ops:
  1.2 11.8 %channelize.5 = (bf16[2,2,16,16,128]{4,3,2,1,0:T(8,128)(2,1)S(1)}, bf16[2,2,16,16,128]{4,3,2,1,0:T(8,128)(2,1)}, bf16[2,2,16,16,128]{4,3,2,1,0:T(8,128)(2,1)S(1)...) custom-call(s32[1]{0:T(128)} %bitcast.place, ...), custom_call_target="tpu_custom_call" | custom-call | flops 4294967296 | bytes 18874368 | tf_op jit(solution)/shard_map/channelize/pallas_call | solution.py:97
  16.9 2.7 collective-permute-start.3
  23.1 3.0 copy.27
  27.6 13.4 %channelize.8 = (bf16[2,2,16,32,128]{4,3,2,1,0:T(8,128)(2,1)S(1)}, bf16[2,2,16,32,128]{4,3,2,1,0:T(8,128)(2,1)}, bf16[2,2,16,32,128]{4,3,2,1,0:T(8,128)(2,1)}, b...) custom-call(s32[1]{0:T(128)} %bitcast.place, ...), custom_call_target="tpu_custom_call" | custom-call | flops 8589934592 | bytes 20971520 | tf_op jit(solution)/shard_map/channelize/pallas_call | solution.py:97
  41.0 18.5 %multiply_convert_fusion.table = bf16[2048,2048]{1,0:T(8,128)(2,1)} fusion(s32[2048]{0:T(1024)S(1)} %get-tuple-element.285, s32[2048]{0:T(1024)S(1)} %get-tuple-element.286, s32[2048]{0:T(1024)S(1)} %get-tuple-element.287, s32[2048]{0:T(1024)S(1)} %get-tuple-element.279, s32[2048]{0:T(1024)S(1)} %get-tuple-element.288, s32[2048]{0:T(1024)S(1)} %get-tuple-element.278), kind=kLoop, calls=%fused_computation | loop fusion | flops 117440512 | bytes 8437760 | tf_op jit(solution)/shard_map/convert_element_type | solution.py:50
  61.9 12.9 %fusion.26 = (s32[1024,8,32]{2,1,0:T(8,128)}, s32[1024,8,32]{2,1,0:T(8,128)}, s32[1024,8,32]{2,1,0:T(8,128)}) fusion(s32[1024,8,128]{2,1,0:T(8,128)} %bitcast.33), kind=kLoop, calls=%fused_computation.76 | loop fusion | bytes 6291456 | tf_op jit(solution)/shard_map/slice | solution.py:315
  75.6 3.6 collective-permute-start.5
  80.6 3.6 copy.37
  86.8 3.7 copy.34
  93.0 3.7 copy.31
  109.9 9.9 %form_beams.9 = (f32[14,16,128]{2,1,0:T(8,128)S(1)}, f32[14,16,128]{2,1,0:T(8,128)S(1)}, f32[14,16,128]{2,1,0:T(8,128)S(1)}, f32[14,16,128]{2,1,0:T(8,128)S(1)},...) custom-call(s32[1]{0:T(128)} %bitcast.place, ...), custom_call_target="tpu_custom_call" | custom-call | flops 4294967296 | bytes 10485760 | tf_op jit(solution)/shard_map/form_beams/pallas_call | solution.py:153
  119.8 8.2 %all-gather.4 = f32[64,128]{1,0:T(8,128)S(1)} all-gather(f32[16,128]{1,0:T(8,128)S(1)} %get-tuple-element.240), channel_id=6, replica_groups=mesh['section'=4,'shard'=8] {'section'}, dimensions={0}, use_global_device_ids=true | all-gather | bytes 40960 | tf_op jit(solution)/shard_map/all_gather | solution.py:312
  129.8 3.5 collective-permute-start.33
  133.3 13.6 %channelize.6 = (bf16[2,2,16,32,128]{4,3,2,1,0:T(8,128)(2,1)S(1)}, bf16[2,2,16,32,128]{4,3,2,1,0:T(8,128)(2,1)S(1)}, bf16[2,2,16,32,128]{4,3,2,1,0:T(8,128)(2,1)...) custom-call(s32[1]{0:T(128)} %bitcast.place, ...), custom_call_target="tpu_custom_call" | custom-call | flops 8589934592 | bytes 20971520 | tf_op jit(solution)/shard_map/channelize/pallas_call | solution.py:97
  147.1 31.0 %collective-permute-done.32.rest_4_.rest_5_ = bf16[2,2,16,32,128]{4,3,2,1,0:T(8,128)(2,1)S(1)} collective-permute-done((bf16[2,2,16,32,128]{4,3,2,1,0:T(8,128)(2,1)S(1)}, bf16[2,2,16,32,128]{4,3,2,1,0:T(8,128)(2,1)S(1)}, u32[]{:S(2)}, u32[]{:S(2)}) %collective-permute-start.32) | collective-permute-done | bytes 524320 | tf_op jit(solution)/shard_map/ppermute | solution.py:286
  178.1 11.5 %collective-permute-start.65 = (bf16[14,16,128]{2,1,0:T(8,128)(2,1)S(1)}, bf16[14,16,128]{2,1,0:T(8,128)(2,1)S(1)}, u32[]{:S(2)}, u32[]{:S(2)}) collective-permute-start(bf16[14,16,128]{2,1,0:T(8,128)(2,1)S(1)} %get-tuple-element.252), channel_id=1, source_target_pairs={{0,3},{1,2},{2,1},{3,0},{4,7},{5,6},{6,5},{7,4},{8,11},{9,10},{10,... | collective-permute-start | bytes 172040 | tf_op jit(solution)/shard_map/ppermute | solution.py:286
  189.6 11.1 %collective-permute-start.66 = (bf16[14,16,128]{2,1,0:T(8,128)(2,1)S(1)}, bf16[14,16,128]{2,1,0:T(8,128)(2,1)S(1)}, u32[]{:S(2)}, u32[]{:S(2)}) collective-permute-start(bf16[14,16,128]{2,1,0:T(8,128)(2,1)S(1)} %get-tuple-element.253), channel_id=1, source_target_pairs={{0,4},{1,5},{2,6},{3,7},{4,0},{5,1},{6,2},{7,3},{8,12},{9,13},{10,... | collective-permute-start | bytes 172040 | tf_op jit(solution)/shard_map/ppermute | solution.py:286
  200.7 16.5 %form_beams.8 = (f32[14,32,128]{2,1,0:T(8,128)S(1)}, f32[14,32,128]{2,1,0:T(8,128)S(1)}, f32[14,32,128]{2,1,0:T(8,128)S(1)}, f32[14,32,128]{2,1,0:T(8,128)S(1)},...) custom-call(s32[1]{0:T(128)} %bitcast.place, ...), custom_call_target="tpu_custom_call" | custom-call | flops 8589934592 | bytes 12582912 | tf_op jit(solution)/shard_map/form_beams/pallas_call | solution.py:153
  217.2 8.2 %all-gather.3 = f32[128,128]{1,0:T(8,128)S(1)} all-gather(f32[32,128]{1,0:T(8,128)S(1)} %get-tuple-element.222), channel_id=5, replica_groups=mesh['section'=4,'shard'=8] {'section'}, dimensions={0}, use_global_device_ids=true | all-gather | bytes 81920 | tf_op jit(solution)/shard_map/all_gather | solution.py:312
  234.4 13.6 %channelize.9 = (bf16[2,2,16,32,128]{4,3,2,1,0:T(8,128)(2,1)S(1)}, bf16[2,2,16,32,128]{4,3,2,1,0:T(8,128)(2,1)}, bf16[2,2,16,32,128]{4,3,2,1,0:T(8,128)(2,1)}, b...) custom-call(s32[1]{0:T(128)} %bitcast.place, ...), custom_call_target="tpu_custom_call" | custom-call | flops 8589934592 | bytes 20971520 | tf_op jit(solution)/shard_map/channelize/pallas_call | solution.py:97
  252.2 35.7 %collective-permute-done.10.rest_3_.rest_4_ = bf16[2,2,16,32,128]{4,3,2,1,0:T(8,128)(2,1)S(1)} collective-permute-done((bf16[2,2,16,32,128]{4,3,2,1,0:T(8,128)(2,1)S(1)}, bf16[2,2,16,32,128]{4,3,2,1,0:T(8,128)(2,1)S(1)}, u32[]{:S(2)}, u32[]{:S(2)}) %collective-permute-start.10) | collective-permute-done | bytes 524320 | tf_op jit(solution)/shard_map/ppermute | solution.py:286
  287.9 2.8 collective-permute-start.68
  290.7 9.2 %collective-permute-done.11.rest_4_.rest_5_ = bf16[2,2,16,32,128]{4,3,2,1,0:T(8,128)(2,1)S(1)} collective-permute-done((bf16[2,2,16,32,128]{4,3,2,1,0:T(8,128)(2,1)S(1)}, bf16[2,2,16,32,128]{4,3,2,1,0:T(8,128)(2,1)S(1)}, u32[]{:S(2)}, u32[]{:S(2)}) %collective-permute-start.11) | collective-permute-done | bytes 524320 | tf_op jit(solution)/shard_map/ppermute | solution.py:286
  302.6 21.5 %collective-permute-start.57 = (bf16[14,32,128]{2,1,0:T(8,128)(2,1)S(1)}, bf16[14,32,128]{2,1,0:T(8,128)(2,1)S(1)}, u32[]{:S(2)}, u32[]{:S(2)}) collective-permute-start(bf16[14,32,128]{2,1,0:T(8,128)(2,1)S(1)} %get-tuple-element.233), channel_id=1, source_target_pairs={{0,2},{1,3},{2,0},{3,1},{4,6},{5,7},{6,4},{7,5},{8,10},{9,11},{10,... | collective-permute-start | bytes 344072 | tf_op jit(solution)/shard_map/ppermute | solution.py:286
  324.1 16.4 %form_beams.7 = (f32[14,32,128]{2,1,0:T(8,128)S(1)}, f32[14,32,128]{2,1,0:T(8,128)S(1)}, f32[14,32,128]{2,1,0:T(8,128)S(1)}, f32[14,32,128]{2,1,0:T(8,128)S(1)},...) custom-call(s32[1]{0:T(128)} %bitcast.place, ...), custom_call_target="tpu_custom_call" | custom-call | flops 8589934592 | bytes 12582912 | tf_op jit(solution)/shard_map/form_beams/pallas_call | solution.py:153
  341.3 3.0 collective-permute-start.59
  348.3 11.6 %channelize.7 = (bf16[2,2,16,16,128]{4,3,2,1,0:T(8,128)(2,1)S(1)}, bf16[2,2,16,16,128]{4,3,2,1,0:T(8,128)(2,1)}, bf16[2,2,16,16,128]{4,3,2,1,0:T(8,128)(2,1)}, b...) custom-call(s32[1]{0:T(128)} %bitcast.place, ...), custom_call_target="tpu_custom_call" | custom-call | flops 4294967296 | bytes 18874368 | tf_op jit(solution)/shard_map/channelize/pallas_call | solution.py:97
  359.9 7.3 %all-gather.2 = f32[128,128]{1,0:T(8,128)S(1)} all-gather(f32[32,128]{1,0:T(8,128)S(1)} %get-tuple-element.204), channel_id=4, replica_groups=mesh['section'=4,'shard'=8] {'section'}, dimensions={0}, use_global_device_ids=true | all-gather | bytes 81920 | tf_op jit(solution)/shard_map/all_gather | solution.py:312
  370.7 36.2 %multiply_convert_fusion.1 = (bf16[7,1024,256]{2,1,0:T(8,128)(2,1)}, bf16[7,1024,256]{2,1,0:T(8,128)(2,1)}, bf16[7,1024,256]{2,1,0:T(8,128)(2,1)}, bf16[7,1024,2...) fusion(s32[1024,256]{1,0:T(8,128)S(1)} %copy-done.70, s32[1024]{0:T(1024)S(1)} %fusion.21, ...), kind=kLoop, calls=%fused_computation.1 | loop fusion | flops 242221056 | bytes 25169948 | tf_op jit(solution)/shard_map/convert_element_type | solution.py:256
  407.6 2.9 collective-permute-start.38
  413.9 8.0 %fusion.25 = (s32[1024,8,16]{2,1,0:T(8,128)}, s32[1024,8,16]{2,1,0:T(8,128)}) fusion(s32[1024,8,128]{2,1,0:T(8,128)} %bitcast.34), kind=kLoop, calls=%fused_computation.75 | loop fusion | bytes 2097152 | tf_op jit(solution)/shard_map/slice | solution.py:315
  421.9 3.5 copy.40
  427.4 3.5 copy.28
  433.0 35.6 %collective-permute-done.38.rest_4_ = bf16[2,2,16,32,128]{4,3,2,1,0:T(8,128)(2,1)} collective-permute-done((bf16[2,2,16,32,128]{4,3,2,1,0:T(8,128)(2,1)}, bf16[2,2,16,32,128]{4,3,2,1,0:T(8,128)(2,1)}, u32[]{:S(2)}, u32[]{:S(2)}) %collective-permute-start.38) | collective-permute-done | bytes 524320 | tf_op jit(solution)/shard_map/ppermute | solution.py:286
  468.5 15.7 %collective-permute-done.39.rest_5_ = bf16[2,2,16,32,128]{4,3,2,1,0:T(8,128)(2,1)} collective-permute-done((bf16[2,2,16,32,128]{4,3,2,1,0:T(8,128)(2,1)}, bf16[2,2,16,32,128]{4,3,2,1,0:T(8,128)(2,1)}, u32[]{:S(2)}, u32[]{:S(2)}) %collective-permute-start.39) | collective-permute-done | bytes 524320 | tf_op jit(solution)/shard_map/ppermute | solution.py:286
  489.4 17.1 %form_beams.6 = (f32[14,32,128]{2,1,0:T(8,128)S(1)}, f32[14,32,128]{2,1,0:T(8,128)S(1)}, f32[14,32,128]{2,1,0:T(8,128)S(1)}, f32[14,32,128]{2,1,0:T(8,128)S(1)},...) custom-call(s32[1]{0:T(128)} %bitcast.place, ...), custom_call_target="tpu_custom_call" | custom-call | flops 8589934592 | bytes 12582912 | tf_op jit(solution)/shard_map/form_beams/pallas_call | solution.py:153
  506.5 38.2 %collective-permute-start.50 = (bf16[14,32,128]{2,1,0:T(8,128)(2,1)S(1)}, bf16[14,32,128]{2,1,0:T(8,128)(2,1)S(1)}, u32[]{:S(2)}, u32[]{:S(2)}) collective-permute-start(bf16[14,32,128]{2,1,0:T(8,128)(2,1)S(1)} %copy-done.61), channel_id=1, source_target_pairs={{0,2},{1,3},{2,0},{3,1},{4,6},{5,7},{6,4},{7,5},{8,10},{9,11},{10,... | collective-permute-start | bytes 344072 | tf_op jit(solution)/shard_map/ppermute | solution.py:286
  549.0 9.9 %form_beams.5 = (f32[14,16,128]{2,1,0:T(8,128)S(1)}, f32[14,16,128]{2,1,0:T(8,128)S(1)}, f32[14,16,128]{2,1,0:T(8,128)S(1)}, f32[14,16,128]{2,1,0:T(8,128)S(1)},...) custom-call(s32[1]{0:T(128)} %bitcast.place, ...), custom_call_target="tpu_custom_call" | custom-call | flops 4294967296 | bytes 10485760 | tf_op jit(solution)/shard_map/form_beams/pallas_call | solution.py:153
  558.9 8.3 %all-gather = f32[64,128]{1,0:T(8,128)S(1)} all-gather(f32[16,128]{1,0:T(8,128)S(1)} %get-tuple-element.154), channel_id=2, replica_groups=mesh['section'=4,'shard'=8] {'section'}, dimensions={0}, use_global_device_ids=true | all-gather | bytes 40960 | tf_op jit(solution)/shard_map/all_gather | solution.py:312
  567.4 7.3 %all-gather.1 = f32[128,128]{1,0:T(8,128)S(1)} all-gather(f32[32,128]{1,0:T(8,128)S(1)} %get-tuple-element.186), channel_id=3, replica_groups=mesh['section'=4,'shard'=8] {'section'}, dimensions={0}, use_global_device_ids=true | all-gather | bytes 81920 | tf_op jit(solution)/shard_map/all_gather | solution.py:312
  579.5 12.2 %multiply_convert_fusion.7 = (bf16[7,1024,128]{2,1,0:T(8,128)(2,1)S(1)}, bf16[7,1024,128]{2,1,0:T(8,128)(2,1)S(1)}, bf16[7,1024,128]{2,1,0:T(8,128)(2,1)S(1)}, bf16[7,1024,128]{2,1,0:T(8,128)(2,1)S(1)}) fusion(s32[1024,128]{1,0:T(8,128)S(1)} %copy-done.74, s32[1024]{0:T(1024)S(1)} %fusion.21, s32[7]{0:T(128)S(1)} %iota_add_fusion, s32[1024,128]{1,0:T(8,128)S(1)} %copy-done.75), kind=kLoop, calls=%fused_computation.10 | loop fusion | flops 80740352 | bytes 8392732 | tf_op jit(solution)/shard_map/convert_element_type | solution.py:256
  600.4 3.2 dedisperse.6.rest_8_
  603.7 3.2 dedisperse.7.rest_8_
  607.0 4.0 collective-permute-done.45.rest_4_
  614.0 3.6 collective-permute-start.27
  617.6 3.2 dedisperse.8.rest_8_
  620.8 3.6 collective-permute-done.24.rest_4_
  624.5 4.0 dedisperse.9
  (305 shorter events, 93.0 us)
Async XLA Ops:
  13.8 61.2 %collective-permute-start = (bf16[2,2,16,16,128]{4,3,2,1,0:T(8,128)(2,1)}, bf16[2,2,16,16,128]{4,3,2,1,0:T(8,128)(2,1)S(1)}, u32[]{:S(2)}, u32[]{:S(2)}) collective-permute-start(bf16[2,2,16,16,128]{4,3,2,1,0:T(8,128)(2,1)} %get-tuple-element.132), channel_id=1, source_target_pairs={{0,1},{1,0},{2,3},{3,2},{4,5},{5,4},{6,7},{7,6},{8,9},{9,8},{10,11... | collective-permute-start | bytes 786440 | tf_op jit(solution)/shard_map/ppermute | solution.py:286
  14.2 65.0 %collective-permute-start.1 = (bf16[2,2,16,16,128]{4,3,2,1,0:T(8,128)(2,1)S(1)}, bf16[2,2,16,16,128]{4,3,2,1,0:T(8,128)(2,1)S(1)}, u32[]{:S(2)}, u32[]{:S(2)}) collective-permute-start(bf16[2,2,16,16,128]{4,3,2,1,0:T(8,128)(2,1)S(1)} %get-tuple-element.133), channel_id=1, source_target_pairs={{0,2},{1,3},{2,0},{3,1},{4,6},{5,7},{6,4},{7,5},{8,10},{9,11},{10,... | collective-permute-start | bytes 786440 | tf_op jit(solution)/shard_map/ppermute | solution.py:286
  16.8 62.7 %collective-permute-start.2 = (bf16[2,2,16,16,128]{4,3,2,1,0:T(8,128)(2,1)S(1)}, bf16[2,2,16,16,128]{4,3,2,1,0:T(8,128)(2,1)S(1)}, u32[]{:S(2)}, u32[]{:S(2)}) collective-permute-start(bf16[2,2,16,16,128]{4,3,2,1,0:T(8,128)(2,1)S(1)} %get-tuple-element.134), channel_id=1, source_target_pairs={{0,3},{1,2},{2,1},{3,0},{4,7},{5,6},{6,5},{7,4},{8,11},{9,10},{10,... | collective-permute-start | bytes 786440 | tf_op jit(solution)/shard_map/ppermute | solution.py:286
  16.9 62.7 %collective-permute-start.3 = (bf16[2,2,16,16,128]{4,3,2,1,0:T(8,128)(2,1)S(1)}, bf16[2,2,16,16,128]{4,3,2,1,0:T(8,128)(2,1)S(1)}, u32[]{:S(2)}, u32[]{:S(2)}) collective-permute-start(bf16[2,2,16,16,128]{4,3,2,1,0:T(8,128)(2,1)S(1)} %get-tuple-element.135), channel_id=1, source_target_pairs={{0,4},{1,5},{2,6},{3,7},{4,0},{5,1},{6,2},{7,3},{8,12},{9,13},{10,... | collective-permute-start | bytes 786440 | tf_op jit(solution)/shard_map/ppermute | solution.py:286
  19.7 79.6 %collective-permute-start.4 = (bf16[2,2,16,16,128]{4,3,2,1,0:T(8,128)(2,1)}, bf16[2,2,16,16,128]{4,3,2,1,0:T(8,128)(2,1)}, u32[]{:S(2)}, u32[]{:S(2)}) collective-permute-start(bf16[2,2,16,16,128]{4,3,2,1,0:T(8,128)(2,1)} %get-tuple-element.136), channel_id=1, source_target_pairs={{0,5},{1,4},{2,7},{3,6},{4,1},{5,0},{6,3},{7,2},{8,13},{9,12},{10,... | collective-permute-start | bytes 786440 | tf_op jit(solution)/shard_map/ppermute | solution.py:286
  79.4 50.3 %collective-permute-start.28 = (bf16[2,2,16,32,128]{4,3,2,1,0:T(8,128)(2,1)}, bf16[2,2,16,32,128]{4,3,2,1,0:T(8,128)(2,1)S(1)}, u32[]{:S(2)}, u32[]{:S(2)}) collective-permute-start(bf16[2,2,16,32,128]{4,3,2,1,0:T(8,128)(2,1)} %get-tuple-element.171), channel_id=1, source_target_pairs={{0,1},{1,0},{2,3},{3,2},{4,5},{5,4},{6,7},{7,6},{8,9},{9,8},{10,11... | collective-permute-start | bytes 1572872 | tf_op jit(solution)/shard_map/ppermute | solution.py:286
  80.4 52.9 %collective-permute-start.29 = (bf16[2,2,16,32,128]{4,3,2,1,0:T(8,128)(2,1)}, bf16[2,2,16,32,128]{4,3,2,1,0:T(8,128)(2,1)S(1)}, u32[]{:S(2)}, u32[]{:S(2)}) collective-permute-start(bf16[2,2,16,32,128]{4,3,2,1,0:T(8,128)(2,1)} %get-tuple-element.172), channel_id=1, source_target_pairs={{0,2},{1,3},{2,0},{3,1},{4,6},{5,7},{6,4},{7,5},{8,10},{9,11},{10,... | collective-permute-start | bytes 1572872 | tf_op jit(solution)/shard_map/ppermute | solution.py:286
  99.3 47.6 %collective-permute-start.30 = (bf16[2,2,16,32,128]{4,3,2,1,0:T(8,128)(2,1)}, bf16[2,2,16,32,128]{4,3,2,1,0:T(8,128)(2,1)S(1)}, u32[]{:S(2)}, u32[]{:S(2)}) collective-permute-start(bf16[2,2,16,32,128]{4,3,2,1,0:T(8,128)(2,1)} %copy-done.31), channel_id=1, source_target_pairs={{0,3},{1,2},{2,1},{3,0},{4,7},{5,6},{6,5},{7,4},{8,11},{9,10},{10,... | collective-permute-start | bytes 1572872 | tf_op jit(solution)/shard_map/ppermute | solution.py:286
  101.7 45.4 %collective-permute-start.31 = (bf16[2,2,16,32,128]{4,3,2,1,0:T(8,128)(2,1)}, bf16[2,2,16,32,128]{4,3,2,1,0:T(8,128)(2,1)S(1)}, u32[]{:S(2)}, u32[]{:S(2)}) collective-permute-start(bf16[2,2,16,32,128]{4,3,2,1,0:T(8,128)(2,1)} %copy-done.30), channel_id=1, source_target_pairs={{0,4},{1,5},{2,6},{3,7},{4,0},{5,1},{6,2},{7,3},{8,12},{9,13},{10,... | collective-permute-start | bytes 1572872 | tf_op jit(solution)/shard_map/ppermute | solution.py:286
  129.5 48.6 %collective-permute-start.32 = (bf16[2,2,16,32,128]{4,3,2,1,0:T(8,128)(2,1)S(1)}, bf16[2,2,16,32,128]{4,3,2,1,0:T(8,128)(2,1)S(1)}, u32[]{:S(2)}, u32[]{:S(2)}) collective-permute-start(bf16[2,2,16,32,128]{4,3,2,1,0:T(8,128)(2,1)S(1)} %copy-done.29), channel_id=1, source_target_pairs={{0,5},{1,4},{2,7},{3,6},{4,1},{5,0},{6,3},{7,2},{8,13},{9,12},{10,... | collective-permute-start | bytes 1572872 | tf_op jit(solution)/shard_map/ppermute | solution.py:286
  129.8 48.4 %collective-permute-start.33 = (bf16[2,2,16,32,128]{4,3,2,1,0:T(8,128)(2,1)S(1)}, bf16[2,2,16,32,128]{4,3,2,1,0:T(8,128)(2,1)S(1)}, u32[]{:S(2)}, u32[]{:S(2)}) collective-permute-start(bf16[2,2,16,32,128]{4,3,2,1,0:T(8,128)(2,1)S(1)} %get-tuple-element.176), channel_id=1, source_target_pairs={{0,6},{1,7},{2,4},{3,5},{4,2},{5,3},{6,0},{7,1},{8,14},{9,15},{10,... | collective-permute-start | bytes 1572872 | tf_op jit(solution)/shard_map/ppermute | solution.py:286
  133.2 56.4 %collective-permute-start.34 = (bf16[2,2,16,32,128]{4,3,2,1,0:T(8,128)(2,1)S(1)}, bf16[2,2,16,32,128]{4,3,2,1,0:T(8,128)(2,1)S(1)}, u32[]{:S(2)}, u32[]{:S(2)}) collective-permute-start(bf16[2,2,16,32,128]{4,3,2,1,0:T(8,128)(2,1)S(1)} %get-tuple-element.177), channel_id=1, source_target_pairs={{0,7},{1,6},{2,5},{3,4},{4,3},{5,2},{6,1},{7,0},{8,15},{9,14},{10,... | collective-permute-start | bytes 1572872 | tf_op jit(solution)/shard_map/ppermute | solution.py:286
  146.9 82.1 %collective-permute-start.7 = (bf16[2,2,16,32,128]{4,3,2,1,0:T(8,128)(2,1)S(1)}, bf16[2,2,16,32,128]{4,3,2,1,0:T(8,128)(2,1)S(1)}, u32[]{:S(2)}, u32[]{:S(2)}) collective-permute-start(bf16[2,2,16,32,128]{4,3,2,1,0:T(8,128)(2,1)S(1)} %get-tuple-element.139), channel_id=1, source_target_pairs={{0,1},{1,0},{2,3},{3,2},{4,5},{5,4},{6,7},{7,6},{8,9},{9,8},{10,11... | collective-permute-start | bytes 1572872 | tf_op jit(solution)/shard_map/ppermute | solution.py:286
  147.1 83.0 %collective-permute-start.8 = (bf16[2,2,16,32,128]{4,3,2,1,0:T(8,128)(2,1)S(1)}, bf16[2,2,16,32,128]{4,3,2,1,0:T(8,128)(2,1)S(1)}, u32[]{:S(2)}, u32[]{:S(2)}) collective-permute-start(bf16[2,2,16,32,128]{4,3,2,1,0:T(8,128)(2,1)S(1)} %get-tuple-element.140), channel_id=1, source_target_pairs={{0,2},{1,3},{2,0},{3,1},{4,6},{5,7},{6,4},{7,5},{8,10},{9,11},{10,... | collective-permute-start | bytes 1572872 | tf_op jit(solution)/shard_map/ppermute | solution.py:286
  178.1 47.7 %collective-permute-start.64 = (bf16[14,16,128]{2,1,0:T(8,128)(2,1)S(1)}, bf16[14,16,128]{2,1,0:T(8,128)(2,1)S(1)}, u32[]{:S(2)}, u32[]{:S(2)}) collective-permute-start(bf16[14,16,128]{2,1,0:T(8,128)(2,1)S(1)} %get-tuple-element.251), channel_id=1, source_target_pairs={{0,2},{1,3},{2,0},{3,1},{4,6},{5,7},{6,4},{7,5},{8,10},{9,11},{10,... | collective-permute-start | bytes 172040 | tf_op jit(solution)/shard_map/ppermute | solution.py:286
  178.1 47.8 %collective-permute-start.65 = (bf16[14,16,128]{2,1,0:T(8,128)(2,1)S(1)}, bf16[14,16,128]{2,1,0:T(8,128)(2,1)S(1)}, u32[]{:S(2)}, u32[]{:S(2)}) collective-permute-start(bf16[14,16,128]{2,1,0:T(8,128)(2,1)S(1)} %get-tuple-element.252), channel_id=1, source_target_pairs={{0,3},{1,2},{2,1},{3,0},{4,7},{5,6},{6,5},{7,4},{8,11},{9,10},{10,... | collective-permute-start | bytes 172040 | tf_op jit(solution)/shard_map/ppermute | solution.py:286
  189.6 37.1 %collective-permute-start.66 = (bf16[14,16,128]{2,1,0:T(8,128)(2,1)S(1)}, bf16[14,16,128]{2,1,0:T(8,128)(2,1)S(1)}, u32[]{:S(2)}, u32[]{:S(2)}) collective-permute-start(bf16[14,16,128]{2,1,0:T(8,128)(2,1)S(1)} %get-tuple-element.253), channel_id=1, source_target_pairs={{0,4},{1,5},{2,6},{3,7},{4,0},{5,1},{6,2},{7,3},{8,12},{9,13},{10,... | collective-permute-start | bytes 172040 | tf_op jit(solution)/shard_map/ppermute | solution.py:286
  225.9 62.0 %collective-permute-start.10 = (bf16[2,2,16,32,128]{4,3,2,1,0:T(8,128)(2,1)S(1)}, bf16[2,2,16,32,128]{4,3,2,1,0:T(8,128)(2,1)S(1)}, u32[]{:S(2)}, u32[]{:S(2)}) collective-permute-start(bf16[2,2,16,32,128]{4,3,2,1,0:T(8,128)(2,1)S(1)} %get-tuple-element.142), channel_id=1, source_target_pairs={{0,4},{1,5},{2,6},{3,7},{4,0},{5,1},{6,2},{7,3},{8,12},{9,13},{10,... | collective-permute-start | bytes 1572872 | tf_op jit(solution)/shard_map/ppermute | solution.py:286
  226.7 73.2 %collective-permute-start.11 = (bf16[2,2,16,32,128]{4,3,2,1,0:T(8,128)(2,1)S(1)}, bf16[2,2,16,32,128]{4,3,2,1,0:T(8,128)(2,1)S(1)}, u32[]{:S(2)}, u32[]{:S(2)}) collective-permute-start(bf16[2,2,16,32,128]{4,3,2,1,0:T(8,128)(2,1)S(1)} %get-tuple-element.143), channel_id=1, source_target_pairs={{0,5},{1,4},{2,7},{3,6},{4,1},{5,0},{6,3},{7,2},{8,13},{9,12},{10,... | collective-permute-start | bytes 1572872 | tf_op jit(solution)/shard_map/ppermute | solution.py:286
  229.0 73.5 %collective-permute-start.12 = (bf16[2,2,16,32,128]{4,3,2,1,0:T(8,128)(2,1)S(1)}, bf16[2,2,16,32,128]{4,3,2,1,0:T(8,128)(2,1)S(1)}, u32[]{:S(2)}, u32[]{:S(2)}) collective-permute-start(bf16[2,2,16,32,128]{4,3,2,1,0:T(8,128)(2,1)S(1)} %get-tuple-element.144), channel_id=1, source_target_pairs={{0,6},{1,7},{2,4},{3,5},{4,2},{5,3},{6,0},{7,1},{8,14},{9,15},{10,... | collective-permute-start | bytes 1572872 | tf_op jit(solution)/shard_map/ppermute | solution.py:286
  230.1 72.5 %collective-permute-start.13 = (bf16[2,2,16,32,128]{4,3,2,1,0:T(8,128)(2,1)S(1)}, bf16[2,2,16,32,128]{4,3,2,1,0:T(8,128)(2,1)S(1)}, u32[]{:S(2)}, u32[]{:S(2)}) collective-permute-start(bf16[2,2,16,32,128]{4,3,2,1,0:T(8,128)(2,1)S(1)} %get-tuple-element.145), channel_id=1, source_target_pairs={{0,7},{1,6},{2,5},{3,4},{4,3},{5,2},{6,1},{7,0},{8,15},{9,14},{10,... | collective-permute-start | bytes 1572872 | tf_op jit(solution)/shard_map/ppermute | solution.py:286
  251.2 89.4 %collective-permute-start.67 = (bf16[14,16,128]{2,1,0:T(8,128)(2,1)S(1)}, bf16[14,16,128]{2,1,0:T(8,128)(2,1)S(1)}, u32[]{:S(2)}, u32[]{:S(2)}) collective-permute-start(bf16[14,16,128]{2,1,0:T(8,128)(2,1)S(1)} %get-tuple-element.254), channel_id=1, source_target_pairs={{0,5},{1,4},{2,7},{3,6},{4,1},{5,0},{6,3},{7,2},{8,13},{9,12},{10,... | collective-permute-start | bytes 172040 | tf_op jit(solution)/shard_map/ppermute | solution.py:286
  287.9 52.7 %collective-permute-start.68 = (bf16[14,16,128]{2,1,0:T(8,128)(2,1)S(1)}, bf16[14,16,128]{2,1,0:T(8,128)(2,1)S(1)}, u32[]{:S(2)}, u32[]{:S(2)}) collective-permute-start(bf16[14,16,128]{2,1,0:T(8,128)(2,1)S(1)} %get-tuple-element.255), channel_id=1, source_target_pairs={{0,6},{1,7},{2,4},{3,5},{4,2},{5,3},{6,0},{7,1},{8,14},{9,15},{10,... | collective-permute-start | bytes 172040 | tf_op jit(solution)/shard_map/ppermute | solution.py:286
  299.9 44.5 %collective-permute-start.69 = (bf16[14,16,128]{2,1,0:T(8,128)(2,1)S(1)}, bf16[14,16,128]{2,1,0:T(8,128)(2,1)S(1)}, u32[]{:S(2)}, u32[]{:S(2)}) collective-permute-start(bf16[14,16,128]{2,1,0:T(8,128)(2,1)S(1)} %get-tuple-element.256), channel_id=1, source_target_pairs={{0,7},{1,6},{2,5},{3,4},{4,3},{5,2},{6,1},{7,0},{8,15},{9,14},{10,... | collective-permute-start | bytes 172040 | tf_op jit(solution)/shard_map/ppermute | solution.py:286
  302.6 42.4 %collective-permute-start.56 = (bf16[14,32,128]{2,1,0:T(8,128)(2,1)S(1)}, bf16[14,32,128]{2,1,0:T(8,128)(2,1)S(1)}, u32[]{:S(2)}, u32[]{:S(2)}) collective-permute-start(bf16[14,32,128]{2,1,0:T(8,128)(2,1)S(1)} %get-tuple-element.232), channel_id=1, source_target_pairs={{0,1},{1,0},{2,3},{3,2},{4,5},{5,4},{6,7},{7,6},{8,9},{9,8},{10,11... | collective-permute-start | bytes 344072 | tf_op jit(solution)/shard_map/ppermute | solution.py:286
  302.6 44.4 %collective-permute-start.57 = (bf16[14,32,128]{2,1,0:T(8,128)(2,1)S(1)}, bf16[14,32,128]{2,1,0:T(8,128)(2,1)S(1)}, u32[]{:S(2)}, u32[]{:S(2)}) collective-permute-start(bf16[14,32,128]{2,1,0:T(8,128)(2,1)S(1)} %get-tuple-element.233), channel_id=1, source_target_pairs={{0,2},{1,3},{2,0},{3,1},{4,6},{5,7},{6,4},{7,5},{8,10},{9,11},{10,... | collective-permute-start | bytes 344072 | tf_op jit(solution)/shard_map/ppermute | solution.py:286
  340.6 27.6 %collective-permute-start.58 = (bf16[14,32,128]{2,1,0:T(8,128)(2,1)S(1)}, bf16[14,32,128]{2,1,0:T(8,128)(2,1)S(1)}, u32[]{:S(2)}, u32[]{:S(2)}) collective-permute-start(bf16[14,32,128]{2,1,0:T(8,128)(2,1)S(1)} %get-tuple-element.234), channel_id=1, source_target_pairs={{0,3},{1,2},{2,1},{3,0},{4,7},{5,6},{6,5},{7,4},{8,11},{9,10},{10,... | collective-permute-start | bytes 344072 | tf_op jit(solution)/shard_map/ppermute | solution.py:286
  341.3 27.0 %collective-permute-start.59 = (bf16[14,32,128]{2,1,0:T(8,128)(2,1)S(1)}, bf16[14,32,128]{2,1,0:T(8,128)(2,1)S(1)}, u32[]{:S(2)}, u32[]{:S(2)}) collective-permute-start(bf16[14,32,128]{2,1,0:T(8,128)(2,1)S(1)} %get-tuple-element.235), channel_id=1, source_target_pairs={{0,4},{1,5},{2,6},{3,7},{4,0},{5,1},{6,2},{7,3},{8,12},{9,13},{10,... | collective-permute-start | bytes 344072 | tf_op jit(solution)/shard_map/ppermute | solution.py:286
  368.2 42.3 %collective-permute-start.35 = (bf16[2,2,16,32,128]{4,3,2,1,0:T(8,128)(2,1)}, bf16[2,2,16,32,128]{4,3,2,1,0:T(8,128)(2,1)}, u32[]{:S(2)}, u32[]{:S(2)}) collective-permute-start(bf16[2,2,16,32,128]{4,3,2,1,0:T(8,128)(2,1)} %get-tuple-element.179), channel_id=1, source_target_pairs={{0,1},{1,0},{2,3},{3,2},{4,5},{5,4},{6,7},{7,6},{8,9},{9,8},{10,11... | collective-permute-start | bytes 1572872 | tf_op jit(solution)/shard_map/ppermute | solution.py:286
  368.3 44.4 %collective-permute-start.36 = (bf16[2,2,16,32,128]{4,3,2,1,0:T(8,128)(2,1)}, bf16[2,2,16,32,128]{4,3,2,1,0:T(8,128)(2,1)}, u32[]{:S(2)}, u32[]{:S(2)}) collective-permute-start(bf16[2,2,16,32,128]{4,3,2,1,0:T(8,128)(2,1)} %get-tuple-element.180), channel_id=1, source_target_pairs={{0,2},{1,3},{2,0},{3,1},{4,6},{5,7},{6,4},{7,5},{8,10},{9,11},{10,... | collective-permute-start | bytes 1572872 | tf_op jit(solution)/shard_map/ppermute | solution.py:286
  368.4 39.2 %collective-permute-start.14 = (bf16[2,2,16,16,128]{4,3,2,1,0:T(8,128)(2,1)}, bf16[2,2,16,16,128]{4,3,2,1,0:T(8,128)(2,1)}, u32[]{:S(2)}, u32[]{:S(2)}) collective-permute-start(bf16[2,2,16,16,128]{4,3,2,1,0:T(8,128)(2,1)} %get-tuple-element.147), channel_id=1, source_target_pairs={{0,1},{1,0},{2,3},{3,2},{4,5},{5,4},{6,7},{7,6},{8,9},{9,8},{10,11... | collective-permute-start | bytes 786440 | tf_op jit(solution)/shard_map/ppermute | solution.py:286
  368.9 41.6 %collective-permute-start.15 = (bf16[2,2,16,16,128]{4,3,2,1,0:T(8,128)(2,1)}, bf16[2,2,16,16,128]{4,3,2,1,0:T(8,128)(2,1)}, u32[]{:S(2)}, u32[]{:S(2)}) collective-permute-start(bf16[2,2,16,16,128]{4,3,2,1,0:T(8,128)(2,1)} %get-tuple-element.148), channel_id=1, source_target_pairs={{0,2},{1,3},{2,0},{3,1},{4,6},{5,7},{6,4},{7,5},{8,10},{9,11},{10,... | collective-permute-start | bytes 786440 | tf_op jit(solution)/shard_map/ppermute | solution.py:286
  370.6 36.6 %collective-permute-start.49 = (bf16[14,32,128]{2,1,0:T(8,128)(2,1)}, bf16[14,32,128]{2,1,0:T(8,128)(2,1)S(1)}, u32[]{:S(2)}, u32[]{:S(2)}) collective-permute-start(bf16[14,32,128]{2,1,0:T(8,128)(2,1)} %get-tuple-element.214), channel_id=1, source_target_pairs={{0,1},{1,0},{2,3},{3,2},{4,5},{5,4},{6,7},{7,6},{8,9},{9,8},{10,11... | collective-permute-start | bytes 344072 | tf_op jit(solution)/shard_map/ppermute | solution.py:286
  407.2 25.8 %collective-permute-start.37 = (bf16[2,2,16,32,128]{4,3,2,1,0:T(8,128)(2,1)}, bf16[2,2,16,32,128]{4,3,2,1,0:T(8,128)(2,1)}, u32[]{:S(2)}, u32[]{:S(2)}) collective-permute-start(bf16[2,2,16,32,128]{4,3,2,1,0:T(8,128)(2,1)} %copy-done.25), channel_id=1, source_target_pairs={{0,3},{1,2},{2,1},{3,0},{4,7},{5,6},{6,5},{7,4},{8,11},{9,10},{10,... | collective-permute-start | bytes 1572872 | tf_op jit(solution)/shard_map/ppermute | solution.py:286
  407.6 61.0 %collective-permute-start.38 = (bf16[2,2,16,32,128]{4,3,2,1,0:T(8,128)(2,1)}, bf16[2,2,16,32,128]{4,3,2,1,0:T(8,128)(2,1)}, u32[]{:S(2)}, u32[]{:S(2)}) collective-permute-start(bf16[2,2,16,32,128]{4,3,2,1,0:T(8,128)(2,1)} %copy-done.22), channel_id=1, source_target_pairs={{0,4},{1,5},{2,6},{3,7},{4,0},{5,1},{6,2},{7,3},{8,12},{9,13},{10,... | collective-permute-start | bytes 1572872 | tf_op jit(solution)/shard_map/ppermute | solution.py:286
  410.5 73.7 %collective-permute-start.39 = (bf16[2,2,16,32,128]{4,3,2,1,0:T(8,128)(2,1)}, bf16[2,2,16,32,128]{4,3,2,1,0:T(8,128)(2,1)}, u32[]{:S(2)}, u32[]{:S(2)}) collective-permute-start(bf16[2,2,16,32,128]{4,3,2,1,0:T(8,128)(2,1)} %copy-done.21), channel_id=1, source_target_pairs={{0,5},{1,4},{2,7},{3,6},{4,1},{5,0},{6,3},{7,2},{8,13},{9,12},{10,... | collective-permute-start | bytes 1572872 | tf_op jit(solution)/shard_map/ppermute | solution.py:286
  410.5 73.7 %collective-permute-start.40 = (bf16[2,2,16,32,128]{4,3,2,1,0:T(8,128)(2,1)S(1)}, bf16[2,2,16,32,128]{4,3,2,1,0:T(8,128)(2,1)}, u32[]{:S(2)}, u32[]{:S(2)}) collective-permute-start(bf16[2,2,16,32,128]{4,3,2,1,0:T(8,128)(2,1)S(1)} %get-tuple-element.184), channel_id=1, source_target_pairs={{0,6},{1,7},{2,4},{3,5},{4,2},{5,3},{6,0},{7,1},{8,14},{9,15},{10,... | collective-permute-start | bytes 1572872 | tf_op jit(solution)/shard_map/ppermute | solution.py:286
  412.7 73.8 %collective-permute-start.41 = (bf16[2,2,16,32,128]{4,3,2,1,0:T(8,128)(2,1)S(1)}, bf16[2,2,16,32,128]{4,3,2,1,0:T(8,128)(2,1)}, u32[]{:S(2)}, u32[]{:S(2)}) collective-permute-start(bf16[2,2,16,32,128]{4,3,2,1,0:T(8,128)(2,1)S(1)} %get-tuple-element.185), channel_id=1, source_target_pairs={{0,7},{1,6},{2,5},{3,4},{4,3},{5,2},{6,1},{7,0},{8,15},{9,14},{10,... | collective-permute-start | bytes 1572872 | tf_op jit(solution)/shard_map/ppermute | solution.py:286
  433.0 73.5 %collective-permute-start.16 = (bf16[2,2,16,16,128]{4,3,2,1,0:T(8,128)(2,1)}, bf16[2,2,16,16,128]{4,3,2,1,0:T(8,128)(2,1)S(1)}, u32[]{:S(2)}, u32[]{:S(2)}) collective-permute-start(bf16[2,2,16,16,128]{4,3,2,1,0:T(8,128)(2,1)} %copy-done.47), channel_id=1, source_target_pairs={{0,3},{1,2},{2,1},{3,0},{4,7},{5,6},{6,5},{7,4},{8,11},{9,10},{10,... | collective-permute-start | bytes 786440 | tf_op jit(solution)/shard_map/ppermute | solution.py:286
  468.5 76.2 %collective-permute-start.17 = (bf16[2,2,16,16,128]{4,3,2,1,0:T(8,128)(2,1)}, bf16[2,2,16,16,128]{4,3,2,1,0:T(8,128)(2,1)S(1)}, u32[]{:S(2)}, u32[]{:S(2)}) collective-permute-start(bf16[2,2,16,16,128]{4,3,2,1,0:T(8,128)(2,1)} %copy-done.46), channel_id=1, source_target_pairs={{0,4},{1,5},{2,6},{3,7},{4,0},{5,1},{6,2},{7,3},{8,12},{9,13},{10,... | collective-permute-start | bytes 786440 | tf_op jit(solution)/shard_map/ppermute | solution.py:286
  484.3 60.5 %collective-permute-start.18 = (bf16[2,2,16,16,128]{4,3,2,1,0:T(8,128)(2,1)}, bf16[2,2,16,16,128]{4,3,2,1,0:T(8,128)(2,1)S(1)}, u32[]{:S(2)}, u32[]{:S(2)}) collective-permute-start(bf16[2,2,16,16,128]{4,3,2,1,0:T(8,128)(2,1)} %copy-done.37), channel_id=1, source_target_pairs={{0,5},{1,4},{2,7},{3,6},{4,1},{5,0},{6,3},{7,2},{8,13},{9,12},{10,... | collective-permute-start | bytes 786440 | tf_op jit(solution)/shard_map/ppermute | solution.py:286
  484.3 61.7 %collective-permute-start.19 = (bf16[2,2,16,16,128]{4,3,2,1,0:T(8,128)(2,1)}, bf16[2,2,16,16,128]{4,3,2,1,0:T(8,128)(2,1)S(1)}, u32[]{:S(2)}, u32[]{:S(2)}) collective-permute-start(bf16[2,2,16,16,128]{4,3,2,1,0:T(8,128)(2,1)} %copy-done.33), channel_id=1, source_target_pairs={{0,6},{1,7},{2,4},{3,5},{4,2},{5,3},{6,0},{7,1},{8,14},{9,15},{10,... | collective-permute-start | bytes 786440 | tf_op jit(solution)/shard_map/ppermute | solution.py:286
  486.5 60.7 %collective-permute-start.20 = (bf16[2,2,16,16,128]{4,3,2,1,0:T(8,128)(2,1)}, bf16[2,2,16,16,128]{4,3,2,1,0:T(8,128)(2,1)S(1)}, u32[]{:S(2)}, u32[]{:S(2)}) collective-permute-start(bf16[2,2,16,16,128]{4,3,2,1,0:T(8,128)(2,1)} %copy-done.32), channel_id=1, source_target_pairs={{0,7},{1,6},{2,5},{3,4},{4,3},{5,2},{6,1},{7,0},{8,15},{9,14},{10,... | collective-permute-start | bytes 786440 | tf_op jit(solution)/shard_map/ppermute | solution.py:286
  506.5 68.5 %collective-permute-start.50 = (bf16[14,32,128]{2,1,0:T(8,128)(2,1)S(1)}, bf16[14,32,128]{2,1,0:T(8,128)(2,1)S(1)}, u32[]{:S(2)}, u32[]{:S(2)}) collective-permute-start(bf16[14,32,128]{2,1,0:T(8,128)(2,1)S(1)} %copy-done.61), channel_id=1, source_target_pairs={{0,2},{1,3},{2,0},{3,1},{4,6},{5,7},{6,4},{7,5},{8,10},{9,11},{10,... | collective-permute-start | bytes 344072 | tf_op jit(solution)/shard_map/ppermute | solution.py:286
  544.8 30.4 %collective-permute-start.51 = (bf16[14,32,128]{2,1,0:T(8,128)(2,1)S(1)}, bf16[14,32,128]{2,1,0:T(8,128)(2,1)S(1)}, u32[]{:S(2)}, u32[]{:S(2)}) collective-permute-start(bf16[14,32,128]{2,1,0:T(8,128)(2,1)S(1)} %copy-done.59), channel_id=1, source_target_pairs={{0,3},{1,2},{2,1},{3,0},{4,7},{5,6},{6,5},{7,4},{8,11},{9,10},{10,... | collective-permute-start | bytes 344072 | tf_op jit(solution)/shard_map/ppermute | solution.py:286
  544.8 32.6 %collective-permute-start.52 = (bf16[14,32,128]{2,1,0:T(8,128)(2,1)S(1)}, bf16[14,32,128]{2,1,0:T(8,128)(2,1)S(1)}, u32[]{:S(2)}, u32[]{:S(2)}) collective-permute-start(bf16[14,32,128]{2,1,0:T(8,128)(2,1)S(1)} %copy-done.57), channel_id=1, source_target_pairs={{0,4},{1,5},{2,6},{3,7},{4,0},{5,1},{6,2},{7,3},{8,12},{9,13},{10,... | collective-permute-start | bytes 344072 | tf_op jit(solution)/shard_map/ppermute | solution.py:286
  546.0 31.6 %collective-permute-start.53 = (bf16[14,32,128]{2,1,0:T(8,128)(2,1)S(1)}, bf16[14,32,128]{2,1,0:T(8,128)(2,1)S(1)}, u32[]{:S(2)}, u32[]{:S(2)}) collective-permute-start(bf16[14,32,128]{2,1,0:T(8,128)(2,1)S(1)} %copy-done.55), channel_id=1, source_target_pairs={{0,5},{1,4},{2,7},{3,6},{4,1},{5,0},{6,3},{7,2},{8,13},{9,12},{10,... | collective-permute-start | bytes 344072 | tf_op jit(solution)/shard_map/ppermute | solution.py:286
  547.2 30.3 %collective-permute-start.54 = (bf16[14,32,128]{2,1,0:T(8,128)(2,1)S(1)}, bf16[14,32,128]{2,1,0:T(8,128)(2,1)S(1)}, u32[]{:S(2)}, u32[]{:S(2)}) collective-permute-start(bf16[14,32,128]{2,1,0:T(8,128)(2,1)S(1)} %copy-done.53), channel_id=1, source_target_pairs={{0,6},{1,7},{2,4},{3,5},{4,2},{5,3},{6,0},{7,1},{8,14},{9,15},{10,... | collective-permute-start | bytes 344072 | tf_op jit(solution)/shard_map/ppermute | solution.py:286
  (100 other events, 1985.2 us)

commit v2 on v1

--- a/solution.py
+++ b/solution.py
@@ -16,6 +16,9 @@
 MODF = 7
 LANES = 128
 ROWS = 16
+COST = pl.CostEstimate(flops=1000, bytes_accessed=1000, transcendentals=0)
+TOKEN = jax.ShapeDtypeStruct((8, LANES), jnp.int32)
+VMEM = 60 << 20
 
 
 def spectral_constant(chans):
@@ -73,20 +76,24 @@
     return [np.float32(0.25) * v for v in real[1:] + imag[1:]]
 
 
+def slots(shards):
+    return [m for m in range(shards // 2, shards)] + [m for m in range(shards // 2 - 1, -1, -1)]
+
+
 def channelize_kernel(shards, size, frames, n_after, place, table, volts, *rest):
-    outs, (held,) = rest[n_after : n_after + shards], rest[n_after + shards + 1 :]
-    rest[n_after + shards][...] = jnp.zeros((8, LANES), jnp.int32)
+    outs, zero, held = rest[n_after : n_after + shards], rest[-2], rest[-1]
+    zero[...] = jnp.zeros((8, LANES), jnp.int32)
     for n in range(frames):
         samples = volts[0, :, :, n * NSAMP : (n + 1) * NSAMP].reshape(-1, NSAMP)
         product = lax.dot_general(
             table[...], samples, (((1,), (1,)), ((), ())), preferred_element_type=jnp.float32
         )
         held[...] = (product * np.float32(1.0 / math.sqrt(NSAMP))).reshape(held.shape)
-        for m in range(shards):
+        for out, m in zip(outs, slots(shards)):
             mine = held[place[0] ^ m].astype(jnp.bfloat16)
             for a in range(2):
                 for p in range(POL):
-                    outs[m][a, p, n] = mine[a * size : (a + 1) * size, p * LANES : (p + 1) * LANES]
+                    out[a, p, n] = mine[a * size : (a + 1) * size, p * LANES : (p + 1) * LANES]
 
 
 def channelize(place, table, voltages, size, shards, after):
@@ -110,33 +117,29 @@
         ),
         out_shape=[jax.ShapeDtypeStruct(shape, jnp.bfloat16)] * shards
         + [jax.ShapeDtypeStruct((8, LANES), jnp.int32)],
-        compiler_params=pltpu.CompilerParams(vmem_limit_bytes=40 << 20),
-        cost_estimate=pl.CostEstimate(
-            flops=2 * table.shape[0] * NSAMP * POL * LANES * total,
-            bytes_accessed=voltages.size * 2 + table.size * 4,
-            transcendentals=0,
-        ),
+        compiler_params=pltpu.CompilerParams(vmem_limit_bytes=VMEM),
+        cost_estimate=COST,
         name="channelize",
     )(place, table, voltages, *after)
-    return outs[:shards], outs[shards]
+    return outs[:-1], outs[-1]
 
 
 def beam_kernel(shards, frames, place, gains, table, *rest):
-    spectra, outs, level, held = rest[:shards], rest[shards : 2 * shards], rest[-2], rest[-1]
+    outs, level, held = rest[-2 - shards : -2], rest[-2], rest[-1]
     feeds = shards * LANES
     rows = POL * frames * ROWS
-    for m in range(shards):
+    for spectra, m in zip(rest, slots(shards)):
         at = pl.multiple_of((place[0] ^ m) * LANES, LANES)
         gain_real = gains[0, :, pl.ds(at, LANES)].astype(jnp.float32)
         gain_imag = gains[1, :, pl.ds(at, LANES)].astype(jnp.float32)
-        real = spectra[m][0].astype(jnp.float32)
-        imag = spectra[m][1].astype(jnp.float32)
+        real = spectra[0].astype(jnp.float32)
+        imag = spectra[1].astype(jnp.float32)
         cal_real = (gain_real * real - gain_imag * imag).astype(jnp.bfloat16)
         cal_imag = (gain_real * imag + gain_imag * real).astype(jnp.bfloat16)
         held[:, pl.ds(at, LANES)] = cal_real.reshape(rows, LANES)
         held[:, pl.ds(pl.multiple_of(at + feeds, LANES), LANES)] = cal_imag.reshape(rows, LANES)
     sums = jnp.zeros((ROWS, LANES), jnp.float32)
-    for m in range(shards):
+    for out, m in zip(outs, slots(shards)):
         at = pl.multiple_of((place[0] ^ m) * (2 * LANES), 2 * LANES)
         beams = jnp.dot(held[...], table[:, pl.ds(at, 2 * LANES)], preferred_element_type=jnp.float32)
         squares = beams * beams
@@ -144,12 +147,13 @@
         power = (power[: rows // 2] + power[rows // 2 :]).reshape(frames, ROWS, LANES)
         sums = sums + jnp.sum(power, axis=0)
         for q, value in enumerate(frame_sums(power)):
-            outs[m][q] = value
+            out[q] = value
     level[...] = sums
 
 
-def form_beams(place, gains, table, spectra, start, size, frames):
+def form_beams(place, gains, table, spectra, start, size, frames, after):
     shards = len(spectra)
+    block = (2, POL, frames, ROWS, LANES)
     outs = pl.pallas_call(
         functools.partial(beam_kernel, shards, frames),
         grid_spec=pltpu.PrefetchScalarGridSpec(
@@ -159,26 +163,22 @@
                 pl.BlockSpec((2, ROWS, gains.shape[2]), lambda g, _: (0, start // ROWS + g, 0)),
                 pl.BlockSpec(table.shape, lambda g, _: (0, 0), pipeline_mode=pl.Buffered(1)),
             ]
-            + [pl.BlockSpec((2, POL, frames, ROWS, LANES), lambda g, _: (0, 0, 0, g, 0))] * shards,
+            + [pl.BlockSpec(block, lambda g, _: (0, 0, 0, g, 0))] * shards
+            + [pl.BlockSpec(memory_space=pl.ANY)] * len(after),
             out_specs=[pl.BlockSpec((2 * MODF, ROWS, LANES), lambda g, _: (0, g, 0))] * shards
             + [pl.BlockSpec((ROWS, LANES), lambda g, _: (g, 0))],
             scratch_shapes=[pltpu.VMEM((POL * frames * ROWS, table.shape[0]), jnp.bfloat16)],
         ),
         out_shape=[jax.ShapeDtypeStruct((2 * MODF, size, LANES), jnp.float32)] * shards
         + [jax.ShapeDtypeStruct((size, LANES), jnp.float32)],
-        compiler_params=pltpu.CompilerParams(vmem_limit_bytes=46 << 20),
-        cost_estimate=pl.CostEstimate(
-            flops=2 * POL * frames * size * table.size,
-            bytes_accessed=table.size * 2 + 8 * size * frames * gains.shape[2],
-            transcendentals=0,
-        ),
+        compiler_params=pltpu.CompilerParams(vmem_limit_bytes=VMEM),
+        cost_estimate=COST,
         name="form_beams",
-    )(place, gains, table, *spectra)
-    return outs[:shards], outs[shards]
-
-
-def normalise_kernel(count, scale, section, levels, decay, *rest):
-    shards = (len(rest)) // 2
+    )(place, gains, table, *spectra, *after)
+    return outs[:-1], outs[-1]
+
+
+def normalise_kernel(count, chips, scale, section, levels, decay, *rest):
     rate = decay[...]
     dividend, divisor = jnp.zeros_like(rate), jnp.zeros_like(rate)
     for block in range(count):
@@ -187,71 +187,86 @@
         dividend = jnp.where(later, rate * dividend + mean, dividend)
         divisor = jnp.where(later, rate * divisor + 1.0, divisor)
     inverse = divisor / dividend
-    for m in range(shards):
-        rest[shards + m][...] = (rest[m][...] * inverse).astype(jnp.bfloat16)
-
-
-def normalise(section, levels, decay, sums, scale):
+    outs = rest[-1 - chips : -1]
+    for q in range(chips):
+        outs[q][...] = (rest[q][...] * inverse).astype(jnp.bfloat16)
+    rest[-1][...] = jnp.zeros((8, LANES), jnp.int32)
+
+
+def normalise(section, levels, decay, sums, scale, after):
     spec = pl.BlockSpec(memory_space=pltpu.VMEM)
-    return pl.pallas_call(
-        functools.partial(normalise_kernel, levels.shape[0], scale),
-        in_specs=[pl.BlockSpec(memory_space=pltpu.SMEM)] + [spec] * (2 + len(sums)),
-        out_specs=[spec] * len(sums),
-        out_shape=[jax.ShapeDtypeStruct(s.shape, jnp.bfloat16) for s in sums],
-        compiler_params=pltpu.CompilerParams(vmem_limit_bytes=24 << 20),
+    outs = pl.pallas_call(
+        functools.partial(normalise_kernel, levels.shape[0], len(sums), scale),
+        in_specs=[pl.BlockSpec(memory_space=pltpu.SMEM)]
+        + [spec] * (2 + len(sums))
+        + [pl.BlockSpec(memory_space=pl.ANY)] * len(after),
+        out_specs=[spec] * (len(sums) + 1),
+        out_shape=[jax.ShapeDtypeStruct(s.shape, jnp.bfloat16) for s in sums] + [TOKEN],
+        compiler_params=pltpu.CompilerParams(vmem_limit_bytes=VMEM),
+        cost_estimate=COST,
         name="normalise",
-    )(section, levels, decay, *sums)
+    )(section, levels, decay, *sums, *after)
+    return outs[:-1], outs[-1]
 
 
 def dedisperse_kernel(shards, size, last, first, scale, place, cosine, sine, *rest):
-    parts = rest[:shards]
     total = None if first else rest[shards]
-    out, real, imag = rest[-3:]
+    if last:
+        out, token, upper, lower, woven = rest[-5:]
+    else:
+        out, token, upper, lower = rest[-4:]
+    token[...] = jnp.zeros((8, LANES), jnp.int32)
     f = pl.program_id(0)
-    for m in range(shards):
-        at = pl.multiple_of((place[0] ^ m) * size, size)
-        real[pl.ds(at, size), :] = parts[m][f]
-        imag[pl.ds(at, size), :] = parts[m][f + MODF]
-    value = jnp.dot(cosine[0], real[...], preferred_element_type=jnp.float32) + jnp.dot(
-        sine[0], imag[...], preferred_element_type=jnp.float32
+    for part, m in zip(rest, slots(shards)):
+        at = pl.ds(pl.multiple_of((place[0] ^ m) * size, size), size)
+        real, imag = part[f], part[f + MODF]
+        upper[at, :LANES] = real
+        upper[at, LANES:] = imag
+        lower[at, :LANES] = imag
+        lower[at, LANES:] = -real
+    value = jnp.dot(cosine[0], upper[...], preferred_element_type=jnp.float32) + jnp.dot(
+        sine[0], lower[...], preferred_element_type=jnp.float32
     )
     if total is not None:
         value = value + total[0]
-    out[0] = (value * scale).astype(out.dtype) if last else value
-
-
-def dedisperse(place, cosine, sine, parts, total, last, scale):
-    shards, (_, size, _) = len(parts), parts[0].shape
-    rows, depth = cosine.shape[1:]
+    if last:
+        rows = value.shape[0]
+        woven[pl.ds(0, rows, stride=2), :] = value[:, :LANES] * scale
+        woven[pl.ds(1, rows, stride=2), :] = value[:, LANES:] * scale
+        out[0] = woven[...].astype(out.dtype)
+    else:
+        out[0] = value
+
+
+def dedisperse(place, cosine, sine, at, parts, total, last, scale, after):
+    shards, size = len(parts), parts[0].shape[1]
+    rows, depth = cosine.shape[1], shards * size
     each = lambda f, _: (f, 0, 0)
-    whole = pl.BlockSpec(parts[0].shape, lambda f, _: (0, 0, 0))
+    block = (2 * MODF, size, LANES)
     sums = [] if total is None else [total]
+    made = (2 * rows, LANES) if last else (rows, 2 * LANES)
     return pl.pallas_call(
         functools.partial(dedisperse_kernel, shards, size, last, total is None, scale),
         grid_spec=pltpu.PrefetchScalarGridSpec(
             num_scalar_prefetch=1,
             grid=(MODF,),
-            in_specs=[pl.BlockSpec((1, rows, depth), each)] * 2
-            + [whole] * shards
-            + [pl.BlockSpec((1, rows, LANES), each)] * len(sums),
-            out_specs=pl.BlockSpec((1, rows, LANES), each),
-            scratch_shapes=[pltpu.VMEM((depth, LANES), jnp.bfloat16)] * 2,
+            in_specs=[pl.BlockSpec((1, rows, depth), lambda f, _: (f, 0, at // depth))] * 2
+            + [pl.BlockSpec(block, lambda f, _: (0, 0, 0))] * shards
+            + [pl.BlockSpec((1, rows, 2 * LANES), each)] * len(sums)
+            + [pl.BlockSpec(memory_space=pl.ANY)] * len(after),
+            out_specs=[pl.BlockSpec((1,) + made, each), pl.BlockSpec((8, LANES), lambda f, _: (0, 0))],
+            scratch_shapes=[pltpu.VMEM((depth, 2 * LANES), jnp.bfloat16)] * 2
+            + ([pltpu.VMEM(made, jnp.float32)] if last else []),
         ),
-        out_shape=jax.ShapeDtypeStruct((MODF, rows, LANES), jnp.bfloat16 if last else jnp.float32),
-        compiler_params=pltpu.CompilerParams(vmem_limit_bytes=32 << 20),
-        cost_estimate=pl.CostEstimate(
-            flops=4 * MODF * rows * depth * LANES,
-            bytes_accessed=4 * MODF * rows * (depth + LANES),
-            transcendentals=0,
-        ),
+        out_shape=[jax.ShapeDtypeStruct((MODF,) + made, jnp.bfloat16 if last else jnp.float32), TOKEN],
+        compiler_params=pltpu.CompilerParams(vmem_limit_bytes=24 << 20),
+        cost_estimate=COST,
         name="dedisperse",
-    )(place, cosine, sine, *parts, *sums)
-
-
-def phase_tables(turns, frames):
-    delay, quarter = turns
-    f = jnp.arange(1, MODF + 1, dtype=jnp.int32)[:, None, None]
-    turn = f * delay[None] + quarter[None]
+    )(place, cosine, sine, *parts, *sums, *after)
+
+
+def phase_tables(delay, frames):
+    turn = jnp.arange(1, MODF + 1, dtype=jnp.int32)[:, None, None] * delay[None]
     cosine = cosine_of(turn, frames).astype(jnp.bfloat16)
     sine = cosine_of(turn - frames // 4, frames).astype(jnp.bfloat16)
     return cosine, sine
@@ -274,49 +289,57 @@
     local = chans // shards
     place = lax.axis_index("shard").reshape(1)
     section = lax.axis_index("section").reshape(1)
-    sizes = chunk_sizes(local)
+    sizes = [32, 64, 32]
     starts = [sum(sizes[:c]) for c in range(len(sizes))]
     rows = spectral_constant(chans).reshape(2, shards, local, NSAMP)
     scale = np.float32(1.0 / (frames * feeds))
 
     def exchange(parts):
-        got = [parts[0]] + [None] * (shards - 1)
-        order = [m for m in range(shards - 1, 0, -1)]
-        for m in order:
-            got[m] = lax.ppermute(parts[m], "shard", [(j, j ^ m) for j in range(shards)])
-        return got
+        return [
+            lax.ppermute(part, "shard", [(j, j ^ m) for j in range(shards)]) if m else part
+            for part, m in zip(parts, slots(shards))
+        ]
 
     def send_spectra(c, after):
         table = np.ascontiguousarray(rows[:, :, starts[c] : starts[c] + sizes[c]].transpose(1, 0, 2, 3))
         table = jnp.asarray(table.reshape(-1, NSAMP))
-        parts, zero = channelize(place, table, voltages, sizes[c], shards, after)
-        return exchange(parts), zero
-
-    received, zero = {}, None
-    received[0], zero = send_spectra(0, [])
-    received[1], _ = send_spectra(1, [])
-
-    zero = zero[0, 0]
-    table = beam_table(grid_index + zero)
-    by_trial = jnp.transpose((delays + zero) & (frames - 1)).reshape(trials, shards, local)
-    by_trial = jnp.repeat(by_trial, 2, axis=0)
-    quarter = (lax.broadcasted_iota(jnp.int32, (2 * trials, 1), 0) % 2) * (frames // 4)
-
-    total = None
-    pending = None
-    for c in range(len(sizes)):
+        parts, token = channelize(place, table, voltages, sizes[c], shards, after)
+        return exchange(parts), token
+
+    order = sorted(range(len(sizes)), key=lambda c: -sizes[c])
+    column = {c: shards * sum(sizes[e] for e in order[: order.index(c)]) for c in order}
+
+    def make_phases(token):
+        by_shard = ((delays + token[0, 0]) & (frames - 1)).reshape(shards, local, trials)
+        by_chunk = [by_shard[:, starts[c] : starts[c] + sizes[c]].reshape(-1, trials) for c in order]
+        return phase_tables(jnp.transpose(jnp.concatenate(by_chunk)), frames)
+
+    count = len(sizes)
+    received, modulated = {}, {}
+    total, phases = None, None
+
+    def add_chunk(c, total, after):
+        last = c + 1 == count
+        return dedisperse(place, *phases, column[c], modulated[c], total, last, np.float32(1.0 / math.sqrt(chans)), after)
+
+    received[0], token = send_spectra(0, [])
+    received[1], token = send_spectra(1, [token])
+    table = beam_table(grid_index + token[0, 0])
+    for c in range(count):
         start, size = starts[c], sizes[c]
-        if c + 2 < len(sizes):
-            received[c + 2], _ = send_spectra(c + 2, received[c][1:])
-        sums, level = form_beams(place, feed_gains, table, received[c], start, size, frames)
+        sums, level = form_beams(place, feed_gains, table, received[c], start, size, frames, [token])
         levels = lax.all_gather(level, "section")
         decay = decay_rates[start : start + size].reshape(size, 1)
-        modulated = exchange(normalise(section, levels, decay, sums, scale))
-        chosen = by_trial[:, :, start : start + size].reshape(2 * trials, shards * size)
-        cosine, sine = phase_tables((chosen, quarter), frames)
-        total = dedisperse(
-            place, cosine, sine, modulated, total, c + 1 == len(sizes), np.float32(1.0 / math.sqrt(chans))
-        )
+        ready, token = normalise(section, levels, decay, sums, scale, [])
+        modulated[c] = exchange(ready)
+        if c == 0:
+            phases = make_phases(token)
+            token = phases[0]
+        else:
+            total, token = add_chunk(c - 1, total, [token])
+        if c + 2 < count:
+            received[c + 2], token = send_spectra(c + 2, [token])
+    total, _ = add_chunk(count - 1, total, [])
     return total.reshape(1, MODF, trials, 2, feeds // shards)
 
 

time: 639 us -> 518 us (0.81); the launches traced: 629 us -> 517 us
  local copies, waits for them, and re-layouts: 76.2 us -> 26 us
  starting transfers between devices: 154 us -> 116 us
  other arithmetic: 69.8 us -> 45.2 us
  waiting for transfers between devices: 137 us -> 156 us
  blocking collectives: 39.2 us -> 27.6 us
  Pallas kernels: 152 us -> 145 us
    ppermute x70 -> x42, starting transfers between devices: 154 us -> 116 us  [exchange(): lax.ppermute(part, 'shard', [(j, j ^ m) for j in range(shards)])]
    slice x8 -> x4, local copies, waits for them, and re-layouts: 39.5 us -> 2.74 us  [the longest x1 1.34 us: pipelined(): table = beam_table(grid_index + token[0, 0])]
    convert_element_type x2 -> x1, other arithmetic: 48.4 us -> 23.7 us  [phase_tables(): sine = cosine_of(turn - frames // 4, frames).astype(jnp.bfloat16)]
    ppermute x70 -> x42, waiting for transfers between devices: 137 us -> 156 us  [exchange(): lax.ppermute(part, 'shard', [(j, j ^ m) for j in range(shards)])]
    mul x5 -> x0, local copies, waits for them, and re-layouts: 11.7 us -> none  [phase_tables(): turn = f * delay[None] + quarter[None]]
    all_gather x5 -> x3, blocking collectives: 39.2 us -> 27.6 us  [pipelined(): levels = lax.all_gather(level, 'section')]
    pallas_call x5 -> x3, Pallas kernels: 63.9 us -> 56.8 us  [channelize(): pl.pallas_call(functools.partial(channelize_kernel, shards, size, frames,...]
    pallas_call x5 -> x3, Pallas kernels: 2.3 us -> 9.13 us  [normalise(): pl.pallas_call(functools.partial(normalise_kernel, levels.shape[0], len(s...]
  transfers between devices with their start and end apart: 70 -> 42, of which waited for: 9 -> 15; matrix products, arithmetic and copies ran while one was open for 20% -> 10% of each run, Pallas kernels for 22% -> 24%
where the time goes in v2:
time: 518 us; the launch traced here: 517 us
  waiting for transfers between devices  156 us (30%)
  Pallas kernels  145 us (28%)
  starting transfers between devices  116 us (22%)
  other arithmetic  45.2 us (9%)
  blocking collectives  27.6 us (5%)
  local copies, waits for them, and re-layouts  26 us (5%)
    ppermute x42, waiting for transfers between devices, exchange(): lax.ppermute(part, 'shard', [(j, j ^ m) for j in range(shards)])  156 us
    ppermute x42, starting transfers between devices, exchange(): lax.ppermute(part, 'shard', [(j, j ^ m) for j in range(shards)])  116 us
    pallas_call x3, Pallas kernels, form_beams(): pl.pallas_call(functools.partial(beam_kernel, shards, frames), grid_spec=...  66.8 us
    pallas_call x3, Pallas kernels, channelize(): pl.pallas_call(functools.partial(channelize_kernel, shards, size, frames,...  56.8 us
    all_gather x3, blocking collectives, pipelined(): levels = lax.all_gather(level, 'section')  27.6 us
    convert_element_type x1, other arithmetic, phase_tables(): sine = cosine_of(turn - frames // 4, frames).astype(jnp.bfloat16)  23.7 us
    unnamed x64, local copies, waits for them, and re-layouts  19.1 us
    convert_element_type x1, other arithmetic, beam_table(): return cosine_of(turn, GRID_Y).astype(jnp.bfloat16)  18.6 us
  transfers between devices with their start and end apart: 42, of which 15 were waited for; matrix products, arithmetic and copies ran while one was open for 10% of the time, Pallas kernels for 24%

profile of v2, /device:TPU:0, one launch (start us, length us, event | category | flops | bytes accessed | tf_op | source)
XLA Modules:
  0.0 517.1 jit_solution(8531152215778680995)
XLA Ops:
  0.0 15.5 %channelize.3 = (bf16[2,2,16,32,128]{4,3,2,1,0:T(8,128)(2,1)}, bf16[2,2,16,32,128]{4,3,2,1,0:T(8,128)(2,1)}, bf16[2,2,16,32,128]{4,3,2,1,0:T(8,128)(2,1)}, bf16[...) custom-call(s32[1]{0:T(128)} %bitcast.place, ...), custom_call_target="tpu_custom_call" | custom-call | flops 1000 | bytes 1000 | tf_op jit(solution)/shard_map/channelize/pallas_call | solution.py:104
  15.5 4.1 collective-permute-start
  19.6 3.1 collective-permute-start.2
  23.3 25.9 %channelize.4 = (bf16[2,2,16,64,128]{4,3,2,1,0:T(8,128)(2,1)}, bf16[2,2,16,64,128]{4,3,2,1,0:T(8,128)(2,1)}, bf16[2,2,16,64,128]{4,3,2,1,0:T(8,128)(2,1)}, bf16[...) custom-call(s32[1]{0:T(128)} %bitcast.place, ...), custom_call_target="tpu_custom_call" | custom-call | flops 1000 | bytes 1000 | tf_op jit(solution)/shard_map/channelize/pallas_call | solution.py:104
  51.1 26.4 %collective-permute-done.rest_0_ = bf16[2,2,16,32,128]{4,3,2,1,0:T(8,128)(2,1)S(1)} collective-permute-done((bf16[2,2,16,32,128]{4,3,2,1,0:T(8,128)(2,1)}, bf16[2,2,16,32,128]{4,3,2,1,0:T(8,128)(2,1)S(1)}, u32[]{:S(2)}, u32[]{:S(2)}) %collective-permute-start) | collective-permute-done | bytes 524320 | tf_op jit(solution)/shard_map/ppermute | solution.py:299
  77.6 9.6 %collective-permute-done.1.rest_1_ = bf16[2,2,16,32,128]{4,3,2,1,0:T(8,128)(2,1)S(1)} collective-permute-done((bf16[2,2,16,32,128]{4,3,2,1,0:T(8,128)(2,1)}, bf16[2,2,16,32,128]{4,3,2,1,0:T(8,128)(2,1)S(1)}, u32[]{:S(2)}, u32[]{:S(2)}) %collective-permute-start.1) | collective-permute-done | bytes 524320 | tf_op jit(solution)/shard_map/ppermute | solution.py:299
  88.6 18.6 %multiply_convert_fusion.table = bf16[2048,2048]{1,0:T(8,128)(2,1)} fusion(s32[2048]{0:T(1024)S(1)} %get-tuple-element.183, s32[2048]{0:T(1024)S(1)} %get-tuple-element.184, s32[2048]{0:T(1024)S(1)} %get-tuple-element.185, s32[2048]{0:T(1024)S(1)} %get-tuple-element.180, s32[2048]{0:T(1024)S(1)} %get-tuple-element.186, s32[2048]{0:T(1024)S(1)} %get-tuple-element.179), kind=kLoop, calls=%fused_computation.2 | loop fusion | flops 117440512 | bytes 8437760 | tf_op jit(solution)/shard_map/convert_element_type | solution.py:53
  107.9 27.3 %collective-permute-start.22 = (bf16[2,2,16,64,128]{4,3,2,1,0:T(8,128)(2,1)}, bf16[2,2,16,64,128]{4,3,2,1,0:T(8,128)(2,1)}, u32[]{:S(2)}, u32[]{:S(2)}) collective-permute-start(bf16[2,2,16,64,128]{4,3,2,1,0:T(8,128)(2,1)} %get-tuple-element.127), channel_id=1, source_target_pairs={{0,5},{1,4},{2,7},{3,6},{4,1},{5,0},{6,3},{7,2},{8,13},{9,12},{10,... | collective-permute-start | bytes 3145736 | tf_op jit(solution)/shard_map/ppermute | solution.py:299
  135.3 18.0 %form_beams.3 = (f32[14,32,128]{2,1,0:T(8,128)}, f32[14,32,128]{2,1,0:T(8,128)}, f32[14,32,128]{2,1,0:T(8,128)}, f32[14,32,128]{2,1,0:T(8,128)}, f32[14,32,128]{...) custom-call(s32[1]{0:T(128)} %bitcast.place, ...), custom_call_target="tpu_custom_call" | custom-call | flops 1000 | bytes 1000 | tf_op jit(solution)/shard_map/form_beams/pallas_call | solution.py:157
  153.3 9.6 %all-gather = f32[128,128]{1,0:T(8,128)} all-gather(f32[32,128]{1,0:T(8,128)} %get-tuple-element.100), channel_id=2, replica_groups=mesh['section'=4,'shard'=8] {'section'}, dimensions={0}, use_global_device_ids=true | all-gather | bytes 81920 | tf_op jit(solution)/shard_map/all_gather | solution.py:331
  162.9 2.8 normalise.3
  169.5 1.9 copy.16
  173.5 23.7 %fusion.39 = (bf16[7,512,1024]{2,1,0:T(8,128)(2,1)}, bf16[7,512,1024]{2,1,0:T(8,128)(2,1)}) fusion(s32[512,1024]{1,0:T(8,128)S(1)} %copy.16, s32[7]{0:T(128)S(1)} %iota_add_fusion), kind=kLoop, calls=%fused_computation.42 | loop fusion | flops 157810688 | bytes 16777244 | tf_op jit(solution)/shard_map/convert_element_type | solution.py:271
  197.2 15.5 %channelize.5 = (bf16[2,2,16,32,128]{4,3,2,1,0:T(8,128)(2,1)}, bf16[2,2,16,32,128]{4,3,2,1,0:T(8,128)(2,1)}, bf16[2,2,16,32,128]{4,3,2,1,0:T(8,128)(2,1)}, bf16[...) custom-call(s32[1]{0:T(128)} %bitcast.place, ...), custom_call_target="tpu_custom_call" | custom-call | flops 1000 | bytes 1000 | tf_op jit(solution)/shard_map/channelize/pallas_call | solution.py:104
  213.8 3.3 collective-permute-start.17
  217.7 14.4 %collective-permute-done.17.rest_3_ = bf16[14,32,128]{2,1,0:T(8,128)(2,1)S(1)} collective-permute-done((bf16[14,32,128]{2,1,0:T(8,128)(2,1)S(1)}, bf16[14,32,128]{2,1,0:T(8,128)(2,1)S(1)}, u32[]{:S(2)}, u32[]{:S(2)}) %collective-permute-start.17) | collective-permute-done | bytes 114720 | tf_op jit(solution)/shard_map/ppermute | solution.py:299
  232.2 24.2 %collective-permute-start.18 = (bf16[14,32,128]{2,1,0:T(8,128)(2,1)S(1)}, bf16[14,32,128]{2,1,0:T(8,128)(2,1)S(1)}, u32[]{:S(2)}, u32[]{:S(2)}) collective-permute-start(bf16[14,32,128]{2,1,0:T(8,128)(2,1)S(1)} %copy-done.25), channel_id=1, source_target_pairs={{0,3},{1,2},{2,1},{3,0},{4,7},{5,6},{6,5},{7,4},{8,11},{9,10},{10,... | collective-permute-start | bytes 344072 | tf_op jit(solution)/shard_map/ppermute | solution.py:299
  256.3 13.4 %collective-permute-done.18.rest_4_ = bf16[14,32,128]{2,1,0:T(8,128)(2,1)S(1)} collective-permute-done((bf16[14,32,128]{2,1,0:T(8,128)(2,1)S(1)}, bf16[14,32,128]{2,1,0:T(8,128)(2,1)S(1)}, u32[]{:S(2)}, u32[]{:S(2)}) %collective-permute-start.18) | collective-permute-done | bytes 114720 | tf_op jit(solution)/shard_map/ppermute | solution.py:299
  269.7 5.2 collective-permute-done.19.rest_5_
  277.5 2.1 collective-permute-start.24
  279.5 2.3 collective-permute-start.26
  281.8 22.6 %collective-permute-done.23.rest_2_ = bf16[2,2,16,64,128]{4,3,2,1,0:T(8,128)(2,1)S(1)} collective-permute-done((bf16[2,2,16,64,128]{4,3,2,1,0:T(8,128)(2,1)}, bf16[2,2,16,64,128]{4,3,2,1,0:T(8,128)(2,1)S(1)}, u32[]{:S(2)}, u32[]{:S(2)}) %collective-permute-start.23) | collective-permute-done | bytes 1048608 | tf_op jit(solution)/shard_map/ppermute | solution.py:299
  305.7 19.6 %collective-permute-done.24.rest_3_ = bf16[2,2,16,64,128]{4,3,2,1,0:T(8,128)(2,1)S(1)} collective-permute-done((bf16[2,2,16,64,128]{4,3,2,1,0:T(8,128)(2,1)}, bf16[2,2,16,64,128]{4,3,2,1,0:T(8,128)(2,1)S(1)}, u32[]{:S(2)}, u32[]{:S(2)}) %collective-permute-start.24) | collective-permute-done | bytes 1048608 | tf_op jit(solution)/shard_map/ppermute | solution.py:299
  325.3 2.2 collective-permute-start.10
  327.5 21.0 %collective-permute-done.25.rest_4_ = bf16[2,2,16,64,128]{4,3,2,1,0:T(8,128)(2,1)} collective-permute-done((bf16[2,2,16,64,128]{4,3,2,1,0:T(8,128)(2,1)}, bf16[2,2,16,64,128]{4,3,2,1,0:T(8,128)(2,1)}, u32[]{:S(2)}, u32[]{:S(2)}) %collective-permute-start.25) | collective-permute-done | bytes 1048608 | tf_op jit(solution)/shard_map/ppermute | solution.py:299
  348.5 21.6 %collective-permute-start.11 = (bf16[2,2,16,32,128]{4,3,2,1,0:T(8,128)(2,1)}, bf16[2,2,16,32,128]{4,3,2,1,0:T(8,128)(2,1)}, u32[]{:S(2)}, u32[]{:S(2)}) collective-permute-start(bf16[2,2,16,32,128]{4,3,2,1,0:T(8,128)(2,1)} %get-tuple-element.114), channel_id=1, source_target_pairs={{0,3},{1,2},{2,1},{3,0},{4,7},{5,6},{6,5},{7,4},{8,11},{9,10},{10,... | collective-permute-start | bytes 1572872 | tf_op jit(solution)/shard_map/ppermute | solution.py:299
  372.7 30.8 %form_beams.4 = (f32[14,64,128]{2,1,0:T(8,128)}, f32[14,64,128]{2,1,0:T(8,128)}, f32[14,64,128]{2,1,0:T(8,128)}, f32[14,64,128]{2,1,0:T(8,128)}, f32[14,64,128]{...) custom-call(s32[1]{0:T(128)} %bitcast.place, ...), custom_call_target="tpu_custom_call" | custom-call | flops 1000 | bytes 1000 | tf_op jit(solution)/shard_map/form_beams/pallas_call | solution.py:157
  403.5 9.3 %all-gather.1 = f32[256,128]{1,0:T(8,128)} all-gather(f32[64,128]{1,0:T(8,128)} %get-tuple-element.135), channel_id=3, replica_groups=mesh['section'=4,'shard'=8] {'section'}, dimensions={0}, use_global_device_ids=true | all-gather | bytes 163840 | tf_op jit(solution)/shard_map/all_gather | solution.py:331
  412.9 3.6 normalise.4
  417.3 2.4 collective-permute-start.35
  420.5 3.1 copy-done
  423.5 3.1 copy-done.2
  427.3 3.0 dedisperse.3
  430.3 1.9 copy-done.4
  432.9 18.0 %form_beams.5 = (f32[14,32,128]{2,1,0:T(8,128)}, f32[14,32,128]{2,1,0:T(8,128)}, f32[14,32,128]{2,1,0:T(8,128)}, f32[14,32,128]{2,1,0:T(8,128)}, f32[14,32,128]{...) custom-call(s32[1]{0:T(128)} %bitcast.place, ...), custom_call_target="tpu_custom_call" | custom-call | flops 1000 | bytes 1000 | tf_op jit(solution)/shard_map/form_beams/pallas_call | solution.py:157
  450.8 8.7 %all-gather.2 = f32[128,128]{1,0:T(8,128)} all-gather(f32[32,128]{1,0:T(8,128)} %get-tuple-element.146), channel_id=4, replica_groups=mesh['section'=4,'shard'=8] {'section'}, dimensions={0}, use_global_device_ids=true | all-gather | bytes 81920 | tf_op jit(solution)/shard_map/all_gather | solution.py:331
  459.5 2.7 normalise.5
  465.6 12.9 %collective-permute-done.28.rest_0_ = bf16[14,32,128]{2,1,0:T(8,128)(2,1)S(1)} collective-permute-done((bf16[14,32,128]{2,1,0:T(8,128)(2,1)}, bf16[14,32,128]{2,1,0:T(8,128)(2,1)S(1)}, u32[]{:S(2)}, u32[]{:S(2)}) %collective-permute-start.28) | collective-permute-done | bytes 114720 | tf_op jit(solution)/shard_map/ppermute | solution.py:299
  478.7 3.7 collective-permute-start.40
  482.4 2.1 collective-permute-start.30
  484.6 3.9 collective-permute-done.38.rest_3_
  488.5 2.6 collective-permute-done.39.rest_4_
  491.1 4.7 collective-permute-start.32
  498.4 3.1 copy-done.1
  501.5 3.1 copy-done.3
  504.6 2.0 copy-done.5
  507.3 4.9 dedisperse.4
  512.3 4.8 dedisperse.5
  (135 shorter events, 28.7 us)
Async XLA Ops:
  15.5 62.0 %collective-permute-start = (bf16[2,2,16,32,128]{4,3,2,1,0:T(8,128)(2,1)}, bf16[2,2,16,32,128]{4,3,2,1,0:T(8,128)(2,1)S(1)}, u32[]{:S(2)}, u32[]{:S(2)}) collective-permute-start(bf16[2,2,16,32,128]{4,3,2,1,0:T(8,128)(2,1)} %get-tuple-element.92), channel_id=1, source_target_pairs={{0,4},{1,5},{2,6},{3,7},{4,0},{5,1},{6,2},{7,3},{8,12},{9,13},{10,... | collective-permute-start | bytes 1572872 | tf_op jit(solution)/shard_map/ppermute | solution.py:299
  19.6 67.6 %collective-permute-start.1 = (bf16[2,2,16,32,128]{4,3,2,1,0:T(8,128)(2,1)}, bf16[2,2,16,32,128]{4,3,2,1,0:T(8,128)(2,1)S(1)}, u32[]{:S(2)}, u32[]{:S(2)}) collective-permute-start(bf16[2,2,16,32,128]{4,3,2,1,0:T(8,128)(2,1)} %get-tuple-element.93), channel_id=1, source_target_pairs={{0,5},{1,4},{2,7},{3,6},{4,1},{5,0},{6,3},{7,2},{8,13},{9,12},{10,... | collective-permute-start | bytes 1572872 | tf_op jit(solution)/shard_map/ppermute | solution.py:299
  19.6 88.4 %collective-permute-start.2 = (bf16[2,2,16,32,128]{4,3,2,1,0:T(8,128)(2,1)}, bf16[2,2,16,32,128]{4,3,2,1,0:T(8,128)(2,1)}, u32[]{:S(2)}, u32[]{:S(2)}) collective-permute-start(bf16[2,2,16,32,128]{4,3,2,1,0:T(8,128)(2,1)} %get-tuple-element.94), channel_id=1, source_target_pairs={{0,6},{1,7},{2,4},{3,5},{4,2},{5,3},{6,0},{7,1},{8,14},{9,15},{10,... | collective-permute-start | bytes 1572872 | tf_op jit(solution)/shard_map/ppermute | solution.py:299
  22.7 85.3 %collective-permute-start.3 = (bf16[2,2,16,32,128]{4,3,2,1,0:T(8,128)(2,1)}, bf16[2,2,16,32,128]{4,3,2,1,0:T(8,128)(2,1)}, u32[]{:S(2)}, u32[]{:S(2)}) collective-permute-start(bf16[2,2,16,32,128]{4,3,2,1,0:T(8,128)(2,1)} %get-tuple-element.95), channel_id=1, source_target_pairs={{0,7},{1,6},{2,5},{3,4},{4,3},{5,2},{6,1},{7,0},{8,15},{9,14},{10,... | collective-permute-start | bytes 1572872 | tf_op jit(solution)/shard_map/ppermute | solution.py:299
  23.3 112.0 %collective-permute-start.4 = (bf16[2,2,16,32,128]{4,3,2,1,0:T(8,128)(2,1)}, bf16[2,2,16,32,128]{4,3,2,1,0:T(8,128)(2,1)}, u32[]{:S(2)}, u32[]{:S(2)}) collective-permute-start(bf16[2,2,16,32,128]{4,3,2,1,0:T(8,128)(2,1)} %get-tuple-element.96), channel_id=1, source_target_pairs={{0,3},{1,2},{2,1},{3,0},{4,7},{5,6},{6,5},{7,4},{8,11},{9,10},{10,... | collective-permute-start | bytes 1572872 | tf_op jit(solution)/shard_map/ppermute | solution.py:299
  23.3 83.9 %copy-start.21 = (f32[128]{0:T(128)S(1)}, f32[128]{0:T(128)}, u32[]{:S(2)}) copy-start(f32[128]{0:T(128)} %param.11) | copy-start | bytes 1540
  49.1 117.8 %copy-start.12 = (s32[1024,512]{1,0:T(8,128)S(1)}, s32[1024,512]{1,0:T(8,128)}, u32[]{:S(2)}) copy-start(s32[1024,512]{1,0:T(8,128)} %param.12) | copy-start | bytes 6291460
  77.5 57.8 %collective-permute-start.5 = (bf16[2,2,16,32,128]{4,3,2,1,0:T(8,128)(2,1)}, bf16[2,2,16,32,128]{4,3,2,1,0:T(8,128)(2,1)}, u32[]{:S(2)}, u32[]{:S(2)}) collective-permute-start(bf16[2,2,16,32,128]{4,3,2,1,0:T(8,128)(2,1)} %get-tuple-element.97), channel_id=1, source_target_pairs={{0,2},{1,3},{2,0},{3,1},{4,6},{5,7},{6,4},{7,5},{8,10},{9,11},{10,... | collective-permute-start | bytes 1572872 | tf_op jit(solution)/shard_map/ppermute | solution.py:299
  87.1 48.1 %collective-permute-start.6 = (bf16[2,2,16,32,128]{4,3,2,1,0:T(8,128)(2,1)}, bf16[2,2,16,32,128]{4,3,2,1,0:T(8,128)(2,1)}, u32[]{:S(2)}, u32[]{:S(2)}) collective-permute-start(bf16[2,2,16,32,128]{4,3,2,1,0:T(8,128)(2,1)} %get-tuple-element.98), channel_id=1, source_target_pairs={{0,1},{1,0},{2,3},{3,2},{4,5},{5,4},{6,7},{7,6},{8,9},{9,8},{10,11... | collective-permute-start | bytes 1572872 | tf_op jit(solution)/shard_map/ppermute | solution.py:299
  107.9 171.6 %collective-permute-start.21 = (bf16[2,2,16,64,128]{4,3,2,1,0:T(8,128)(2,1)}, bf16[2,2,16,64,128]{4,3,2,1,0:T(8,128)(2,1)}, u32[]{:S(2)}, u32[]{:S(2)}) collective-permute-start(bf16[2,2,16,64,128]{4,3,2,1,0:T(8,128)(2,1)} %get-tuple-element.126), channel_id=1, source_target_pairs={{0,4},{1,5},{2,6},{3,7},{4,0},{5,1},{6,2},{7,3},{8,12},{9,13},{10,... | collective-permute-start | bytes 3145736 | tf_op jit(solution)/shard_map/ppermute | solution.py:299
  107.9 173.9 %collective-permute-start.22 = (bf16[2,2,16,64,128]{4,3,2,1,0:T(8,128)(2,1)}, bf16[2,2,16,64,128]{4,3,2,1,0:T(8,128)(2,1)}, u32[]{:S(2)}, u32[]{:S(2)}) collective-permute-start(bf16[2,2,16,64,128]{4,3,2,1,0:T(8,128)(2,1)} %get-tuple-element.127), channel_id=1, source_target_pairs={{0,5},{1,4},{2,7},{3,6},{4,1},{5,0},{6,3},{7,2},{8,13},{9,12},{10,... | collective-permute-start | bytes 3145736 | tf_op jit(solution)/shard_map/ppermute | solution.py:299
  171.4 41.3 %collective-permute-start.14 = (bf16[14,32,128]{2,1,0:T(8,128)(2,1)S(1)}, bf16[14,32,128]{2,1,0:T(8,128)(2,1)S(1)}, u32[]{:S(2)}, u32[]{:S(2)}) collective-permute-start(bf16[14,32,128]{2,1,0:T(8,128)(2,1)S(1)} %copy-done.29), channel_id=1, source_target_pairs={{0,4},{1,5},{2,6},{3,7},{4,0},{5,1},{6,2},{7,3},{8,12},{9,13},{10,... | collective-permute-start | bytes 344072 | tf_op jit(solution)/shard_map/ppermute | solution.py:299
  171.7 42.0 %collective-permute-start.15 = (bf16[14,32,128]{2,1,0:T(8,128)(2,1)S(1)}, bf16[14,32,128]{2,1,0:T(8,128)(2,1)S(1)}, u32[]{:S(2)}, u32[]{:S(2)}) collective-permute-start(bf16[14,32,128]{2,1,0:T(8,128)(2,1)S(1)} %copy-done.28), channel_id=1, source_target_pairs={{0,5},{1,4},{2,7},{3,6},{4,1},{5,0},{6,3},{7,2},{8,13},{9,12},{10,... | collective-permute-start | bytes 344072 | tf_op jit(solution)/shard_map/ppermute | solution.py:299
  172.9 44.1 %collective-permute-start.16 = (bf16[14,32,128]{2,1,0:T(8,128)(2,1)S(1)}, bf16[14,32,128]{2,1,0:T(8,128)(2,1)S(1)}, u32[]{:S(2)}, u32[]{:S(2)}) collective-permute-start(bf16[14,32,128]{2,1,0:T(8,128)(2,1)S(1)} %copy-done.27), channel_id=1, source_target_pairs={{0,6},{1,7},{2,4},{3,5},{4,2},{5,3},{6,0},{7,1},{8,14},{9,15},{10,... | collective-permute-start | bytes 344072 | tf_op jit(solution)/shard_map/ppermute | solution.py:299
  197.2 72.5 %copy-start.24 = (bf16[14,32,128]{2,1,0:T(8,128)(2,1)S(1)}, bf16[14,32,128]{2,1,0:T(8,128)(2,1)}, u32[]{:S(2)}) copy-start(bf16[14,32,128]{2,1,0:T(8,128)(2,1)} %get-tuple-element.123) | copy-start | bytes 344068
  197.2 77.7 %copy-start.23 = (bf16[14,32,128]{2,1,0:T(8,128)(2,1)S(1)}, bf16[14,32,128]{2,1,0:T(8,128)(2,1)}, u32[]{:S(2)}) copy-start(bf16[14,32,128]{2,1,0:T(8,128)(2,1)} %get-tuple-element.124) | copy-start | bytes 344068
  212.7 207.7 %copy-start.7 = (bf16[14,32,128]{2,1,0:T(8,128)(2,1)S(1)}, bf16[14,32,128]{2,1,0:T(8,128)(2,1)}, u32[]{:S(2)}) copy-start(bf16[14,32,128]{2,1,0:T(8,128)(2,1)} %get-tuple-element.125.rest_7_) | copy-start | bytes 344068
  212.7 64.7 %collective-permute-start.7 = (bf16[2,2,16,32,128]{4,3,2,1,0:T(8,128)(2,1)}, bf16[2,2,16,32,128]{4,3,2,1,0:T(8,128)(2,1)S(1)}, u32[]{:S(2)}, u32[]{:S(2)}) collective-permute-start(bf16[2,2,16,32,128]{4,3,2,1,0:T(8,128)(2,1)} %get-tuple-element.110), channel_id=1, source_target_pairs={{0,4},{1,5},{2,6},{3,7},{4,0},{5,1},{6,2},{7,3},{8,12},{9,13},{10,... | collective-permute-start | bytes 1572872 | tf_op jit(solution)/shard_map/ppermute | solution.py:299
  213.8 18.4 %collective-permute-start.17 = (bf16[14,32,128]{2,1,0:T(8,128)(2,1)S(1)}, bf16[14,32,128]{2,1,0:T(8,128)(2,1)S(1)}, u32[]{:S(2)}, u32[]{:S(2)}) collective-permute-start(bf16[14,32,128]{2,1,0:T(8,128)(2,1)S(1)} %copy-done.26), channel_id=1, source_target_pairs={{0,7},{1,6},{2,5},{3,4},{4,3},{5,2},{6,1},{7,0},{8,15},{9,14},{10,... | collective-permute-start | bytes 344072 | tf_op jit(solution)/shard_map/ppermute | solution.py:299
  217.0 62.5 %collective-permute-start.8 = (bf16[2,2,16,32,128]{4,3,2,1,0:T(8,128)(2,1)}, bf16[2,2,16,32,128]{4,3,2,1,0:T(8,128)(2,1)S(1)}, u32[]{:S(2)}, u32[]{:S(2)}) collective-permute-start(bf16[2,2,16,32,128]{4,3,2,1,0:T(8,128)(2,1)} %get-tuple-element.111), channel_id=1, source_target_pairs={{0,5},{1,4},{2,7},{3,6},{4,1},{5,0},{6,3},{7,2},{8,13},{9,12},{10,... | collective-permute-start | bytes 1572872 | tf_op jit(solution)/shard_map/ppermute | solution.py:299
  232.2 37.6 %collective-permute-start.18 = (bf16[14,32,128]{2,1,0:T(8,128)(2,1)S(1)}, bf16[14,32,128]{2,1,0:T(8,128)(2,1)S(1)}, u32[]{:S(2)}, u32[]{:S(2)}) collective-permute-start(bf16[14,32,128]{2,1,0:T(8,128)(2,1)S(1)} %copy-done.25), channel_id=1, source_target_pairs={{0,3},{1,2},{2,1},{3,0},{4,7},{5,6},{6,5},{7,4},{8,11},{9,10},{10,... | collective-permute-start | bytes 344072 | tf_op jit(solution)/shard_map/ppermute | solution.py:299
  269.7 5.2 collective-permute-start.19
  274.9 1.3 collective-permute-start.20
  276.2 28.2 %collective-permute-start.23 = (bf16[2,2,16,64,128]{4,3,2,1,0:T(8,128)(2,1)}, bf16[2,2,16,64,128]{4,3,2,1,0:T(8,128)(2,1)S(1)}, u32[]{:S(2)}, u32[]{:S(2)}) collective-permute-start(bf16[2,2,16,64,128]{4,3,2,1,0:T(8,128)(2,1)} %get-tuple-element.128), channel_id=1, source_target_pairs={{0,6},{1,7},{2,4},{3,5},{4,2},{5,3},{6,0},{7,1},{8,14},{9,15},{10,... | collective-permute-start | bytes 3145736 | tf_op jit(solution)/shard_map/ppermute | solution.py:299
  277.5 47.9 %collective-permute-start.24 = (bf16[2,2,16,64,128]{4,3,2,1,0:T(8,128)(2,1)}, bf16[2,2,16,64,128]{4,3,2,1,0:T(8,128)(2,1)S(1)}, u32[]{:S(2)}, u32[]{:S(2)}) collective-permute-start(bf16[2,2,16,64,128]{4,3,2,1,0:T(8,128)(2,1)} %get-tuple-element.129), channel_id=1, source_target_pairs={{0,7},{1,6},{2,5},{3,4},{4,3},{5,2},{6,1},{7,0},{8,15},{9,14},{10,... | collective-permute-start | bytes 3145736 | tf_op jit(solution)/shard_map/ppermute | solution.py:299
  279.5 69.0 %collective-permute-start.25 = (bf16[2,2,16,64,128]{4,3,2,1,0:T(8,128)(2,1)}, bf16[2,2,16,64,128]{4,3,2,1,0:T(8,128)(2,1)}, u32[]{:S(2)}, u32[]{:S(2)}) collective-permute-start(bf16[2,2,16,64,128]{4,3,2,1,0:T(8,128)(2,1)} %get-tuple-element.130), channel_id=1, source_target_pairs={{0,3},{1,2},{2,1},{3,0},{4,7},{5,6},{6,5},{7,4},{8,11},{9,10},{10,... | collective-permute-start | bytes 3145736 | tf_op jit(solution)/shard_map/ppermute | solution.py:299
  279.5 92.4 %collective-permute-start.26 = (bf16[2,2,16,64,128]{4,3,2,1,0:T(8,128)(2,1)}, bf16[2,2,16,64,128]{4,3,2,1,0:T(8,128)(2,1)}, u32[]{:S(2)}, u32[]{:S(2)}) collective-permute-start(bf16[2,2,16,64,128]{4,3,2,1,0:T(8,128)(2,1)} %get-tuple-element.131), channel_id=1, source_target_pairs={{0,2},{1,3},{2,0},{3,1},{4,6},{5,7},{6,4},{7,5},{8,10},{9,11},{10,... | collective-permute-start | bytes 3145736 | tf_op jit(solution)/shard_map/ppermute | solution.py:299
  281.8 90.1 %collective-permute-start.27 = (bf16[2,2,16,64,128]{4,3,2,1,0:T(8,128)(2,1)}, bf16[2,2,16,64,128]{4,3,2,1,0:T(8,128)(2,1)}, u32[]{:S(2)}, u32[]{:S(2)}) collective-permute-start(bf16[2,2,16,64,128]{4,3,2,1,0:T(8,128)(2,1)} %get-tuple-element.132), channel_id=1, source_target_pairs={{0,1},{1,0},{2,3},{3,2},{4,5},{5,4},{6,7},{7,6},{8,9},{9,8},{10,11... | collective-permute-start | bytes 3145736 | tf_op jit(solution)/shard_map/ppermute | solution.py:299
  304.4 112.1 %collective-permute-start.9 = (bf16[2,2,16,32,128]{4,3,2,1,0:T(8,128)(2,1)}, bf16[2,2,16,32,128]{4,3,2,1,0:T(8,128)(2,1)S(1)}, u32[]{:S(2)}, u32[]{:S(2)}) collective-permute-start(bf16[2,2,16,32,128]{4,3,2,1,0:T(8,128)(2,1)} %get-tuple-element.112), channel_id=1, source_target_pairs={{0,6},{1,7},{2,4},{3,5},{4,2},{5,3},{6,0},{7,1},{8,14},{9,15},{10,... | collective-permute-start | bytes 1572872 | tf_op jit(solution)/shard_map/ppermute | solution.py:299
  325.3 94.4 %collective-permute-start.10 = (bf16[2,2,16,32,128]{4,3,2,1,0:T(8,128)(2,1)}, bf16[2,2,16,32,128]{4,3,2,1,0:T(8,128)(2,1)}, u32[]{:S(2)}, u32[]{:S(2)}) collective-permute-start(bf16[2,2,16,32,128]{4,3,2,1,0:T(8,128)(2,1)} %get-tuple-element.113), channel_id=1, source_target_pairs={{0,7},{1,6},{2,5},{3,4},{4,3},{5,2},{6,1},{7,0},{8,15},{9,14},{10,... | collective-permute-start | bytes 1572872 | tf_op jit(solution)/shard_map/ppermute | solution.py:299
  348.5 84.3 %collective-permute-start.11 = (bf16[2,2,16,32,128]{4,3,2,1,0:T(8,128)(2,1)}, bf16[2,2,16,32,128]{4,3,2,1,0:T(8,128)(2,1)}, u32[]{:S(2)}, u32[]{:S(2)}) collective-permute-start(bf16[2,2,16,32,128]{4,3,2,1,0:T(8,128)(2,1)} %get-tuple-element.114), channel_id=1, source_target_pairs={{0,3},{1,2},{2,1},{3,0},{4,7},{5,6},{6,5},{7,4},{8,11},{9,10},{10,... | collective-permute-start | bytes 1572872 | tf_op jit(solution)/shard_map/ppermute | solution.py:299
  371.9 60.9 %collective-permute-start.12 = (bf16[2,2,16,32,128]{4,3,2,1,0:T(8,128)(2,1)}, bf16[2,2,16,32,128]{4,3,2,1,0:T(8,128)(2,1)}, u32[]{:S(2)}, u32[]{:S(2)}) collective-permute-start(bf16[2,2,16,32,128]{4,3,2,1,0:T(8,128)(2,1)} %get-tuple-element.115), channel_id=1, source_target_pairs={{0,2},{1,3},{2,0},{3,1},{4,6},{5,7},{6,4},{7,5},{8,10},{9,11},{10,... | collective-permute-start | bytes 1572872 | tf_op jit(solution)/shard_map/ppermute | solution.py:299
  371.9 60.9 %collective-permute-start.13 = (bf16[2,2,16,32,128]{4,3,2,1,0:T(8,128)(2,1)}, bf16[2,2,16,32,128]{4,3,2,1,0:T(8,128)(2,1)}, u32[]{:S(2)}, u32[]{:S(2)}) collective-permute-start(bf16[2,2,16,32,128]{4,3,2,1,0:T(8,128)(2,1)} %get-tuple-element.116), channel_id=1, source_target_pairs={{0,1},{1,0},{2,3},{3,2},{4,5},{5,4},{6,7},{7,6},{8,9},{9,8},{10,11... | collective-permute-start | bytes 1572872 | tf_op jit(solution)/shard_map/ppermute | solution.py:299
  417.3 61.4 %collective-permute-start.35 = (bf16[14,64,128]{2,1,0:T(8,128)(2,1)}, bf16[14,64,128]{2,1,0:T(8,128)(2,1)S(1)}, u32[]{:S(2)}, u32[]{:S(2)}) collective-permute-start(bf16[14,64,128]{2,1,0:T(8,128)(2,1)} %get-tuple-element.163), channel_id=1, source_target_pairs={{0,4},{1,5},{2,6},{3,7},{4,0},{5,1},{6,2},{7,3},{8,12},{9,13},{10,... | collective-permute-start | bytes 688136 | tf_op jit(solution)/shard_map/ppermute | solution.py:299
  419.8 62.7 %collective-permute-start.36 = (bf16[14,64,128]{2,1,0:T(8,128)(2,1)}, bf16[14,64,128]{2,1,0:T(8,128)(2,1)S(1)}, u32[]{:S(2)}, u32[]{:S(2)}) collective-permute-start(bf16[14,64,128]{2,1,0:T(8,128)(2,1)} %get-tuple-element.164), channel_id=1, source_target_pairs={{0,5},{1,4},{2,7},{3,6},{4,1},{5,0},{6,3},{7,2},{8,13},{9,12},{10,... | collective-permute-start | bytes 688136 | tf_op jit(solution)/shard_map/ppermute | solution.py:299
  432.8 79.4 %slice-start = ((s8[7340032]{0:T(1024)(128)(4,1)}), s8[3145728]{0:T(1024)(128)(4,1)S(1)}, s32[]{:S(2)}) async-start(s8[7340032]{0:T(1024)(128)(4,1)} %bitcast.20), calls=%async_computation | async-start | bytes 6291456
  462.2 16.3 %collective-permute-start.28 = (bf16[14,32,128]{2,1,0:T(8,128)(2,1)}, bf16[14,32,128]{2,1,0:T(8,128)(2,1)S(1)}, u32[]{:S(2)}, u32[]{:S(2)}) collective-permute-start(bf16[14,32,128]{2,1,0:T(8,128)(2,1)} %get-tuple-element.155), channel_id=1, source_target_pairs={{0,4},{1,5},{2,6},{3,7},{4,0},{5,1},{6,2},{7,3},{8,12},{9,13},{10,... | collective-permute-start | bytes 344072 | tf_op jit(solution)/shard_map/ppermute | solution.py:299
  463.8 14.9 %collective-permute-start.29 = (bf16[14,32,128]{2,1,0:T(8,128)(2,1)}, bf16[14,32,128]{2,1,0:T(8,128)(2,1)S(1)}, u32[]{:S(2)}, u32[]{:S(2)}) collective-permute-start(bf16[14,32,128]{2,1,0:T(8,128)(2,1)} %get-tuple-element.156), channel_id=1, source_target_pairs={{0,5},{1,4},{2,7},{3,6},{4,1},{5,0},{6,3},{7,2},{8,13},{9,12},{10,... | collective-permute-start | bytes 344072 | tf_op jit(solution)/shard_map/ppermute | solution.py:299
  463.8 18.6 %collective-permute-start.37 = (bf16[14,64,128]{2,1,0:T(8,128)(2,1)}, bf16[14,64,128]{2,1,0:T(8,128)(2,1)S(1)}, u32[]{:S(2)}, u32[]{:S(2)}) collective-permute-start(bf16[14,64,128]{2,1,0:T(8,128)(2,1)} %get-tuple-element.165), channel_id=1, source_target_pairs={{0,6},{1,7},{2,4},{3,5},{4,2},{5,3},{6,0},{7,1},{8,14},{9,15},{10,... | collective-permute-start | bytes 688136 | tf_op jit(solution)/shard_map/ppermute | solution.py:299
  478.5 9.9 %collective-permute-start.38 = (bf16[14,64,128]{2,1,0:T(8,128)(2,1)}, bf16[14,64,128]{2,1,0:T(8,128)(2,1)S(1)}, u32[]{:S(2)}, u32[]{:S(2)}) collective-permute-start(bf16[14,64,128]{2,1,0:T(8,128)(2,1)} %get-tuple-element.166), channel_id=1, source_target_pairs={{0,7},{1,6},{2,5},{3,4},{4,3},{5,2},{6,1},{7,0},{8,15},{9,14},{10,... | collective-permute-start | bytes 688136 | tf_op jit(solution)/shard_map/ppermute | solution.py:299
  478.7 12.4 %collective-permute-start.39 = (bf16[14,64,128]{2,1,0:T(8,128)(2,1)}, bf16[14,64,128]{2,1,0:T(8,128)(2,1)S(1)}, u32[]{:S(2)}, u32[]{:S(2)}) collective-permute-start(bf16[14,64,128]{2,1,0:T(8,128)(2,1)} %get-tuple-element.167), channel_id=1, source_target_pairs={{0,3},{1,2},{2,1},{3,0},{4,7},{5,6},{6,5},{7,4},{8,11},{9,10},{10,... | collective-permute-start | bytes 688136 | tf_op jit(solution)/shard_map/ppermute | solution.py:299
  478.7 18.6 %collective-permute-start.40 = (bf16[14,64,128]{2,1,0:T(8,128)(2,1)}, bf16[14,64,128]{2,1,0:T(8,128)(2,1)S(1)}, u32[]{:S(2)}, u32[]{:S(2)}) collective-permute-start(bf16[14,64,128]{2,1,0:T(8,128)(2,1)} %get-tuple-element.168), channel_id=1, source_target_pairs={{0,2},{1,3},{2,0},{3,1},{4,6},{5,7},{6,4},{7,5},{8,10},{9,11},{10,... | collective-permute-start | bytes 688136 | tf_op jit(solution)/shard_map/ppermute | solution.py:299
  482.4 15.0 %collective-permute-start.41 = (bf16[14,64,128]{2,1,0:T(8,128)(2,1)S(1)}, bf16[14,64,128]{2,1,0:T(8,128)(2,1)S(1)}, u32[]{:S(2)}, u32[]{:S(2)}) collective-permute-start(bf16[14,64,128]{2,1,0:T(8,128)(2,1)S(1)} %copy-done.22), channel_id=1, source_target_pairs={{0,1},{1,0},{2,3},{3,2},{4,5},{5,4},{6,7},{7,6},{8,9},{9,8},{10,11... | collective-permute-start | bytes 688136 | tf_op jit(solution)/shard_map/ppermute | solution.py:299
  482.4 29.8 %collective-permute-start.30 = (bf16[14,32,128]{2,1,0:T(8,128)(2,1)}, bf16[14,32,128]{2,1,0:T(8,128)(2,1)S(1)}, u32[]{:S(2)}, u32[]{:S(2)}) collective-permute-start(bf16[14,32,128]{2,1,0:T(8,128)(2,1)} %get-tuple-element.157), channel_id=1, source_target_pairs={{0,6},{1,7},{2,4},{3,5},{4,2},{5,3},{6,0},{7,1},{8,14},{9,15},{10,... | collective-permute-start | bytes 344072 | tf_op jit(solution)/shard_map/ppermute | solution.py:299
  488.4 23.8 %collective-permute-start.31 = (bf16[14,32,128]{2,1,0:T(8,128)(2,1)}, bf16[14,32,128]{2,1,0:T(8,128)(2,1)S(1)}, u32[]{:S(2)}, u32[]{:S(2)}) collective-permute-start(bf16[14,32,128]{2,1,0:T(8,128)(2,1)} %get-tuple-element.158), channel_id=1, source_target_pairs={{0,7},{1,6},{2,5},{3,4},{4,3},{5,2},{6,1},{7,0},{8,15},{9,14},{10,... | collective-permute-start | bytes 344072 | tf_op jit(solution)/shard_map/ppermute | solution.py:299
  491.1 21.2 %collective-permute-start.32 = (bf16[14,32,128]{2,1,0:T(8,128)(2,1)}, bf16[14,32,128]{2,1,0:T(8,128)(2,1)S(1)}, u32[]{:S(2)}, u32[]{:S(2)}) collective-permute-start(bf16[14,32,128]{2,1,0:T(8,128)(2,1)} %get-tuple-element.159), channel_id=1, source_target_pairs={{0,3},{1,2},{2,1},{3,0},{4,7},{5,6},{6,5},{7,4},{8,11},{9,10},{10,... | collective-permute-start | bytes 344072 | tf_op jit(solution)/shard_map/ppermute | solution.py:299
  497.3 14.9 %collective-permute-start.33 = (bf16[14,32,128]{2,1,0:T(8,128)(2,1)}, bf16[14,32,128]{2,1,0:T(8,128)(2,1)S(1)}, u32[]{:S(2)}, u32[]{:S(2)}) collective-permute-start(bf16[14,32,128]{2,1,0:T(8,128)(2,1)} %get-tuple-element.160), channel_id=1, source_target_pairs={{0,2},{1,3},{2,0},{3,1},{4,6},{5,7},{6,4},{7,5},{8,10},{9,11},{10,... | collective-permute-start | bytes 344072 | tf_op jit(solution)/shard_map/ppermute | solution.py:299
  497.4 14.8 %collective-permute-start.34 = (bf16[14,32,128]{2,1,0:T(8,128)(2,1)}, bf16[14,32,128]{2,1,0:T(8,128)(2,1)S(1)}, u32[]{:S(2)}, u32[]{:S(2)}) collective-permute-start(bf16[14,32,128]{2,1,0:T(8,128)(2,1)} %get-tuple-element.161), channel_id=1, source_target_pairs={{0,1},{1,0},{2,3},{3,2},{4,5},{5,4},{6,7},{7,6},{8,9},{9,8},{10,11... | collective-permute-start | bytes 344072 | tf_op jit(solution)/shard_map/ppermute | solution.py:299
  (26 other events, 575.9 us)

commit v3 on v2

--- a/solution.py
+++ b/solution.py
@@ -178,7 +178,7 @@
     return outs[:-1], outs[-1]
 
 
-def normalise_kernel(count, chips, scale, section, levels, decay, *rest):
+def normalise_kernel(count, shards, scale, section, levels, decay, *rest):
     rate = decay[...]
     dividend, divisor = jnp.zeros_like(rate), jnp.zeros_like(rate)
     for block in range(count):
@@ -187,9 +187,9 @@
         dividend = jnp.where(later, rate * dividend + mean, dividend)
         divisor = jnp.where(later, rate * divisor + 1.0, divisor)
     inverse = divisor / dividend
-    outs = rest[-1 - chips : -1]
-    for q in range(chips):
-        outs[q][...] = (rest[q][...] * inverse).astype(jnp.bfloat16)
+    outs = rest[-1 - shards : -1]
+    for m in range(shards):
+        outs[m][...] = (rest[m][...] * inverse).astype(jnp.bfloat16)
     rest[-1][...] = jnp.zeros((8, LANES), jnp.int32)
 
 
@@ -209,60 +209,47 @@
     return outs[:-1], outs[-1]
 
 
-def dedisperse_kernel(shards, size, last, first, scale, place, cosine, sine, *rest):
-    total = None if first else rest[shards]
-    if last:
-        out, token, upper, lower, woven = rest[-5:]
-    else:
-        out, token, upper, lower = rest[-4:]
-    token[...] = jnp.zeros((8, LANES), jnp.int32)
+def dedisperse_kernel(shards, columns, sizes, scale, place, cosine, sine, *rest):
+    out, upper, lower, woven = rest[-4:]
     f = pl.program_id(0)
-    for part, m in zip(rest, slots(shards)):
-        at = pl.ds(pl.multiple_of((place[0] ^ m) * size, size), size)
-        real, imag = part[f], part[f + MODF]
-        upper[at, :LANES] = real
-        upper[at, LANES:] = imag
-        lower[at, :LANES] = imag
-        lower[at, LANES:] = -real
+    for c, (column, size) in enumerate(zip(columns, sizes)):
+        for part, m in zip(rest[c * shards : (c + 1) * shards], slots(shards)):
+            at = pl.ds(pl.multiple_of(column + (place[0] ^ m) * size, ROWS), size)
+            real, imag = part[f], part[f + MODF]
+            upper[at, :LANES] = real
+            upper[at, LANES:] = imag
+            lower[at, :LANES] = imag
+            lower[at, LANES:] = -real
     value = jnp.dot(cosine[0], upper[...], preferred_element_type=jnp.float32) + jnp.dot(
         sine[0], lower[...], preferred_element_type=jnp.float32
     )
-    if total is not None:
-        value = value + total[0]
-    if last:
-        rows = value.shape[0]
-        woven[pl.ds(0, rows, stride=2), :] = value[:, :LANES] * scale
-        woven[pl.ds(1, rows, stride=2), :] = value[:, LANES:] * scale
-        out[0] = woven[...].astype(out.dtype)
-    else:
-        out[0] = value
-
-
-def dedisperse(place, cosine, sine, at, parts, total, last, scale, after):
-    shards, size = len(parts), parts[0].shape[1]
-    rows, depth = cosine.shape[1], shards * size
+    rows = value.shape[0]
+    woven[pl.ds(0, rows, stride=2), :] = value[:, :LANES] * scale
+    woven[pl.ds(1, rows, stride=2), :] = value[:, LANES:] * scale
+    out[0] = woven[...].astype(out.dtype)
+
+
+def dedisperse(place, cosine, sine, columns, chunks, scale):
+    shards = len(chunks[0])
+    sizes = [parts[0].shape[1] for parts in chunks]
+    rows, depth = cosine.shape[1:]
     each = lambda f, _: (f, 0, 0)
-    block = (2 * MODF, size, LANES)
-    sums = [] if total is None else [total]
-    made = (2 * rows, LANES) if last else (rows, 2 * LANES)
+    made = (2 * rows, LANES)
     return pl.pallas_call(
-        functools.partial(dedisperse_kernel, shards, size, last, total is None, scale),
+        functools.partial(dedisperse_kernel, shards, columns, sizes, scale),
         grid_spec=pltpu.PrefetchScalarGridSpec(
             num_scalar_prefetch=1,
             grid=(MODF,),
-            in_specs=[pl.BlockSpec((1, rows, depth), lambda f, _: (f, 0, at // depth))] * 2
-            + [pl.BlockSpec(block, lambda f, _: (0, 0, 0))] * shards
-            + [pl.BlockSpec((1, rows, 2 * LANES), each)] * len(sums)
-            + [pl.BlockSpec(memory_space=pl.ANY)] * len(after),
-            out_specs=[pl.BlockSpec((1,) + made, each), pl.BlockSpec((8, LANES), lambda f, _: (0, 0))],
-            scratch_shapes=[pltpu.VMEM((depth, 2 * LANES), jnp.bfloat16)] * 2
-            + ([pltpu.VMEM(made, jnp.float32)] if last else []),
+            in_specs=[pl.BlockSpec((1, rows, depth), each)] * 2
+            + [pl.BlockSpec((2 * MODF, size, LANES), lambda f, _: (0, 0, 0)) for size in sizes for _ in range(shards)],
+            out_specs=pl.BlockSpec((1,) + made, each),
+            scratch_shapes=[pltpu.VMEM((depth, 2 * LANES), jnp.bfloat16)] * 2 + [pltpu.VMEM(made, jnp.float32)],
         ),
-        out_shape=[jax.ShapeDtypeStruct((MODF,) + made, jnp.bfloat16 if last else jnp.float32), TOKEN],
-        compiler_params=pltpu.CompilerParams(vmem_limit_bytes=24 << 20),
+        out_shape=jax.ShapeDtypeStruct((MODF,) + made, jnp.bfloat16),
+        compiler_params=pltpu.CompilerParams(vmem_limit_bytes=60 << 20),
         cost_estimate=COST,
         name="dedisperse",
-    )(place, cosine, sine, *parts, *sums, *after)
+    )(place, cosine, sine, *[part for parts in chunks for part in parts])
 
 
 def phase_tables(delay, frames):
@@ -294,52 +281,60 @@
     rows = spectral_constant(chans).reshape(2, shards, local, NSAMP)
     scale = np.float32(1.0 / (frames * feeds))
 
-    def exchange(parts):
+    far, near = slots(shards)[: shards // 2], slots(shards)[shards // 2 :]
+
+    def exchange(parts, partners):
         return [
             lax.ppermute(part, "shard", [(j, j ^ m) for j in range(shards)]) if m else part
-            for part, m in zip(parts, slots(shards))
+            for part, m in zip(parts, partners)
         ]
 
     def send_spectra(c, after):
         table = np.ascontiguousarray(rows[:, :, starts[c] : starts[c] + sizes[c]].transpose(1, 0, 2, 3))
         table = jnp.asarray(table.reshape(-1, NSAMP))
         parts, token = channelize(place, table, voltages, sizes[c], shards, after)
-        return exchange(parts), token
-
-    order = sorted(range(len(sizes)), key=lambda c: -sizes[c])
-    column = {c: shards * sum(sizes[e] for e in order[: order.index(c)]) for c in order}
+        return exchange(parts, far + near), token
+
+    columns = [shards * at for at in starts]
 
     def make_phases(token):
         by_shard = ((delays + token[0, 0]) & (frames - 1)).reshape(shards, local, trials)
-        by_chunk = [by_shard[:, starts[c] : starts[c] + sizes[c]].reshape(-1, trials) for c in order]
+        by_chunk = [by_shard[:, at : at + size].reshape(-1, trials) for at, size in zip(starts, sizes)]
         return phase_tables(jnp.transpose(jnp.concatenate(by_chunk)), frames)
 
     count = len(sizes)
     received, modulated = {}, {}
-    total, phases = None, None
-
-    def add_chunk(c, total, after):
-        last = c + 1 == count
-        return dedisperse(place, *phases, column[c], modulated[c], total, last, np.float32(1.0 / math.sqrt(chans)), after)
+    phases = None
 
     received[0], token = send_spectra(0, [])
     received[1], token = send_spectra(1, [token])
     table = beam_table(grid_index + token[0, 0])
+    half, late = shards // 2, []
     for c in range(count):
         start, size = starts[c], sizes[c]
-        sums, level = form_beams(place, feed_gains, table, received[c], start, size, frames, [token])
+        last = c + 1 == count
+        ahead = modulated[c - 1] if 0 < c < count - 1 else []
+        sums, level = form_beams(place, feed_gains, table, received[c], start, size, frames, [token] + ahead)
         levels = lax.all_gather(level, "section")
         decay = decay_rates[start : start + size].reshape(size, 1)
-        ready, token = normalise(section, levels, decay, sums, scale, [])
-        modulated[c] = exchange(ready)
+        if not last:
+            ready, token = normalise(section, levels, decay, sums[:half], scale, [])
+            modulated[c] = exchange(ready, far)
+            late.append((c, (levels, decay, sums[half:])))
+        else:
+            after = modulated[c - 1][:half] if c else []
+            ready, token = normalise(section, levels, decay, sums, scale, after)
+            modulated[c] = exchange(ready, far + near)
+        if last:
+            for e, held in late:
+                modulated[e] = modulated[e] + exchange(normalise(section, *held, scale, [token])[0], near)
         if c == 0:
             phases = make_phases(token)
             token = phases[0]
-        else:
-            total, token = add_chunk(c - 1, total, [token])
         if c + 2 < count:
             received[c + 2], token = send_spectra(c + 2, [token])
-    total, _ = add_chunk(count - 1, total, [])
+    chunks = [modulated[c] for c in reversed(range(count))]
+    total = dedisperse(place, *phases, columns[::-1], chunks, np.float32(1.0 / math.sqrt(chans)))
     return total.reshape(1, MODF, trials, 2, feeds // shards)
 
 

time: 518 us -> 511 us (0.986)
  local copies, waits for them, and re-layouts: 26 us -> 10.4 us
  waiting for transfers between devices: 156 us -> 165 us
    unnamed x64 -> x68, local copies, waits for them, and re-layouts: 19.1 us -> 3.45 us
    ppermute x42, waiting for transfers between devices: 156 us -> 165 us  [exchange(): lax.ppermute(part, 'shard', [(j, j ^ m) for j in range(shards)])]
    pallas_call x3 -> x5, Pallas kernels: 9.13 us -> 12.9 us  [normalise(): pl.pallas_call(functools.partial(normalise_kernel, levels.shape[0], len(s...]
    pallas_call x3 -> x1, Pallas kernels: 12.7 us -> 12.3 us  [dedisperse(): pl.pallas_call(functools.partial(dedisperse_kernel, shards, columns, size...]
  transfers between devices with their start and end apart: 42 -> 42, of which waited for: 15 -> 13; matrix products, arithmetic and copies ran while one was open for 10% -> 10% of each run, Pallas kernels for 24% -> 23%
where the time goes in v3:
time: 511 us; the launch traced here: 510 us
  waiting for transfers between devices  165 us (32%)
  Pallas kernels  149 us (29%)
  starting transfers between devices  112 us (22%)
  other arithmetic  45.4 us (9%)
  blocking collectives  27.5 us (5%)
  local copies, waits for them, and re-layouts  10.4 us (2%)
    ppermute x42, waiting for transfers between devices, exchange(): lax.ppermute(part, 'shard', [(j, j ^ m) for j in range(shards)])  165 us
    ppermute x42, starting transfers between devices, exchange(): lax.ppermute(part, 'shard', [(j, j ^ m) for j in range(shards)])  112 us
    pallas_call x3, Pallas kernels, form_beams(): pl.pallas_call(functools.partial(beam_kernel, shards, frames), grid_spec=...  67.1 us
    pallas_call x3, Pallas kernels, channelize(): pl.pallas_call(functools.partial(channelize_kernel, shards, size, frames,...  56.9 us
    all_gather x3, blocking collectives, pipelined(): levels = lax.all_gather(level, 'section')  27.5 us
    convert_element_type x1, other arithmetic, phase_tables(): sine = cosine_of(turn - frames // 4, frames).astype(jnp.bfloat16)  23.8 us
    convert_element_type x1, other arithmetic, beam_table(): return cosine_of(turn, GRID_Y).astype(jnp.bfloat16)  18.6 us
    pallas_call x5, Pallas kernels, normalise(): pl.pallas_call(functools.partial(normalise_kernel, levels.shape[0], len(s...  12.9 us
  transfers between devices with their start and end apart: 42, of which 13 were waited for; matrix products, arithmetic and copies ran while one was open for 10% of the time, Pallas kernels for 23%

profile of v3, /device:TPU:0, one launch (start us, length us, event | category | flops | bytes accessed | tf_op | source)
XLA Modules:
  0.0 510.4 jit_solution(2747667598234600204)
XLA Ops:
  0.0 15.5 %channelize.3 = (bf16[2,2,16,32,128]{4,3,2,1,0:T(8,128)(2,1)}, bf16[2,2,16,32,128]{4,3,2,1,0:T(8,128)(2,1)}, bf16[2,2,16,32,128]{4,3,2,1,0:T(8,128)(2,1)}, bf16[...) custom-call(s32[1]{0:T(128)} %bitcast.place, ...), custom_call_target="tpu_custom_call" | custom-call | flops 1000 | bytes 1000 | tf_op jit(solution)/shard_map/channelize/pallas_call | solution.py:104
  15.5 4.1 collective-permute-start
  19.6 3.1 collective-permute-start.2
  23.3 25.9 %channelize.4 = (bf16[2,2,16,64,128]{4,3,2,1,0:T(8,128)(2,1)}, bf16[2,2,16,64,128]{4,3,2,1,0:T(8,128)(2,1)}, bf16[2,2,16,64,128]{4,3,2,1,0:T(8,128)(2,1)}, bf16[...) custom-call(s32[1]{0:T(128)} %bitcast.place, ...), custom_call_target="tpu_custom_call" | custom-call | flops 1000 | bytes 1000 | tf_op jit(solution)/shard_map/channelize/pallas_call | solution.py:104
  51.2 26.4 %collective-permute-done.rest_0_ = bf16[2,2,16,32,128]{4,3,2,1,0:T(8,128)(2,1)} collective-permute-done((bf16[2,2,16,32,128]{4,3,2,1,0:T(8,128)(2,1)}, bf16[2,2,16,32,128]{4,3,2,1,0:T(8,128)(2,1)}, u32[]{:S(2)}, u32[]{:S(2)}) %collective-permute-start) | collective-permute-done | bytes 524320 | tf_op jit(solution)/shard_map/ppermute | solution.py:288
  77.6 9.7 %collective-permute-done.1.rest_1_ = bf16[2,2,16,32,128]{4,3,2,1,0:T(8,128)(2,1)} collective-permute-done((bf16[2,2,16,32,128]{4,3,2,1,0:T(8,128)(2,1)}, bf16[2,2,16,32,128]{4,3,2,1,0:T(8,128)(2,1)}, u32[]{:S(2)}, u32[]{:S(2)}) %collective-permute-start.1) | collective-permute-done | bytes 524320 | tf_op jit(solution)/shard_map/ppermute | solution.py:288
  88.7 18.6 %multiply_convert_fusion.table = bf16[2048,2048]{1,0:T(8,128)(2,1)} fusion(s32[2048]{0:T(1024)S(1)} %get-tuple-element.175, s32[2048]{0:T(1024)S(1)} %get-tuple-element.176, s32[2048]{0:T(1024)S(1)} %get-tuple-element.177, s32[2048]{0:T(1024)S(1)} %get-tuple-element.172, s32[2048]{0:T(1024)S(1)} %get-tuple-element.178, s32[2048]{0:T(1024)S(1)} %get-tuple-element.171), kind=kLoop, calls=%fused_computation.2 | loop fusion | flops 117440512 | bytes 8437760 | tf_op jit(solution)/shard_map/convert_element_type | solution.py:53
  108.9 37.6 %collective-permute-start.15 = (bf16[2,2,16,64,128]{4,3,2,1,0:T(8,128)(2,1)}, bf16[2,2,16,64,128]{4,3,2,1,0:T(8,128)(2,1)}, u32[]{:S(2)}, u32[]{:S(2)}) collective-permute-start(bf16[2,2,16,64,128]{4,3,2,1,0:T(8,128)(2,1)} %get-tuple-element.111), channel_id=1, source_target_pairs={{0,5},{1,4},{2,7},{3,6},{4,1},{5,0},{6,3},{7,2},{8,13},{9,12},{10,... | collective-permute-start | bytes 3145736 | tf_op jit(solution)/shard_map/ppermute | solution.py:288
  146.5 18.0 %form_beams.3 = (f32[14,32,128]{2,1,0:T(8,128)}, f32[14,32,128]{2,1,0:T(8,128)}, f32[14,32,128]{2,1,0:T(8,128)}, f32[14,32,128]{2,1,0:T(8,128)}, f32[14,32,128]{...) custom-call(s32[1]{0:T(128)} %bitcast.place, ...), custom_call_target="tpu_custom_call" | custom-call | flops 1000 | bytes 1000 | tf_op jit(solution)/shard_map/form_beams/pallas_call | solution.py:157
  164.5 8.6 %all-gather = f32[128,128]{1,0:T(8,128)} all-gather(f32[32,128]{1,0:T(8,128)} %get-tuple-element.96), channel_id=2, replica_groups=mesh['section'=4,'shard'=8] {'section'}, dimensions={0}, use_global_device_ids=true | all-gather | bytes 81920 | tf_op jit(solution)/shard_map/all_gather | solution.py:318
  173.2 2.3 normalise.5
  179.3 1.9 copy.18
  181.2 23.8 %fusion.39 = (bf16[7,512,1024]{2,1,0:T(8,128)(2,1)}, bf16[7,512,1024]{2,1,0:T(8,128)(2,1)}) fusion(s32[512,1024]{1,0:T(8,128)S(1)} %copy.18, s32[7]{0:T(128)S(1)} %iota_add_fusion), kind=kLoop, calls=%fused_computation.42 | loop fusion | flops 157810688 | bytes 16777244 | tf_op jit(solution)/shard_map/convert_element_type | solution.py:258
  205.0 15.5 %channelize.5 = (bf16[2,2,16,32,128]{4,3,2,1,0:T(8,128)(2,1)}, bf16[2,2,16,32,128]{4,3,2,1,0:T(8,128)(2,1)}, bf16[2,2,16,32,128]{4,3,2,1,0:T(8,128)(2,1)}, bf16[...) custom-call(s32[1]{0:T(128)} %bitcast.place, ...), custom_call_target="tpu_custom_call" | custom-call | flops 1000 | bytes 1000 | tf_op jit(solution)/shard_map/channelize/pallas_call | solution.py:104
  220.7 2.9 collective-permute-start.21
  223.5 28.8 %collective-permute-done.21.rest_9_.rest_16_ = bf16[14,32,128]{2,1,0:T(8,128)(2,1)S(1)} collective-permute-done((bf16[14,32,128]{2,1,0:T(8,128)(2,1)S(1)}, bf16[14,32,128]{2,1,0:T(8,128)(2,1)S(1)}, u32[]{:S(2)}, u32[]{:S(2)}) %collective-permute-start.21) | collective-permute-done | bytes 114720 | tf_op jit(solution)/shard_map/ppermute | solution.py:288
  252.4 7.2 %collective-permute-done.22.rest_10_.rest_17_ = bf16[14,32,128]{2,1,0:T(8,128)(2,1)S(1)} collective-permute-done((bf16[14,32,128]{2,1,0:T(8,128)(2,1)S(1)}, bf16[14,32,128]{2,1,0:T(8,128)(2,1)S(1)}, u32[]{:S(2)}, u32[]{:S(2)}) %collective-permute-start.22) | collective-permute-done | bytes 114720 | tf_op jit(solution)/shard_map/ppermute | solution.py:288
  259.6 2.0 collective-permute-start.23
  261.6 5.0 collective-permute-done.23.rest_11_.rest_18_
  267.4 5.8 %collective-permute-done.24.rest_12_.rest_19_ = bf16[14,32,128]{2,1,0:T(8,128)(2,1)S(1)} collective-permute-done((bf16[14,32,128]{2,1,0:T(8,128)(2,1)S(1)}, bf16[14,32,128]{2,1,0:T(8,128)(2,1)S(1)}, u32[]{:S(2)}, u32[]{:S(2)}) %collective-permute-start.24) | collective-permute-done | bytes 114720 | tf_op jit(solution)/shard_map/ppermute | solution.py:288
  273.3 2.1 collective-permute-start.16
  276.7 3.0 collective-permute-start.19
  279.7 21.9 %collective-permute-done.16.rest_2_ = bf16[2,2,16,64,128]{4,3,2,1,0:T(8,128)(2,1)S(1)} collective-permute-done((bf16[2,2,16,64,128]{4,3,2,1,0:T(8,128)(2,1)}, bf16[2,2,16,64,128]{4,3,2,1,0:T(8,128)(2,1)S(1)}, u32[]{:S(2)}, u32[]{:S(2)}) %collective-permute-start.16) | collective-permute-done | bytes 1048608 | tf_op jit(solution)/shard_map/ppermute | solution.py:288
  301.5 2.1 collective-permute-start.9
  303.6 18.2 %collective-permute-done.17.rest_3_ = bf16[2,2,16,64,128]{4,3,2,1,0:T(8,128)(2,1)S(1)} collective-permute-done((bf16[2,2,16,64,128]{4,3,2,1,0:T(8,128)(2,1)}, bf16[2,2,16,64,128]{4,3,2,1,0:T(8,128)(2,1)S(1)}, u32[]{:S(2)}, u32[]{:S(2)}) %collective-permute-start.17) | collective-permute-done | bytes 1048608 | tf_op jit(solution)/shard_map/ppermute | solution.py:288
  321.8 3.6 collective-permute-start.10
  325.4 19.4 %collective-permute-done.18.rest_4_ = bf16[2,2,16,64,128]{4,3,2,1,0:T(8,128)(2,1)} collective-permute-done((bf16[2,2,16,64,128]{4,3,2,1,0:T(8,128)(2,1)}, bf16[2,2,16,64,128]{4,3,2,1,0:T(8,128)(2,1)}, u32[]{:S(2)}, u32[]{:S(2)}) %collective-permute-start.18) | collective-permute-done | bytes 1048608 | tf_op jit(solution)/shard_map/ppermute | solution.py:288
  344.8 19.7 %collective-permute-start.11 = (bf16[2,2,16,32,128]{4,3,2,1,0:T(8,128)(2,1)}, bf16[2,2,16,32,128]{4,3,2,1,0:T(8,128)(2,1)}, u32[]{:S(2)}, u32[]{:S(2)}) collective-permute-start(bf16[2,2,16,32,128]{4,3,2,1,0:T(8,128)(2,1)} %get-tuple-element.106), channel_id=1, source_target_pairs={{0,3},{1,2},{2,1},{3,0},{4,7},{5,6},{6,5},{7,4},{8,11},{9,10},{10,... | collective-permute-start | bytes 1572872 | tf_op jit(solution)/shard_map/ppermute | solution.py:288
  364.5 4.6 collective-permute-done.19.rest_5_
  370.1 31.0 %form_beams.4 = (f32[14,64,128]{2,1,0:T(8,128)}, f32[14,64,128]{2,1,0:T(8,128)}, f32[14,64,128]{2,1,0:T(8,128)}, f32[14,64,128]{2,1,0:T(8,128)}, f32[14,64,128]{...) custom-call(s32[1]{0:T(128)} %bitcast.place, ...), custom_call_target="tpu_custom_call" | custom-call | flops 1000 | bytes 1000 | tf_op jit(solution)/shard_map/form_beams/pallas_call | solution.py:157
  401.0 10.2 %all-gather.1 = f32[256,128]{1,0:T(8,128)} all-gather(f32[64,128]{1,0:T(8,128)} %get-tuple-element.123), channel_id=3, replica_groups=mesh['section'=4,'shard'=8] {'section'}, dimensions={0}, use_global_device_ids=true | all-gather | bytes 163840 | tf_op jit(solution)/shard_map/all_gather | solution.py:318
  411.3 2.8 normalise.6
  414.1 2.5 collective-permute-start.25
  418.2 2.1 collective-permute-start.28
  421.0 18.1 %form_beams.5 = (f32[14,32,128]{2,1,0:T(8,128)}, f32[14,32,128]{2,1,0:T(8,128)}, f32[14,32,128]{2,1,0:T(8,128)}, f32[14,32,128]{2,1,0:T(8,128)}, f32[14,32,128]{...) custom-call(s32[1]{0:T(128)} %bitcast.place, ...), custom_call_target="tpu_custom_call" | custom-call | flops 1000 | bytes 1000 | tf_op jit(solution)/shard_map/form_beams/pallas_call | solution.py:157
  439.1 8.6 %all-gather.2 = f32[128,128]{1,0:T(8,128)} all-gather(f32[32,128]{1,0:T(8,128)} %get-tuple-element.129), channel_id=4, replica_groups=mesh['section'=4,'shard'=8] {'section'}, dimensions={0}, use_global_device_ids=true | all-gather | bytes 81920 | tf_op jit(solution)/shard_map/all_gather | solution.py:318
  448.8 2.7 normalise.7
  451.5 8.0 %collective-permute-start.29 = (bf16[14,32,128]{2,1,0:T(8,128)(2,1)}, bf16[14,32,128]{2,1,0:T(8,128)(2,1)S(1)}, u32[]{:S(2)}, u32[]{:S(2)}) collective-permute-start(bf16[14,32,128]{2,1,0:T(8,128)(2,1)} %get-tuple-element.142), channel_id=1, source_target_pairs={{0,4},{1,5},{2,6},{3,7},{4,0},{5,1},{6,2},{7,3},{8,12},{9,13},{10,... | collective-permute-start | bytes 344072 | tf_op jit(solution)/shard_map/ppermute | solution.py:288
  460.5 1.9 collective-permute-start.31
  464.3 1.9 collective-permute-start.34
  466.2 2.8 normalise.8
  469.0 2.3 normalise.9
  471.3 5.1 collective-permute-done.30.rest_1_
  476.4 2.6 collective-permute-start.35
  481.0 1.6 collective-permute-start.37
  483.4 5.9 %collective-permute-done.39.rest_20_ = bf16[14,32,128]{2,1,0:T(8,128)(2,1)S(1)} collective-permute-done((bf16[14,32,128]{2,1,0:T(8,128)(2,1)}, bf16[14,32,128]{2,1,0:T(8,128)(2,1)S(1)}, u32[]{:S(2)}, u32[]{:S(2)}) %collective-permute-start.39) | collective-permute-done | bytes 114720 | tf_op jit(solution)/shard_map/ppermute | solution.py:288
  489.7 7.3 %collective-permute-done.40.rest_21_ = bf16[14,32,128]{2,1,0:T(8,128)(2,1)S(1)} collective-permute-done((bf16[14,32,128]{2,1,0:T(8,128)(2,1)}, bf16[14,32,128]{2,1,0:T(8,128)(2,1)S(1)}, u32[]{:S(2)}, u32[]{:S(2)}) %collective-permute-start.40) | collective-permute-done | bytes 114720 | tf_op jit(solution)/shard_map/ppermute | solution.py:288
  497.9 12.3 %dedisperse.1 = bf16[7,1024,128]{2,1,0:T(8,128)(2,1)} custom-call(s32[1]{0:T(128)} %bitcast.place, bf16[7,512,1024]{2,1,0:T(8,128)(2,1)} %get-tuple-element.168.rest_0_.cosine, bf16[7,512,1024]{2,1,0:T(8,128)(2,1)} %get-tuple-element.167.sine, bf16[14,32,128]{2,1,0:T(8,128)(2,1)} %copy-done.18, bf16[14,32,128]{2,1,0:T(8,128)(2,1)} %copy-done.19, ...), custom_call_target="tpu_custom_call" | custom-call | flops 1000 | bytes 1000 | tf_op jit(solution)/shard_map/dedisperse/pallas_call | solution.py:238
  (138 shorter events, 22.8 us)
Async XLA Ops:
  15.5 62.1 %collective-permute-start = (bf16[2,2,16,32,128]{4,3,2,1,0:T(8,128)(2,1)}, bf16[2,2,16,32,128]{4,3,2,1,0:T(8,128)(2,1)}, u32[]{:S(2)}, u32[]{:S(2)}) collective-permute-start(bf16[2,2,16,32,128]{4,3,2,1,0:T(8,128)(2,1)} %get-tuple-element.88), channel_id=1, source_target_pairs={{0,4},{1,5},{2,6},{3,7},{4,0},{5,1},{6,2},{7,3},{8,12},{9,13},{10,... | collective-permute-start | bytes 1572872 | tf_op jit(solution)/shard_map/ppermute | solution.py:288
  19.6 67.7 %collective-permute-start.1 = (bf16[2,2,16,32,128]{4,3,2,1,0:T(8,128)(2,1)}, bf16[2,2,16,32,128]{4,3,2,1,0:T(8,128)(2,1)}, u32[]{:S(2)}, u32[]{:S(2)}) collective-permute-start(bf16[2,2,16,32,128]{4,3,2,1,0:T(8,128)(2,1)} %get-tuple-element.89), channel_id=1, source_target_pairs={{0,5},{1,4},{2,7},{3,6},{4,1},{5,0},{6,3},{7,2},{8,13},{9,12},{10,... | collective-permute-start | bytes 1572872 | tf_op jit(solution)/shard_map/ppermute | solution.py:288
  19.6 88.5 %collective-permute-start.2 = (bf16[2,2,16,32,128]{4,3,2,1,0:T(8,128)(2,1)}, bf16[2,2,16,32,128]{4,3,2,1,0:T(8,128)(2,1)S(1)}, u32[]{:S(2)}, u32[]{:S(2)}) collective-permute-start(bf16[2,2,16,32,128]{4,3,2,1,0:T(8,128)(2,1)} %get-tuple-element.90), channel_id=1, source_target_pairs={{0,6},{1,7},{2,4},{3,5},{4,2},{5,3},{6,0},{7,1},{8,14},{9,15},{10,... | collective-permute-start | bytes 1572872 | tf_op jit(solution)/shard_map/ppermute | solution.py:288
  22.7 86.2 %collective-permute-start.3 = (bf16[2,2,16,32,128]{4,3,2,1,0:T(8,128)(2,1)}, bf16[2,2,16,32,128]{4,3,2,1,0:T(8,128)(2,1)}, u32[]{:S(2)}, u32[]{:S(2)}) collective-permute-start(bf16[2,2,16,32,128]{4,3,2,1,0:T(8,128)(2,1)} %get-tuple-element.91), channel_id=1, source_target_pairs={{0,7},{1,6},{2,5},{3,4},{4,3},{5,2},{6,1},{7,0},{8,15},{9,14},{10,... | collective-permute-start | bytes 1572872 | tf_op jit(solution)/shard_map/ppermute | solution.py:288
  23.3 123.2 %collective-permute-start.4 = (bf16[2,2,16,32,128]{4,3,2,1,0:T(8,128)(2,1)}, bf16[2,2,16,32,128]{4,3,2,1,0:T(8,128)(2,1)}, u32[]{:S(2)}, u32[]{:S(2)}) collective-permute-start(bf16[2,2,16,32,128]{4,3,2,1,0:T(8,128)(2,1)} %get-tuple-element.92), channel_id=1, source_target_pairs={{0,3},{1,2},{2,1},{3,0},{4,7},{5,6},{6,5},{7,4},{8,11},{9,10},{10,... | collective-permute-start | bytes 1572872 | tf_op jit(solution)/shard_map/ppermute | solution.py:288
  23.3 84.0 %copy-start.29 = (f32[128]{0:T(128)S(1)}, f32[128]{0:T(128)}, u32[]{:S(2)}) copy-start(f32[128]{0:T(128)} %param.11) | copy-start | bytes 1540
  49.2 127.5 %copy-start = (s32[1024,512]{1,0:T(8,128)S(1)}, s32[1024,512]{1,0:T(8,128)}, u32[]{:S(2)}) copy-start(s32[1024,512]{1,0:T(8,128)} %param.12) | copy-start | bytes 6291460
  77.6 68.9 %collective-permute-start.5 = (bf16[2,2,16,32,128]{4,3,2,1,0:T(8,128)(2,1)}, bf16[2,2,16,32,128]{4,3,2,1,0:T(8,128)(2,1)}, u32[]{:S(2)}, u32[]{:S(2)}) collective-permute-start(bf16[2,2,16,32,128]{4,3,2,1,0:T(8,128)(2,1)} %get-tuple-element.93), channel_id=1, source_target_pairs={{0,2},{1,3},{2,0},{3,1},{4,6},{5,7},{6,4},{7,5},{8,10},{9,11},{10,... | collective-permute-start | bytes 1572872 | tf_op jit(solution)/shard_map/ppermute | solution.py:288
  87.3 59.2 %collective-permute-start.6 = (bf16[2,2,16,32,128]{4,3,2,1,0:T(8,128)(2,1)}, bf16[2,2,16,32,128]{4,3,2,1,0:T(8,128)(2,1)}, u32[]{:S(2)}, u32[]{:S(2)}) collective-permute-start(bf16[2,2,16,32,128]{4,3,2,1,0:T(8,128)(2,1)} %get-tuple-element.94), channel_id=1, source_target_pairs={{0,1},{1,0},{2,3},{3,2},{4,5},{5,4},{6,7},{7,6},{8,9},{9,8},{10,11... | collective-permute-start | bytes 1572872 | tf_op jit(solution)/shard_map/ppermute | solution.py:288
  108.9 167.7 %collective-permute-start.14 = (bf16[2,2,16,64,128]{4,3,2,1,0:T(8,128)(2,1)}, bf16[2,2,16,64,128]{4,3,2,1,0:T(8,128)(2,1)S(1)}, u32[]{:S(2)}, u32[]{:S(2)}) collective-permute-start(bf16[2,2,16,64,128]{4,3,2,1,0:T(8,128)(2,1)} %get-tuple-element.110), channel_id=1, source_target_pairs={{0,4},{1,5},{2,6},{3,7},{4,0},{5,1},{6,2},{7,3},{8,12},{9,13},{10,... | collective-permute-start | bytes 3145736 | tf_op jit(solution)/shard_map/ppermute | solution.py:288
  108.9 170.8 %collective-permute-start.15 = (bf16[2,2,16,64,128]{4,3,2,1,0:T(8,128)(2,1)}, bf16[2,2,16,64,128]{4,3,2,1,0:T(8,128)(2,1)}, u32[]{:S(2)}, u32[]{:S(2)}) collective-permute-start(bf16[2,2,16,64,128]{4,3,2,1,0:T(8,128)(2,1)} %get-tuple-element.111), channel_id=1, source_target_pairs={{0,5},{1,4},{2,7},{3,6},{4,1},{5,0},{6,3},{7,2},{8,13},{9,12},{10,... | collective-permute-start | bytes 3145736 | tf_op jit(solution)/shard_map/ppermute | solution.py:288
  220.5 54.9 %collective-permute-start.7 = (bf16[2,2,16,32,128]{4,3,2,1,0:T(8,128)(2,1)}, bf16[2,2,16,32,128]{4,3,2,1,0:T(8,128)(2,1)S(1)}, u32[]{:S(2)}, u32[]{:S(2)}) collective-permute-start(bf16[2,2,16,32,128]{4,3,2,1,0:T(8,128)(2,1)} %get-tuple-element.102), channel_id=1, source_target_pairs={{0,4},{1,5},{2,6},{3,7},{4,0},{5,1},{6,2},{7,3},{8,12},{9,13},{10,... | collective-permute-start | bytes 1572872 | tf_op jit(solution)/shard_map/ppermute | solution.py:288
  220.6 56.1 %collective-permute-start.8 = (bf16[2,2,16,32,128]{4,3,2,1,0:T(8,128)(2,1)}, bf16[2,2,16,32,128]{4,3,2,1,0:T(8,128)(2,1)S(1)}, u32[]{:S(2)}, u32[]{:S(2)}) collective-permute-start(bf16[2,2,16,32,128]{4,3,2,1,0:T(8,128)(2,1)} %get-tuple-element.103), channel_id=1, source_target_pairs={{0,5},{1,4},{2,7},{3,6},{4,1},{5,0},{6,3},{7,2},{8,13},{9,12},{10,... | collective-permute-start | bytes 1572872 | tf_op jit(solution)/shard_map/ppermute | solution.py:288
  220.7 31.7 %collective-permute-start.21 = (bf16[14,32,128]{2,1,0:T(8,128)(2,1)S(1)}, bf16[14,32,128]{2,1,0:T(8,128)(2,1)S(1)}, u32[]{:S(2)}, u32[]{:S(2)}) collective-permute-start(bf16[14,32,128]{2,1,0:T(8,128)(2,1)S(1)} %copy-done.33), channel_id=1, source_target_pairs={{0,4},{1,5},{2,6},{3,7},{4,0},{5,1},{6,2},{7,3},{8,12},{9,13},{10,... | collective-permute-start | bytes 344072 | tf_op jit(solution)/shard_map/ppermute | solution.py:288
  252.4 117.7 %copy-start.11 = (bf16[14,32,128]{2,1,0:T(8,128)(2,1)}, bf16[14,32,128]{2,1,0:T(8,128)(2,1)S(1)}, u32[]{:S(2)}) copy-start(bf16[14,32,128]{2,1,0:T(8,128)(2,1)S(1)} %collective-permute-done.21.rest_9_.rest_16_) | copy-start | bytes 344068
  252.4 7.2 %collective-permute-start.22 = (bf16[14,32,128]{2,1,0:T(8,128)(2,1)S(1)}, bf16[14,32,128]{2,1,0:T(8,128)(2,1)S(1)}, u32[]{:S(2)}, u32[]{:S(2)}) collective-permute-start(bf16[14,32,128]{2,1,0:T(8,128)(2,1)S(1)} %copy-done.32), channel_id=1, source_target_pairs={{0,5},{1,4},{2,7},{3,6},{4,1},{5,0},{6,3},{7,2},{8,13},{9,12},{10,... | collective-permute-start | bytes 344072 | tf_op jit(solution)/shard_map/ppermute | solution.py:288
  259.6 110.4 %copy-start.12 = (bf16[14,32,128]{2,1,0:T(8,128)(2,1)}, bf16[14,32,128]{2,1,0:T(8,128)(2,1)S(1)}, u32[]{:S(2)}) copy-start(bf16[14,32,128]{2,1,0:T(8,128)(2,1)S(1)} %collective-permute-done.22.rest_10_.rest_17_) | copy-start | bytes 344068
  259.6 7.0 %collective-permute-start.23 = (bf16[14,32,128]{2,1,0:T(8,128)(2,1)S(1)}, bf16[14,32,128]{2,1,0:T(8,128)(2,1)S(1)}, u32[]{:S(2)}, u32[]{:S(2)}) collective-permute-start(bf16[14,32,128]{2,1,0:T(8,128)(2,1)S(1)} %copy-done.31), channel_id=1, source_target_pairs={{0,6},{1,7},{2,4},{3,5},{4,2},{5,3},{6,0},{7,1},{8,14},{9,15},{10,... | collective-permute-start | bytes 344072 | tf_op jit(solution)/shard_map/ppermute | solution.py:288
  266.6 103.5 %copy-start.13 = (bf16[14,32,128]{2,1,0:T(8,128)(2,1)}, bf16[14,32,128]{2,1,0:T(8,128)(2,1)S(1)}, u32[]{:S(2)}) copy-start(bf16[14,32,128]{2,1,0:T(8,128)(2,1)S(1)} %collective-permute-done.23.rest_11_.rest_18_) | copy-start | bytes 344068
  266.6 6.7 %collective-permute-start.24 = (bf16[14,32,128]{2,1,0:T(8,128)(2,1)S(1)}, bf16[14,32,128]{2,1,0:T(8,128)(2,1)S(1)}, u32[]{:S(2)}, u32[]{:S(2)}) collective-permute-start(bf16[14,32,128]{2,1,0:T(8,128)(2,1)S(1)} %copy-done.30), channel_id=1, source_target_pairs={{0,7},{1,6},{2,5},{3,4},{4,3},{5,2},{6,1},{7,0},{8,15},{9,14},{10,... | collective-permute-start | bytes 344072 | tf_op jit(solution)/shard_map/ppermute | solution.py:288
  273.3 28.3 %collective-permute-start.16 = (bf16[2,2,16,64,128]{4,3,2,1,0:T(8,128)(2,1)}, bf16[2,2,16,64,128]{4,3,2,1,0:T(8,128)(2,1)S(1)}, u32[]{:S(2)}, u32[]{:S(2)}) collective-permute-start(bf16[2,2,16,64,128]{4,3,2,1,0:T(8,128)(2,1)} %get-tuple-element.112), channel_id=1, source_target_pairs={{0,6},{1,7},{2,4},{3,5},{4,2},{5,3},{6,0},{7,1},{8,14},{9,15},{10,... | collective-permute-start | bytes 3145736 | tf_op jit(solution)/shard_map/ppermute | solution.py:288
  276.2 45.6 %collective-permute-start.17 = (bf16[2,2,16,64,128]{4,3,2,1,0:T(8,128)(2,1)}, bf16[2,2,16,64,128]{4,3,2,1,0:T(8,128)(2,1)S(1)}, u32[]{:S(2)}, u32[]{:S(2)}) collective-permute-start(bf16[2,2,16,64,128]{4,3,2,1,0:T(8,128)(2,1)} %get-tuple-element.113), channel_id=1, source_target_pairs={{0,7},{1,6},{2,5},{3,4},{4,3},{5,2},{6,1},{7,0},{8,15},{9,14},{10,... | collective-permute-start | bytes 3145736 | tf_op jit(solution)/shard_map/ppermute | solution.py:288
  276.6 68.2 %collective-permute-start.18 = (bf16[2,2,16,64,128]{4,3,2,1,0:T(8,128)(2,1)}, bf16[2,2,16,64,128]{4,3,2,1,0:T(8,128)(2,1)}, u32[]{:S(2)}, u32[]{:S(2)}) collective-permute-start(bf16[2,2,16,64,128]{4,3,2,1,0:T(8,128)(2,1)} %get-tuple-element.114), channel_id=1, source_target_pairs={{0,3},{1,2},{2,1},{3,0},{4,7},{5,6},{6,5},{7,4},{8,11},{9,10},{10,... | collective-permute-start | bytes 3145736 | tf_op jit(solution)/shard_map/ppermute | solution.py:288
  276.7 93.4 %copy-start.1 = (bf16[2,2,16,64,128]{4,3,2,1,0:T(8,128)(2,1)}, bf16[2,2,16,64,128]{4,3,2,1,0:T(8,128)(2,1)S(1)}, u32[]{:S(2)}) copy-start(bf16[2,2,16,64,128]{4,3,2,1,0:T(8,128)(2,1)S(1)} %collective-permute-done.14.rest_0_) | copy-start | bytes 3145732
  276.7 92.4 %collective-permute-start.19 = (bf16[2,2,16,64,128]{4,3,2,1,0:T(8,128)(2,1)}, bf16[2,2,16,64,128]{4,3,2,1,0:T(8,128)(2,1)}, u32[]{:S(2)}, u32[]{:S(2)}) collective-permute-start(bf16[2,2,16,64,128]{4,3,2,1,0:T(8,128)(2,1)} %get-tuple-element.115), channel_id=1, source_target_pairs={{0,2},{1,3},{2,0},{3,1},{4,6},{5,7},{6,4},{7,5},{8,10},{9,11},{10,... | collective-permute-start | bytes 3145736 | tf_op jit(solution)/shard_map/ppermute | solution.py:288
  279.7 89.6 %collective-permute-start.20 = (bf16[2,2,16,64,128]{4,3,2,1,0:T(8,128)(2,1)}, bf16[2,2,16,64,128]{4,3,2,1,0:T(8,128)(2,1)}, u32[]{:S(2)}, u32[]{:S(2)}) collective-permute-start(bf16[2,2,16,64,128]{4,3,2,1,0:T(8,128)(2,1)} %get-tuple-element.116), channel_id=1, source_target_pairs={{0,1},{1,0},{2,3},{3,2},{4,5},{5,4},{6,7},{7,6},{8,9},{9,8},{10,11... | collective-permute-start | bytes 3145736 | tf_op jit(solution)/shard_map/ppermute | solution.py:288
  301.5 112.6 %collective-permute-start.9 = (bf16[2,2,16,32,128]{4,3,2,1,0:T(8,128)(2,1)}, bf16[2,2,16,32,128]{4,3,2,1,0:T(8,128)(2,1)}, u32[]{:S(2)}, u32[]{:S(2)}) collective-permute-start(bf16[2,2,16,32,128]{4,3,2,1,0:T(8,128)(2,1)} %get-tuple-element.104), channel_id=1, source_target_pairs={{0,6},{1,7},{2,4},{3,5},{4,2},{5,3},{6,0},{7,1},{8,14},{9,15},{10,... | collective-permute-start | bytes 1572872 | tf_op jit(solution)/shard_map/ppermute | solution.py:288
  321.8 94.8 %collective-permute-start.10 = (bf16[2,2,16,32,128]{4,3,2,1,0:T(8,128)(2,1)}, bf16[2,2,16,32,128]{4,3,2,1,0:T(8,128)(2,1)}, u32[]{:S(2)}, u32[]{:S(2)}) collective-permute-start(bf16[2,2,16,32,128]{4,3,2,1,0:T(8,128)(2,1)} %get-tuple-element.105), channel_id=1, source_target_pairs={{0,7},{1,6},{2,5},{3,4},{4,3},{5,2},{6,1},{7,0},{8,15},{9,14},{10,... | collective-permute-start | bytes 1572872 | tf_op jit(solution)/shard_map/ppermute | solution.py:288
  344.8 71.8 %collective-permute-start.11 = (bf16[2,2,16,32,128]{4,3,2,1,0:T(8,128)(2,1)}, bf16[2,2,16,32,128]{4,3,2,1,0:T(8,128)(2,1)}, u32[]{:S(2)}, u32[]{:S(2)}) collective-permute-start(bf16[2,2,16,32,128]{4,3,2,1,0:T(8,128)(2,1)} %get-tuple-element.106), channel_id=1, source_target_pairs={{0,3},{1,2},{2,1},{3,0},{4,7},{5,6},{6,5},{7,4},{8,11},{9,10},{10,... | collective-permute-start | bytes 1572872 | tf_op jit(solution)/shard_map/ppermute | solution.py:288
  369.1 49.1 %collective-permute-start.12 = (bf16[2,2,16,32,128]{4,3,2,1,0:T(8,128)(2,1)}, bf16[2,2,16,32,128]{4,3,2,1,0:T(8,128)(2,1)}, u32[]{:S(2)}, u32[]{:S(2)}) collective-permute-start(bf16[2,2,16,32,128]{4,3,2,1,0:T(8,128)(2,1)} %get-tuple-element.107), channel_id=1, source_target_pairs={{0,2},{1,3},{2,0},{3,1},{4,6},{5,7},{6,4},{7,5},{8,10},{9,11},{10,... | collective-permute-start | bytes 1572872 | tf_op jit(solution)/shard_map/ppermute | solution.py:288
  369.2 51.8 %collective-permute-start.13 = (bf16[2,2,16,32,128]{4,3,2,1,0:T(8,128)(2,1)}, bf16[2,2,16,32,128]{4,3,2,1,0:T(8,128)(2,1)}, u32[]{:S(2)}, u32[]{:S(2)}) collective-permute-start(bf16[2,2,16,32,128]{4,3,2,1,0:T(8,128)(2,1)} %get-tuple-element.108), channel_id=1, source_target_pairs={{0,1},{1,0},{2,3},{3,2},{4,5},{5,4},{6,7},{7,6},{8,9},{9,8},{10,11... | collective-permute-start | bytes 1572872 | tf_op jit(solution)/shard_map/ppermute | solution.py:288
  414.1 33.7 %collective-permute-start.25 = (bf16[14,64,128]{2,1,0:T(8,128)(2,1)}, bf16[14,64,128]{2,1,0:T(8,128)(2,1)S(1)}, u32[]{:S(2)}, u32[]{:S(2)}) collective-permute-start(bf16[14,64,128]{2,1,0:T(8,128)(2,1)} %get-tuple-element.138), channel_id=1, source_target_pairs={{0,4},{1,5},{2,6},{3,7},{4,0},{5,1},{6,2},{7,3},{8,12},{9,13},{10,... | collective-permute-start | bytes 688136 | tf_op jit(solution)/shard_map/ppermute | solution.py:288
  416.6 31.2 %collective-permute-start.26 = (bf16[14,64,128]{2,1,0:T(8,128)(2,1)}, bf16[14,64,128]{2,1,0:T(8,128)(2,1)S(1)}, u32[]{:S(2)}, u32[]{:S(2)}) collective-permute-start(bf16[14,64,128]{2,1,0:T(8,128)(2,1)} %get-tuple-element.139), channel_id=1, source_target_pairs={{0,5},{1,4},{2,7},{3,6},{4,1},{5,0},{6,3},{7,2},{8,13},{9,12},{10,... | collective-permute-start | bytes 688136 | tf_op jit(solution)/shard_map/ppermute | solution.py:288
  416.6 31.2 %collective-permute-start.27 = (bf16[14,64,128]{2,1,0:T(8,128)(2,1)}, bf16[14,64,128]{2,1,0:T(8,128)(2,1)S(1)}, u32[]{:S(2)}, u32[]{:S(2)}) collective-permute-start(bf16[14,64,128]{2,1,0:T(8,128)(2,1)} %get-tuple-element.140), channel_id=1, source_target_pairs={{0,6},{1,7},{2,4},{3,5},{4,2},{5,3},{6,0},{7,1},{8,14},{9,15},{10,... | collective-permute-start | bytes 688136 | tf_op jit(solution)/shard_map/ppermute | solution.py:288
  418.2 29.7 %collective-permute-start.28 = (bf16[14,64,128]{2,1,0:T(8,128)(2,1)}, bf16[14,64,128]{2,1,0:T(8,128)(2,1)S(1)}, u32[]{:S(2)}, u32[]{:S(2)}) collective-permute-start(bf16[14,64,128]{2,1,0:T(8,128)(2,1)} %get-tuple-element.141), channel_id=1, source_target_pairs={{0,7},{1,6},{2,5},{3,4},{4,3},{5,2},{6,1},{7,0},{8,15},{9,14},{10,... | collective-permute-start | bytes 688136 | tf_op jit(solution)/shard_map/ppermute | solution.py:288
  451.5 12.8 %collective-permute-start.29 = (bf16[14,32,128]{2,1,0:T(8,128)(2,1)}, bf16[14,32,128]{2,1,0:T(8,128)(2,1)S(1)}, u32[]{:S(2)}, u32[]{:S(2)}) collective-permute-start(bf16[14,32,128]{2,1,0:T(8,128)(2,1)} %get-tuple-element.142), channel_id=1, source_target_pairs={{0,4},{1,5},{2,6},{3,7},{4,0},{5,1},{6,2},{7,3},{8,12},{9,13},{10,... | collective-permute-start | bytes 344072 | tf_op jit(solution)/shard_map/ppermute | solution.py:288
  459.5 16.9 %collective-permute-start.30 = (bf16[14,32,128]{2,1,0:T(8,128)(2,1)}, bf16[14,32,128]{2,1,0:T(8,128)(2,1)S(1)}, u32[]{:S(2)}, u32[]{:S(2)}) collective-permute-start(bf16[14,32,128]{2,1,0:T(8,128)(2,1)} %get-tuple-element.143), channel_id=1, source_target_pairs={{0,5},{1,4},{2,7},{3,6},{4,1},{5,0},{6,3},{7,2},{8,13},{9,12},{10,... | collective-permute-start | bytes 344072 | tf_op jit(solution)/shard_map/ppermute | solution.py:288
  460.5 18.6 %collective-permute-start.31 = (bf16[14,32,128]{2,1,0:T(8,128)(2,1)}, bf16[14,32,128]{2,1,0:T(8,128)(2,1)S(1)}, u32[]{:S(2)}, u32[]{:S(2)}) collective-permute-start(bf16[14,32,128]{2,1,0:T(8,128)(2,1)} %get-tuple-element.144), channel_id=1, source_target_pairs={{0,6},{1,7},{2,4},{3,5},{4,2},{5,3},{6,0},{7,1},{8,14},{9,15},{10,... | collective-permute-start | bytes 344072 | tf_op jit(solution)/shard_map/ppermute | solution.py:288
  462.3 18.1 %collective-permute-start.32 = (bf16[14,32,128]{2,1,0:T(8,128)(2,1)}, bf16[14,32,128]{2,1,0:T(8,128)(2,1)S(1)}, u32[]{:S(2)}, u32[]{:S(2)}) collective-permute-start(bf16[14,32,128]{2,1,0:T(8,128)(2,1)} %get-tuple-element.145), channel_id=1, source_target_pairs={{0,7},{1,6},{2,5},{3,4},{4,3},{5,2},{6,1},{7,0},{8,15},{9,14},{10,... | collective-permute-start | bytes 344072 | tf_op jit(solution)/shard_map/ppermute | solution.py:288
  463.6 17.3 %collective-permute-start.33 = (bf16[14,32,128]{2,1,0:T(8,128)(2,1)}, bf16[14,32,128]{2,1,0:T(8,128)(2,1)S(1)}, u32[]{:S(2)}, u32[]{:S(2)}) collective-permute-start(bf16[14,32,128]{2,1,0:T(8,128)(2,1)} %get-tuple-element.146), channel_id=1, source_target_pairs={{0,3},{1,2},{2,1},{3,0},{4,7},{5,6},{6,5},{7,4},{8,11},{9,10},{10,... | collective-permute-start | bytes 344072 | tf_op jit(solution)/shard_map/ppermute | solution.py:288
  464.3 18.3 %collective-permute-start.34 = (bf16[14,32,128]{2,1,0:T(8,128)(2,1)}, bf16[14,32,128]{2,1,0:T(8,128)(2,1)S(1)}, u32[]{:S(2)}, u32[]{:S(2)}) collective-permute-start(bf16[14,32,128]{2,1,0:T(8,128)(2,1)} %get-tuple-element.147), channel_id=1, source_target_pairs={{0,2},{1,3},{2,0},{3,1},{4,6},{5,7},{6,4},{7,5},{8,10},{9,11},{10,... | collective-permute-start | bytes 344072 | tf_op jit(solution)/shard_map/ppermute | solution.py:288
  476.4 6.1 %collective-permute-start.35 = (bf16[14,32,128]{2,1,0:T(8,128)(2,1)}, bf16[14,32,128]{2,1,0:T(8,128)(2,1)S(1)}, u32[]{:S(2)}, u32[]{:S(2)}) collective-permute-start(bf16[14,32,128]{2,1,0:T(8,128)(2,1)} %get-tuple-element.148), channel_id=1, source_target_pairs={{0,1},{1,0},{2,3},{3,2},{4,5},{5,4},{6,7},{7,6},{8,9},{9,8},{10,11... | collective-permute-start | bytes 344072 | tf_op jit(solution)/shard_map/ppermute | solution.py:288
  479.0 18.0 %collective-permute-start.36 = (bf16[14,64,128]{2,1,0:T(8,128)(2,1)}, bf16[14,64,128]{2,1,0:T(8,128)(2,1)S(1)}, u32[]{:S(2)}, u32[]{:S(2)}) collective-permute-start(bf16[14,64,128]{2,1,0:T(8,128)(2,1)} %get-tuple-element.155), channel_id=1, source_target_pairs={{0,3},{1,2},{2,1},{3,0},{4,7},{5,6},{6,5},{7,4},{8,11},{9,10},{10,... | collective-permute-start | bytes 688136 | tf_op jit(solution)/shard_map/ppermute | solution.py:288
  480.4 8.9 %collective-permute-start.39 = (bf16[14,32,128]{2,1,0:T(8,128)(2,1)}, bf16[14,32,128]{2,1,0:T(8,128)(2,1)S(1)}, u32[]{:S(2)}, u32[]{:S(2)}) collective-permute-start(bf16[14,32,128]{2,1,0:T(8,128)(2,1)} %get-tuple-element.163), channel_id=1, source_target_pairs={{0,3},{1,2},{2,1},{3,0},{4,7},{5,6},{6,5},{7,4},{8,11},{9,10},{10,... | collective-permute-start | bytes 344072 | tf_op jit(solution)/shard_map/ppermute | solution.py:288
  481.0 16.1 %collective-permute-start.37 = (bf16[14,64,128]{2,1,0:T(8,128)(2,1)}, bf16[14,64,128]{2,1,0:T(8,128)(2,1)S(1)}, u32[]{:S(2)}, u32[]{:S(2)}) collective-permute-start(bf16[14,64,128]{2,1,0:T(8,128)(2,1)} %get-tuple-element.156), channel_id=1, source_target_pairs={{0,2},{1,3},{2,0},{3,1},{4,6},{5,7},{6,4},{7,5},{8,10},{9,11},{10,... | collective-permute-start | bytes 688136 | tf_op jit(solution)/shard_map/ppermute | solution.py:288
  482.5 14.5 %collective-permute-start.38 = (bf16[14,64,128]{2,1,0:T(8,128)(2,1)}, bf16[14,64,128]{2,1,0:T(8,128)(2,1)S(1)}, u32[]{:S(2)}, u32[]{:S(2)}) collective-permute-start(bf16[14,64,128]{2,1,0:T(8,128)(2,1)} %get-tuple-element.157), channel_id=1, source_target_pairs={{0,1},{1,0},{2,3},{3,2},{4,5},{5,4},{6,7},{7,6},{8,9},{9,8},{10,11... | collective-permute-start | bytes 688136 | tf_op jit(solution)/shard_map/ppermute | solution.py:288
  482.6 14.4 %collective-permute-start.40 = (bf16[14,32,128]{2,1,0:T(8,128)(2,1)}, bf16[14,32,128]{2,1,0:T(8,128)(2,1)S(1)}, u32[]{:S(2)}, u32[]{:S(2)}) collective-permute-start(bf16[14,32,128]{2,1,0:T(8,128)(2,1)} %get-tuple-element.164), channel_id=1, source_target_pairs={{0,2},{1,3},{2,0},{3,1},{4,6},{5,7},{6,4},{7,5},{8,10},{9,11},{10,... | collective-permute-start | bytes 344072 | tf_op jit(solution)/shard_map/ppermute | solution.py:288
  489.3 7.7 %collective-permute-start.41 = (bf16[14,32,128]{2,1,0:T(8,128)(2,1)}, bf16[14,32,128]{2,1,0:T(8,128)(2,1)S(1)}, u32[]{:S(2)}, u32[]{:S(2)}) collective-permute-start(bf16[14,32,128]{2,1,0:T(8,128)(2,1)} %get-tuple-element.165), channel_id=1, source_target_pairs={{0,1},{1,0},{2,3},{3,2},{4,5},{5,4},{6,7},{7,6},{8,9},{9,8},{10,11... | collective-permute-start | bytes 344072 | tf_op jit(solution)/shard_map/ppermute | solution.py:288
  (28 other events, 528.2 us)

commit v4 on v3

--- a/solution.py
+++ b/solution.py
@@ -210,22 +210,18 @@
 
 
 def dedisperse_kernel(shards, columns, sizes, scale, place, cosine, sine, *rest):
-    out, upper, lower, woven = rest[-4:]
+    out, held, woven = rest[-3:]
     f = pl.program_id(0)
     for c, (column, size) in enumerate(zip(columns, sizes)):
         for part, m in zip(rest[c * shards : (c + 1) * shards], slots(shards)):
             at = pl.ds(pl.multiple_of(column + (place[0] ^ m) * size, ROWS), size)
-            real, imag = part[f], part[f + MODF]
-            upper[at, :LANES] = real
-            upper[at, LANES:] = imag
-            lower[at, :LANES] = imag
-            lower[at, LANES:] = -real
-    value = jnp.dot(cosine[0], upper[...], preferred_element_type=jnp.float32) + jnp.dot(
-        sine[0], lower[...], preferred_element_type=jnp.float32
-    )
-    rows = value.shape[0]
-    woven[pl.ds(0, rows, stride=2), :] = value[:, :LANES] * scale
-    woven[pl.ds(1, rows, stride=2), :] = value[:, LANES:] * scale
+            held[at, :LANES] = part[f]
+            held[at, LANES:] = part[f + MODF]
+    by_cosine = jnp.dot(cosine[0], held[...], preferred_element_type=jnp.float32)
+    by_sine = jnp.dot(sine[0], held[...], preferred_element_type=jnp.float32)
+    rows = by_cosine.shape[0]
+    woven[pl.ds(0, rows, stride=2), :] = (by_cosine[:, :LANES] + by_sine[:, LANES:]) * scale
+    woven[pl.ds(1, rows, stride=2), :] = (by_cosine[:, LANES:] - by_sine[:, :LANES]) * scale
     out[0] = woven[...].astype(out.dtype)
 
 
@@ -243,7 +239,7 @@
             in_specs=[pl.BlockSpec((1, rows, depth), each)] * 2
             + [pl.BlockSpec((2 * MODF, size, LANES), lambda f, _: (0, 0, 0)) for size in sizes for _ in range(shards)],
             out_specs=pl.BlockSpec((1,) + made, each),
-            scratch_shapes=[pltpu.VMEM((depth, 2 * LANES), jnp.bfloat16)] * 2 + [pltpu.VMEM(made, jnp.float32)],
+            scratch_shapes=[pltpu.VMEM((depth, 2 * LANES), jnp.bfloat16), pltpu.VMEM(made, jnp.float32)],
         ),
         out_shape=jax.ShapeDtypeStruct((MODF,) + made, jnp.bfloat16),
         compiler_params=pltpu.CompilerParams(vmem_limit_bytes=60 << 20),

time: 511 us -> 511 us (level)
  no operation moved by 1% of the time
where the time goes in v4:
time: 511 us; the launch traced here: 510 us
  waiting for transfers between devices  165 us (32%)
  Pallas kernels  149 us (29%)
  starting transfers between devices  112 us (22%)
  other arithmetic  45.4 us (9%)
  blocking collectives  27.5 us (5%)
  local copies, waits for them, and re-layouts  10.4 us (2%)
    ppermute x42, waiting for transfers between devices, exchange(): lax.ppermute(part, 'shard', [(j, j ^ m) for j in range(shards)])  165 us
    ppermute x42, starting transfers between devices, exchange(): lax.ppermute(part, 'shard', [(j, j ^ m) for j in range(shards)])  112 us
    pallas_call x3, Pallas kernels, form_beams(): pl.pallas_call(functools.partial(beam_kernel, shards, frames), grid_spec=...  67.1 us
    pallas_call x3, Pallas kernels, channelize(): pl.pallas_call(functools.partial(channelize_kernel, shards, size, frames,...  56.9 us
    all_gather x3, blocking collectives, pipelined(): levels = lax.all_gather(level, 'section')  27.5 us
    convert_element_type x1, other arithmetic, phase_tables(): sine = cosine_of(turn - frames // 4, frames).astype(jnp.bfloat16)  23.8 us
    convert_element_type x1, other arithmetic, beam_table(): return cosine_of(turn, GRID_Y).astype(jnp.bfloat16)  18.6 us
    pallas_call x5, Pallas kernels, normalise(): pl.pallas_call(functools.partial(normalise_kernel, levels.shape[0], len(s...  12.9 us
  transfers between devices with their start and end apart: 42, of which 13 were waited for; matrix products, arithmetic and copies ran while one was open for 10% of the time, Pallas kernels for 23%

profile of v4, /device:TPU:0, one launch (start us, length us, event | category | flops | bytes accessed | tf_op | source)
XLA Modules:
  0.0 510.0 jit_solution(14534191117489940842)
XLA Ops:
  0.0 15.5 %channelize.3 = (bf16[2,2,16,32,128]{4,3,2,1,0:T(8,128)(2,1)}, bf16[2,2,16,32,128]{4,3,2,1,0:T(8,128)(2,1)}, bf16[2,2,16,32,128]{4,3,2,1,0:T(8,128)(2,1)}, bf16[...) custom-call(s32[1]{0:T(128)} %bitcast.place, ...), custom_call_target="tpu_custom_call" | custom-call | flops 1000 | bytes 1000 | tf_op jit(solution)/shard_map/channelize/pallas_call | solution.py:104
  15.5 4.1 collective-permute-start
  19.6 3.1 collective-permute-start.2
  23.3 25.9 %channelize.4 = (bf16[2,2,16,64,128]{4,3,2,1,0:T(8,128)(2,1)}, bf16[2,2,16,64,128]{4,3,2,1,0:T(8,128)(2,1)}, bf16[2,2,16,64,128]{4,3,2,1,0:T(8,128)(2,1)}, bf16[...) custom-call(s32[1]{0:T(128)} %bitcast.place, ...), custom_call_target="tpu_custom_call" | custom-call | flops 1000 | bytes 1000 | tf_op jit(solution)/shard_map/channelize/pallas_call | solution.py:104
  51.2 26.4 %collective-permute-done.rest_0_ = bf16[2,2,16,32,128]{4,3,2,1,0:T(8,128)(2,1)} collective-permute-done((bf16[2,2,16,32,128]{4,3,2,1,0:T(8,128)(2,1)}, bf16[2,2,16,32,128]{4,3,2,1,0:T(8,128)(2,1)}, u32[]{:S(2)}, u32[]{:S(2)}) %collective-permute-start) | collective-permute-done | bytes 524320 | tf_op jit(solution)/shard_map/ppermute | solution.py:284
  77.6 9.7 %collective-permute-done.1.rest_1_ = bf16[2,2,16,32,128]{4,3,2,1,0:T(8,128)(2,1)} collective-permute-done((bf16[2,2,16,32,128]{4,3,2,1,0:T(8,128)(2,1)}, bf16[2,2,16,32,128]{4,3,2,1,0:T(8,128)(2,1)}, u32[]{:S(2)}, u32[]{:S(2)}) %collective-permute-start.1) | collective-permute-done | bytes 524320 | tf_op jit(solution)/shard_map/ppermute | solution.py:284
  88.7 18.6 %multiply_convert_fusion.table = bf16[2048,2048]{1,0:T(8,128)(2,1)} fusion(s32[2048]{0:T(1024)S(1)} %get-tuple-element.175, s32[2048]{0:T(1024)S(1)} %get-tuple-element.176, s32[2048]{0:T(1024)S(1)} %get-tuple-element.177, s32[2048]{0:T(1024)S(1)} %get-tuple-element.172, s32[2048]{0:T(1024)S(1)} %get-tuple-element.178, s32[2048]{0:T(1024)S(1)} %get-tuple-element.171), kind=kLoop, calls=%fused_computation.2 | loop fusion | flops 117440512 | bytes 8437760 | tf_op jit(solution)/shard_map/convert_element_type | solution.py:53
  108.9 37.6 %collective-permute-start.15 = (bf16[2,2,16,64,128]{4,3,2,1,0:T(8,128)(2,1)}, bf16[2,2,16,64,128]{4,3,2,1,0:T(8,128)(2,1)}, u32[]{:S(2)}, u32[]{:S(2)}) collective-permute-start(bf16[2,2,16,64,128]{4,3,2,1,0:T(8,128)(2,1)} %get-tuple-element.111), channel_id=1, source_target_pairs={{0,5},{1,4},{2,7},{3,6},{4,1},{5,0},{6,3},{7,2},{8,13},{9,12},{10,... | collective-permute-start | bytes 3145736 | tf_op jit(solution)/shard_map/ppermute | solution.py:284
  146.5 18.0 %form_beams.3 = (f32[14,32,128]{2,1,0:T(8,128)}, f32[14,32,128]{2,1,0:T(8,128)}, f32[14,32,128]{2,1,0:T(8,128)}, f32[14,32,128]{2,1,0:T(8,128)}, f32[14,32,128]{...) custom-call(s32[1]{0:T(128)} %bitcast.place, ...), custom_call_target="tpu_custom_call" | custom-call | flops 1000 | bytes 1000 | tf_op jit(solution)/shard_map/form_beams/pallas_call | solution.py:157
  164.5 8.6 %all-gather = f32[128,128]{1,0:T(8,128)} all-gather(f32[32,128]{1,0:T(8,128)} %get-tuple-element.96), channel_id=2, replica_groups=mesh['section'=4,'shard'=8] {'section'}, dimensions={0}, use_global_device_ids=true | all-gather | bytes 81920 | tf_op jit(solution)/shard_map/all_gather | solution.py:314
  173.2 2.3 normalise.5
  179.3 1.9 copy.18
  181.2 23.8 %fusion.39 = (bf16[7,512,1024]{2,1,0:T(8,128)(2,1)}, bf16[7,512,1024]{2,1,0:T(8,128)(2,1)}) fusion(s32[512,1024]{1,0:T(8,128)S(1)} %copy.18, s32[7]{0:T(128)S(1)} %iota_add_fusion), kind=kLoop, calls=%fused_computation.42 | loop fusion | flops 157810688 | bytes 16777244 | tf_op jit(solution)/shard_map/convert_element_type | solution.py:254
  205.0 15.5 %channelize.5 = (bf16[2,2,16,32,128]{4,3,2,1,0:T(8,128)(2,1)}, bf16[2,2,16,32,128]{4,3,2,1,0:T(8,128)(2,1)}, bf16[2,2,16,32,128]{4,3,2,1,0:T(8,128)(2,1)}, bf16[...) custom-call(s32[1]{0:T(128)} %bitcast.place, ...), custom_call_target="tpu_custom_call" | custom-call | flops 1000 | bytes 1000 | tf_op jit(solution)/shard_map/channelize/pallas_call | solution.py:104
  220.7 2.9 collective-permute-start.21
  223.5 28.8 %collective-permute-done.21.rest_9_.rest_16_ = bf16[14,32,128]{2,1,0:T(8,128)(2,1)S(1)} collective-permute-done((bf16[14,32,128]{2,1,0:T(8,128)(2,1)S(1)}, bf16[14,32,128]{2,1,0:T(8,128)(2,1)S(1)}, u32[]{:S(2)}, u32[]{:S(2)}) %collective-permute-start.21) | collective-permute-done | bytes 114720 | tf_op jit(solution)/shard_map/ppermute | solution.py:284
  252.4 7.2 %collective-permute-done.22.rest_10_.rest_17_ = bf16[14,32,128]{2,1,0:T(8,128)(2,1)S(1)} collective-permute-done((bf16[14,32,128]{2,1,0:T(8,128)(2,1)S(1)}, bf16[14,32,128]{2,1,0:T(8,128)(2,1)S(1)}, u32[]{:S(2)}, u32[]{:S(2)}) %collective-permute-start.22) | collective-permute-done | bytes 114720 | tf_op jit(solution)/shard_map/ppermute | solution.py:284
  259.6 2.0 collective-permute-start.23
  261.6 5.0 collective-permute-done.23.rest_11_.rest_18_
  267.4 5.8 %collective-permute-done.24.rest_12_.rest_19_ = bf16[14,32,128]{2,1,0:T(8,128)(2,1)S(1)} collective-permute-done((bf16[14,32,128]{2,1,0:T(8,128)(2,1)S(1)}, bf16[14,32,128]{2,1,0:T(8,128)(2,1)S(1)}, u32[]{:S(2)}, u32[]{:S(2)}) %collective-permute-start.24) | collective-permute-done | bytes 114720 | tf_op jit(solution)/shard_map/ppermute | solution.py:284
  273.3 2.1 collective-permute-start.16
  276.7 3.0 collective-permute-start.19
  279.7 21.9 %collective-permute-done.16.rest_2_ = bf16[2,2,16,64,128]{4,3,2,1,0:T(8,128)(2,1)S(1)} collective-permute-done((bf16[2,2,16,64,128]{4,3,2,1,0:T(8,128)(2,1)}, bf16[2,2,16,64,128]{4,3,2,1,0:T(8,128)(2,1)S(1)}, u32[]{:S(2)}, u32[]{:S(2)}) %collective-permute-start.16) | collective-permute-done | bytes 1048608 | tf_op jit(solution)/shard_map/ppermute | solution.py:284
  301.5 2.1 collective-permute-start.9
  303.6 18.2 %collective-permute-done.17.rest_3_ = bf16[2,2,16,64,128]{4,3,2,1,0:T(8,128)(2,1)S(1)} collective-permute-done((bf16[2,2,16,64,128]{4,3,2,1,0:T(8,128)(2,1)}, bf16[2,2,16,64,128]{4,3,2,1,0:T(8,128)(2,1)S(1)}, u32[]{:S(2)}, u32[]{:S(2)}) %collective-permute-start.17) | collective-permute-done | bytes 1048608 | tf_op jit(solution)/shard_map/ppermute | solution.py:284
  321.8 3.6 collective-permute-start.10
  325.4 19.4 %collective-permute-done.18.rest_4_ = bf16[2,2,16,64,128]{4,3,2,1,0:T(8,128)(2,1)} collective-permute-done((bf16[2,2,16,64,128]{4,3,2,1,0:T(8,128)(2,1)}, bf16[2,2,16,64,128]{4,3,2,1,0:T(8,128)(2,1)}, u32[]{:S(2)}, u32[]{:S(2)}) %collective-permute-start.18) | collective-permute-done | bytes 1048608 | tf_op jit(solution)/shard_map/ppermute | solution.py:284
  344.8 19.7 %collective-permute-start.11 = (bf16[2,2,16,32,128]{4,3,2,1,0:T(8,128)(2,1)}, bf16[2,2,16,32,128]{4,3,2,1,0:T(8,128)(2,1)}, u32[]{:S(2)}, u32[]{:S(2)}) collective-permute-start(bf16[2,2,16,32,128]{4,3,2,1,0:T(8,128)(2,1)} %get-tuple-element.106), channel_id=1, source_target_pairs={{0,3},{1,2},{2,1},{3,0},{4,7},{5,6},{6,5},{7,4},{8,11},{9,10},{10,... | collective-permute-start | bytes 1572872 | tf_op jit(solution)/shard_map/ppermute | solution.py:284
  364.5 4.6 collective-permute-done.19.rest_5_
  370.1 31.0 %form_beams.4 = (f32[14,64,128]{2,1,0:T(8,128)}, f32[14,64,128]{2,1,0:T(8,128)}, f32[14,64,128]{2,1,0:T(8,128)}, f32[14,64,128]{2,1,0:T(8,128)}, f32[14,64,128]{...) custom-call(s32[1]{0:T(128)} %bitcast.place, ...), custom_call_target="tpu_custom_call" | custom-call | flops 1000 | bytes 1000 | tf_op jit(solution)/shard_map/form_beams/pallas_call | solution.py:157
  401.0 10.2 %all-gather.1 = f32[256,128]{1,0:T(8,128)} all-gather(f32[64,128]{1,0:T(8,128)} %get-tuple-element.123), channel_id=3, replica_groups=mesh['section'=4,'shard'=8] {'section'}, dimensions={0}, use_global_device_ids=true | all-gather | bytes 163840 | tf_op jit(solution)/shard_map/all_gather | solution.py:314
  411.3 2.8 normalise.6
  414.1 2.5 collective-permute-start.25
  418.2 2.1 collective-permute-start.28
  421.0 18.1 %form_beams.5 = (f32[14,32,128]{2,1,0:T(8,128)}, f32[14,32,128]{2,1,0:T(8,128)}, f32[14,32,128]{2,1,0:T(8,128)}, f32[14,32,128]{2,1,0:T(8,128)}, f32[14,32,128]{...) custom-call(s32[1]{0:T(128)} %bitcast.place, ...), custom_call_target="tpu_custom_call" | custom-call | flops 1000 | bytes 1000 | tf_op jit(solution)/shard_map/form_beams/pallas_call | solution.py:157
  439.1 8.6 %all-gather.2 = f32[128,128]{1,0:T(8,128)} all-gather(f32[32,128]{1,0:T(8,128)} %get-tuple-element.129), channel_id=4, replica_groups=mesh['section'=4,'shard'=8] {'section'}, dimensions={0}, use_global_device_ids=true | all-gather | bytes 81920 | tf_op jit(solution)/shard_map/all_gather | solution.py:314
  448.8 2.7 normalise.7
  451.5 8.0 %collective-permute-start.29 = (bf16[14,32,128]{2,1,0:T(8,128)(2,1)}, bf16[14,32,128]{2,1,0:T(8,128)(2,1)S(1)}, u32[]{:S(2)}, u32[]{:S(2)}) collective-permute-start(bf16[14,32,128]{2,1,0:T(8,128)(2,1)} %get-tuple-element.142), channel_id=1, source_target_pairs={{0,4},{1,5},{2,6},{3,7},{4,0},{5,1},{6,2},{7,3},{8,12},{9,13},{10,... | collective-permute-start | bytes 344072 | tf_op jit(solution)/shard_map/ppermute | solution.py:284
  460.5 1.9 collective-permute-start.31
  464.3 1.9 collective-permute-start.34
  466.2 2.8 normalise.8
  469.0 2.3 normalise.9
  471.3 5.1 collective-permute-done.30.rest_1_
  476.4 2.6 collective-permute-start.35
  481.0 1.6 collective-permute-start.37
  483.4 5.9 %collective-permute-done.39.rest_20_ = bf16[14,32,128]{2,1,0:T(8,128)(2,1)S(1)} collective-permute-done((bf16[14,32,128]{2,1,0:T(8,128)(2,1)}, bf16[14,32,128]{2,1,0:T(8,128)(2,1)S(1)}, u32[]{:S(2)}, u32[]{:S(2)}) %collective-permute-start.39) | collective-permute-done | bytes 114720 | tf_op jit(solution)/shard_map/ppermute | solution.py:284
  489.7 7.3 %collective-permute-done.40.rest_21_ = bf16[14,32,128]{2,1,0:T(8,128)(2,1)S(1)} collective-permute-done((bf16[14,32,128]{2,1,0:T(8,128)(2,1)}, bf16[14,32,128]{2,1,0:T(8,128)(2,1)S(1)}, u32[]{:S(2)}, u32[]{:S(2)}) %collective-permute-start.40) | collective-permute-done | bytes 114720 | tf_op jit(solution)/shard_map/ppermute | solution.py:284
  497.9 11.9 %dedisperse.1 = bf16[7,1024,128]{2,1,0:T(8,128)(2,1)} custom-call(s32[1]{0:T(128)} %bitcast.place, bf16[7,512,1024]{2,1,0:T(8,128)(2,1)} %get-tuple-element.168.rest_0_.cosine, bf16[7,512,1024]{2,1,0:T(8,128)(2,1)} %get-tuple-element.167.sine, bf16[14,32,128]{2,1,0:T(8,128)(2,1)} %copy-done.18, bf16[14,32,128]{2,1,0:T(8,128)(2,1)} %copy-done.19, ...), custom_call_target="tpu_custom_call" | custom-call | flops 1000 | bytes 1000 | tf_op jit(solution)/shard_map/dedisperse/pallas_call | solution.py:234
  (138 shorter events, 22.8 us)
Async XLA Ops:
  15.5 62.1 %collective-permute-start = (bf16[2,2,16,32,128]{4,3,2,1,0:T(8,128)(2,1)}, bf16[2,2,16,32,128]{4,3,2,1,0:T(8,128)(2,1)}, u32[]{:S(2)}, u32[]{:S(2)}) collective-permute-start(bf16[2,2,16,32,128]{4,3,2,1,0:T(8,128)(2,1)} %get-tuple-element.88), channel_id=1, source_target_pairs={{0,4},{1,5},{2,6},{3,7},{4,0},{5,1},{6,2},{7,3},{8,12},{9,13},{10,... | collective-permute-start | bytes 1572872 | tf_op jit(solution)/shard_map/ppermute | solution.py:284
  19.6 67.7 %collective-permute-start.1 = (bf16[2,2,16,32,128]{4,3,2,1,0:T(8,128)(2,1)}, bf16[2,2,16,32,128]{4,3,2,1,0:T(8,128)(2,1)}, u32[]{:S(2)}, u32[]{:S(2)}) collective-permute-start(bf16[2,2,16,32,128]{4,3,2,1,0:T(8,128)(2,1)} %get-tuple-element.89), channel_id=1, source_target_pairs={{0,5},{1,4},{2,7},{3,6},{4,1},{5,0},{6,3},{7,2},{8,13},{9,12},{10,... | collective-permute-start | bytes 1572872 | tf_op jit(solution)/shard_map/ppermute | solution.py:284
  19.6 88.5 %collective-permute-start.2 = (bf16[2,2,16,32,128]{4,3,2,1,0:T(8,128)(2,1)}, bf16[2,2,16,32,128]{4,3,2,1,0:T(8,128)(2,1)S(1)}, u32[]{:S(2)}, u32[]{:S(2)}) collective-permute-start(bf16[2,2,16,32,128]{4,3,2,1,0:T(8,128)(2,1)} %get-tuple-element.90), channel_id=1, source_target_pairs={{0,6},{1,7},{2,4},{3,5},{4,2},{5,3},{6,0},{7,1},{8,14},{9,15},{10,... | collective-permute-start | bytes 1572872 | tf_op jit(solution)/shard_map/ppermute | solution.py:284
  22.7 86.2 %collective-permute-start.3 = (bf16[2,2,16,32,128]{4,3,2,1,0:T(8,128)(2,1)}, bf16[2,2,16,32,128]{4,3,2,1,0:T(8,128)(2,1)}, u32[]{:S(2)}, u32[]{:S(2)}) collective-permute-start(bf16[2,2,16,32,128]{4,3,2,1,0:T(8,128)(2,1)} %get-tuple-element.91), channel_id=1, source_target_pairs={{0,7},{1,6},{2,5},{3,4},{4,3},{5,2},{6,1},{7,0},{8,15},{9,14},{10,... | collective-permute-start | bytes 1572872 | tf_op jit(solution)/shard_map/ppermute | solution.py:284
  23.3 123.2 %collective-permute-start.4 = (bf16[2,2,16,32,128]{4,3,2,1,0:T(8,128)(2,1)}, bf16[2,2,16,32,128]{4,3,2,1,0:T(8,128)(2,1)}, u32[]{:S(2)}, u32[]{:S(2)}) collective-permute-start(bf16[2,2,16,32,128]{4,3,2,1,0:T(8,128)(2,1)} %get-tuple-element.92), channel_id=1, source_target_pairs={{0,3},{1,2},{2,1},{3,0},{4,7},{5,6},{6,5},{7,4},{8,11},{9,10},{10,... | collective-permute-start | bytes 1572872 | tf_op jit(solution)/shard_map/ppermute | solution.py:284
  23.3 84.0 %copy-start.29 = (f32[128]{0:T(128)S(1)}, f32[128]{0:T(128)}, u32[]{:S(2)}) copy-start(f32[128]{0:T(128)} %param.11) | copy-start | bytes 1540
  49.2 127.5 %copy-start = (s32[1024,512]{1,0:T(8,128)S(1)}, s32[1024,512]{1,0:T(8,128)}, u32[]{:S(2)}) copy-start(s32[1024,512]{1,0:T(8,128)} %param.12) | copy-start | bytes 6291460
  77.6 68.9 %collective-permute-start.5 = (bf16[2,2,16,32,128]{4,3,2,1,0:T(8,128)(2,1)}, bf16[2,2,16,32,128]{4,3,2,1,0:T(8,128)(2,1)}, u32[]{:S(2)}, u32[]{:S(2)}) collective-permute-start(bf16[2,2,16,32,128]{4,3,2,1,0:T(8,128)(2,1)} %get-tuple-element.93), channel_id=1, source_target_pairs={{0,2},{1,3},{2,0},{3,1},{4,6},{5,7},{6,4},{7,5},{8,10},{9,11},{10,... | collective-permute-start | bytes 1572872 | tf_op jit(solution)/shard_map/ppermute | solution.py:284
  87.3 59.2 %collective-permute-start.6 = (bf16[2,2,16,32,128]{4,3,2,1,0:T(8,128)(2,1)}, bf16[2,2,16,32,128]{4,3,2,1,0:T(8,128)(2,1)}, u32[]{:S(2)}, u32[]{:S(2)}) collective-permute-start(bf16[2,2,16,32,128]{4,3,2,1,0:T(8,128)(2,1)} %get-tuple-element.94), channel_id=1, source_target_pairs={{0,1},{1,0},{2,3},{3,2},{4,5},{5,4},{6,7},{7,6},{8,9},{9,8},{10,11... | collective-permute-start | bytes 1572872 | tf_op jit(solution)/shard_map/ppermute | solution.py:284
  108.9 167.7 %collective-permute-start.14 = (bf16[2,2,16,64,128]{4,3,2,1,0:T(8,128)(2,1)}, bf16[2,2,16,64,128]{4,3,2,1,0:T(8,128)(2,1)S(1)}, u32[]{:S(2)}, u32[]{:S(2)}) collective-permute-start(bf16[2,2,16,64,128]{4,3,2,1,0:T(8,128)(2,1)} %get-tuple-element.110), channel_id=1, source_target_pairs={{0,4},{1,5},{2,6},{3,7},{4,0},{5,1},{6,2},{7,3},{8,12},{9,13},{10,... | collective-permute-start | bytes 3145736 | tf_op jit(solution)/shard_map/ppermute | solution.py:284
  108.9 170.8 %collective-permute-start.15 = (bf16[2,2,16,64,128]{4,3,2,1,0:T(8,128)(2,1)}, bf16[2,2,16,64,128]{4,3,2,1,0:T(8,128)(2,1)}, u32[]{:S(2)}, u32[]{:S(2)}) collective-permute-start(bf16[2,2,16,64,128]{4,3,2,1,0:T(8,128)(2,1)} %get-tuple-element.111), channel_id=1, source_target_pairs={{0,5},{1,4},{2,7},{3,6},{4,1},{5,0},{6,3},{7,2},{8,13},{9,12},{10,... | collective-permute-start | bytes 3145736 | tf_op jit(solution)/shard_map/ppermute | solution.py:284
  220.5 54.9 %collective-permute-start.7 = (bf16[2,2,16,32,128]{4,3,2,1,0:T(8,128)(2,1)}, bf16[2,2,16,32,128]{4,3,2,1,0:T(8,128)(2,1)S(1)}, u32[]{:S(2)}, u32[]{:S(2)}) collective-permute-start(bf16[2,2,16,32,128]{4,3,2,1,0:T(8,128)(2,1)} %get-tuple-element.102), channel_id=1, source_target_pairs={{0,4},{1,5},{2,6},{3,7},{4,0},{5,1},{6,2},{7,3},{8,12},{9,13},{10,... | collective-permute-start | bytes 1572872 | tf_op jit(solution)/shard_map/ppermute | solution.py:284
  220.6 56.1 %collective-permute-start.8 = (bf16[2,2,16,32,128]{4,3,2,1,0:T(8,128)(2,1)}, bf16[2,2,16,32,128]{4,3,2,1,0:T(8,128)(2,1)S(1)}, u32[]{:S(2)}, u32[]{:S(2)}) collective-permute-start(bf16[2,2,16,32,128]{4,3,2,1,0:T(8,128)(2,1)} %get-tuple-element.103), channel_id=1, source_target_pairs={{0,5},{1,4},{2,7},{3,6},{4,1},{5,0},{6,3},{7,2},{8,13},{9,12},{10,... | collective-permute-start | bytes 1572872 | tf_op jit(solution)/shard_map/ppermute | solution.py:284
  220.7 31.7 %collective-permute-start.21 = (bf16[14,32,128]{2,1,0:T(8,128)(2,1)S(1)}, bf16[14,32,128]{2,1,0:T(8,128)(2,1)S(1)}, u32[]{:S(2)}, u32[]{:S(2)}) collective-permute-start(bf16[14,32,128]{2,1,0:T(8,128)(2,1)S(1)} %copy-done.33), channel_id=1, source_target_pairs={{0,4},{1,5},{2,6},{3,7},{4,0},{5,1},{6,2},{7,3},{8,12},{9,13},{10,... | collective-permute-start | bytes 344072 | tf_op jit(solution)/shard_map/ppermute | solution.py:284
  252.4 117.7 %copy-start.11 = (bf16[14,32,128]{2,1,0:T(8,128)(2,1)}, bf16[14,32,128]{2,1,0:T(8,128)(2,1)S(1)}, u32[]{:S(2)}) copy-start(bf16[14,32,128]{2,1,0:T(8,128)(2,1)S(1)} %collective-permute-done.21.rest_9_.rest_16_) | copy-start | bytes 344068
  252.4 7.2 %collective-permute-start.22 = (bf16[14,32,128]{2,1,0:T(8,128)(2,1)S(1)}, bf16[14,32,128]{2,1,0:T(8,128)(2,1)S(1)}, u32[]{:S(2)}, u32[]{:S(2)}) collective-permute-start(bf16[14,32,128]{2,1,0:T(8,128)(2,1)S(1)} %copy-done.32), channel_id=1, source_target_pairs={{0,5},{1,4},{2,7},{3,6},{4,1},{5,0},{6,3},{7,2},{8,13},{9,12},{10,... | collective-permute-start | bytes 344072 | tf_op jit(solution)/shard_map/ppermute | solution.py:284
  259.6 110.4 %copy-start.12 = (bf16[14,32,128]{2,1,0:T(8,128)(2,1)}, bf16[14,32,128]{2,1,0:T(8,128)(2,1)S(1)}, u32[]{:S(2)}) copy-start(bf16[14,32,128]{2,1,0:T(8,128)(2,1)S(1)} %collective-permute-done.22.rest_10_.rest_17_) | copy-start | bytes 344068
  259.6 7.0 %collective-permute-start.23 = (bf16[14,32,128]{2,1,0:T(8,128)(2,1)S(1)}, bf16[14,32,128]{2,1,0:T(8,128)(2,1)S(1)}, u32[]{:S(2)}, u32[]{:S(2)}) collective-permute-start(bf16[14,32,128]{2,1,0:T(8,128)(2,1)S(1)} %copy-done.31), channel_id=1, source_target_pairs={{0,6},{1,7},{2,4},{3,5},{4,2},{5,3},{6,0},{7,1},{8,14},{9,15},{10,... | collective-permute-start | bytes 344072 | tf_op jit(solution)/shard_map/ppermute | solution.py:284
  266.6 103.5 %copy-start.13 = (bf16[14,32,128]{2,1,0:T(8,128)(2,1)}, bf16[14,32,128]{2,1,0:T(8,128)(2,1)S(1)}, u32[]{:S(2)}) copy-start(bf16[14,32,128]{2,1,0:T(8,128)(2,1)S(1)} %collective-permute-done.23.rest_11_.rest_18_) | copy-start | bytes 344068
  266.6 6.7 %collective-permute-start.24 = (bf16[14,32,128]{2,1,0:T(8,128)(2,1)S(1)}, bf16[14,32,128]{2,1,0:T(8,128)(2,1)S(1)}, u32[]{:S(2)}, u32[]{:S(2)}) collective-permute-start(bf16[14,32,128]{2,1,0:T(8,128)(2,1)S(1)} %copy-done.30), channel_id=1, source_target_pairs={{0,7},{1,6},{2,5},{3,4},{4,3},{5,2},{6,1},{7,0},{8,15},{9,14},{10,... | collective-permute-start | bytes 344072 | tf_op jit(solution)/shard_map/ppermute | solution.py:284
  273.3 28.3 %collective-permute-start.16 = (bf16[2,2,16,64,128]{4,3,2,1,0:T(8,128)(2,1)}, bf16[2,2,16,64,128]{4,3,2,1,0:T(8,128)(2,1)S(1)}, u32[]{:S(2)}, u32[]{:S(2)}) collective-permute-start(bf16[2,2,16,64,128]{4,3,2,1,0:T(8,128)(2,1)} %get-tuple-element.112), channel_id=1, source_target_pairs={{0,6},{1,7},{2,4},{3,5},{4,2},{5,3},{6,0},{7,1},{8,14},{9,15},{10,... | collective-permute-start | bytes 3145736 | tf_op jit(solution)/shard_map/ppermute | solution.py:284
  276.2 45.6 %collective-permute-start.17 = (bf16[2,2,16,64,128]{4,3,2,1,0:T(8,128)(2,1)}, bf16[2,2,16,64,128]{4,3,2,1,0:T(8,128)(2,1)S(1)}, u32[]{:S(2)}, u32[]{:S(2)}) collective-permute-start(bf16[2,2,16,64,128]{4,3,2,1,0:T(8,128)(2,1)} %get-tuple-element.113), channel_id=1, source_target_pairs={{0,7},{1,6},{2,5},{3,4},{4,3},{5,2},{6,1},{7,0},{8,15},{9,14},{10,... | collective-permute-start | bytes 3145736 | tf_op jit(solution)/shard_map/ppermute | solution.py:284
  276.6 68.2 %collective-permute-start.18 = (bf16[2,2,16,64,128]{4,3,2,1,0:T(8,128)(2,1)}, bf16[2,2,16,64,128]{4,3,2,1,0:T(8,128)(2,1)}, u32[]{:S(2)}, u32[]{:S(2)}) collective-permute-start(bf16[2,2,16,64,128]{4,3,2,1,0:T(8,128)(2,1)} %get-tuple-element.114), channel_id=1, source_target_pairs={{0,3},{1,2},{2,1},{3,0},{4,7},{5,6},{6,5},{7,4},{8,11},{9,10},{10,... | collective-permute-start | bytes 3145736 | tf_op jit(solution)/shard_map/ppermute | solution.py:284
  276.7 93.4 %copy-start.1 = (bf16[2,2,16,64,128]{4,3,2,1,0:T(8,128)(2,1)}, bf16[2,2,16,64,128]{4,3,2,1,0:T(8,128)(2,1)S(1)}, u32[]{:S(2)}) copy-start(bf16[2,2,16,64,128]{4,3,2,1,0:T(8,128)(2,1)S(1)} %collective-permute-done.14.rest_0_) | copy-start | bytes 3145732
  276.7 92.4 %collective-permute-start.19 = (bf16[2,2,16,64,128]{4,3,2,1,0:T(8,128)(2,1)}, bf16[2,2,16,64,128]{4,3,2,1,0:T(8,128)(2,1)}, u32[]{:S(2)}, u32[]{:S(2)}) collective-permute-start(bf16[2,2,16,64,128]{4,3,2,1,0:T(8,128)(2,1)} %get-tuple-element.115), channel_id=1, source_target_pairs={{0,2},{1,3},{2,0},{3,1},{4,6},{5,7},{6,4},{7,5},{8,10},{9,11},{10,... | collective-permute-start | bytes 3145736 | tf_op jit(solution)/shard_map/ppermute | solution.py:284
  279.7 89.6 %collective-permute-start.20 = (bf16[2,2,16,64,128]{4,3,2,1,0:T(8,128)(2,1)}, bf16[2,2,16,64,128]{4,3,2,1,0:T(8,128)(2,1)}, u32[]{:S(2)}, u32[]{:S(2)}) collective-permute-start(bf16[2,2,16,64,128]{4,3,2,1,0:T(8,128)(2,1)} %get-tuple-element.116), channel_id=1, source_target_pairs={{0,1},{1,0},{2,3},{3,2},{4,5},{5,4},{6,7},{7,6},{8,9},{9,8},{10,11... | collective-permute-start | bytes 3145736 | tf_op jit(solution)/shard_map/ppermute | solution.py:284
  301.5 112.6 %collective-permute-start.9 = (bf16[2,2,16,32,128]{4,3,2,1,0:T(8,128)(2,1)}, bf16[2,2,16,32,128]{4,3,2,1,0:T(8,128)(2,1)}, u32[]{:S(2)}, u32[]{:S(2)}) collective-permute-start(bf16[2,2,16,32,128]{4,3,2,1,0:T(8,128)(2,1)} %get-tuple-element.104), channel_id=1, source_target_pairs={{0,6},{1,7},{2,4},{3,5},{4,2},{5,3},{6,0},{7,1},{8,14},{9,15},{10,... | collective-permute-start | bytes 1572872 | tf_op jit(solution)/shard_map/ppermute | solution.py:284
  321.8 94.8 %collective-permute-start.10 = (bf16[2,2,16,32,128]{4,3,2,1,0:T(8,128)(2,1)}, bf16[2,2,16,32,128]{4,3,2,1,0:T(8,128)(2,1)}, u32[]{:S(2)}, u32[]{:S(2)}) collective-permute-start(bf16[2,2,16,32,128]{4,3,2,1,0:T(8,128)(2,1)} %get-tuple-element.105), channel_id=1, source_target_pairs={{0,7},{1,6},{2,5},{3,4},{4,3},{5,2},{6,1},{7,0},{8,15},{9,14},{10,... | collective-permute-start | bytes 1572872 | tf_op jit(solution)/shard_map/ppermute | solution.py:284
  344.8 71.8 %collective-permute-start.11 = (bf16[2,2,16,32,128]{4,3,2,1,0:T(8,128)(2,1)}, bf16[2,2,16,32,128]{4,3,2,1,0:T(8,128)(2,1)}, u32[]{:S(2)}, u32[]{:S(2)}) collective-permute-start(bf16[2,2,16,32,128]{4,3,2,1,0:T(8,128)(2,1)} %get-tuple-element.106), channel_id=1, source_target_pairs={{0,3},{1,2},{2,1},{3,0},{4,7},{5,6},{6,5},{7,4},{8,11},{9,10},{10,... | collective-permute-start | bytes 1572872 | tf_op jit(solution)/shard_map/ppermute | solution.py:284
  369.1 49.1 %collective-permute-start.12 = (bf16[2,2,16,32,128]{4,3,2,1,0:T(8,128)(2,1)}, bf16[2,2,16,32,128]{4,3,2,1,0:T(8,128)(2,1)}, u32[]{:S(2)}, u32[]{:S(2)}) collective-permute-start(bf16[2,2,16,32,128]{4,3,2,1,0:T(8,128)(2,1)} %get-tuple-element.107), channel_id=1, source_target_pairs={{0,2},{1,3},{2,0},{3,1},{4,6},{5,7},{6,4},{7,5},{8,10},{9,11},{10,... | collective-permute-start | bytes 1572872 | tf_op jit(solution)/shard_map/ppermute | solution.py:284
  369.2 51.8 %collective-permute-start.13 = (bf16[2,2,16,32,128]{4,3,2,1,0:T(8,128)(2,1)}, bf16[2,2,16,32,128]{4,3,2,1,0:T(8,128)(2,1)}, u32[]{:S(2)}, u32[]{:S(2)}) collective-permute-start(bf16[2,2,16,32,128]{4,3,2,1,0:T(8,128)(2,1)} %get-tuple-element.108), channel_id=1, source_target_pairs={{0,1},{1,0},{2,3},{3,2},{4,5},{5,4},{6,7},{7,6},{8,9},{9,8},{10,11... | collective-permute-start | bytes 1572872 | tf_op jit(solution)/shard_map/ppermute | solution.py:284
  414.1 33.7 %collective-permute-start.25 = (bf16[14,64,128]{2,1,0:T(8,128)(2,1)}, bf16[14,64,128]{2,1,0:T(8,128)(2,1)S(1)}, u32[]{:S(2)}, u32[]{:S(2)}) collective-permute-start(bf16[14,64,128]{2,1,0:T(8,128)(2,1)} %get-tuple-element.138), channel_id=1, source_target_pairs={{0,4},{1,5},{2,6},{3,7},{4,0},{5,1},{6,2},{7,3},{8,12},{9,13},{10,... | collective-permute-start | bytes 688136 | tf_op jit(solution)/shard_map/ppermute | solution.py:284
  416.6 31.2 %collective-permute-start.26 = (bf16[14,64,128]{2,1,0:T(8,128)(2,1)}, bf16[14,64,128]{2,1,0:T(8,128)(2,1)S(1)}, u32[]{:S(2)}, u32[]{:S(2)}) collective-permute-start(bf16[14,64,128]{2,1,0:T(8,128)(2,1)} %get-tuple-element.139), channel_id=1, source_target_pairs={{0,5},{1,4},{2,7},{3,6},{4,1},{5,0},{6,3},{7,2},{8,13},{9,12},{10,... | collective-permute-start | bytes 688136 | tf_op jit(solution)/shard_map/ppermute | solution.py:284
  416.6 31.2 %collective-permute-start.27 = (bf16[14,64,128]{2,1,0:T(8,128)(2,1)}, bf16[14,64,128]{2,1,0:T(8,128)(2,1)S(1)}, u32[]{:S(2)}, u32[]{:S(2)}) collective-permute-start(bf16[14,64,128]{2,1,0:T(8,128)(2,1)} %get-tuple-element.140), channel_id=1, source_target_pairs={{0,6},{1,7},{2,4},{3,5},{4,2},{5,3},{6,0},{7,1},{8,14},{9,15},{10,... | collective-permute-start | bytes 688136 | tf_op jit(solution)/shard_map/ppermute | solution.py:284
  418.2 29.7 %collective-permute-start.28 = (bf16[14,64,128]{2,1,0:T(8,128)(2,1)}, bf16[14,64,128]{2,1,0:T(8,128)(2,1)S(1)}, u32[]{:S(2)}, u32[]{:S(2)}) collective-permute-start(bf16[14,64,128]{2,1,0:T(8,128)(2,1)} %get-tuple-element.141), channel_id=1, source_target_pairs={{0,7},{1,6},{2,5},{3,4},{4,3},{5,2},{6,1},{7,0},{8,15},{9,14},{10,... | collective-permute-start | bytes 688136 | tf_op jit(solution)/shard_map/ppermute | solution.py:284
  451.5 12.8 %collective-permute-start.29 = (bf16[14,32,128]{2,1,0:T(8,128)(2,1)}, bf16[14,32,128]{2,1,0:T(8,128)(2,1)S(1)}, u32[]{:S(2)}, u32[]{:S(2)}) collective-permute-start(bf16[14,32,128]{2,1,0:T(8,128)(2,1)} %get-tuple-element.142), channel_id=1, source_target_pairs={{0,4},{1,5},{2,6},{3,7},{4,0},{5,1},{6,2},{7,3},{8,12},{9,13},{10,... | collective-permute-start | bytes 344072 | tf_op jit(solution)/shard_map/ppermute | solution.py:284
  459.5 16.9 %collective-permute-start.30 = (bf16[14,32,128]{2,1,0:T(8,128)(2,1)}, bf16[14,32,128]{2,1,0:T(8,128)(2,1)S(1)}, u32[]{:S(2)}, u32[]{:S(2)}) collective-permute-start(bf16[14,32,128]{2,1,0:T(8,128)(2,1)} %get-tuple-element.143), channel_id=1, source_target_pairs={{0,5},{1,4},{2,7},{3,6},{4,1},{5,0},{6,3},{7,2},{8,13},{9,12},{10,... | collective-permute-start | bytes 344072 | tf_op jit(solution)/shard_map/ppermute | solution.py:284
  460.5 18.6 %collective-permute-start.31 = (bf16[14,32,128]{2,1,0:T(8,128)(2,1)}, bf16[14,32,128]{2,1,0:T(8,128)(2,1)S(1)}, u32[]{:S(2)}, u32[]{:S(2)}) collective-permute-start(bf16[14,32,128]{2,1,0:T(8,128)(2,1)} %get-tuple-element.144), channel_id=1, source_target_pairs={{0,6},{1,7},{2,4},{3,5},{4,2},{5,3},{6,0},{7,1},{8,14},{9,15},{10,... | collective-permute-start | bytes 344072 | tf_op jit(solution)/shard_map/ppermute | solution.py:284
  462.3 18.1 %collective-permute-start.32 = (bf16[14,32,128]{2,1,0:T(8,128)(2,1)}, bf16[14,32,128]{2,1,0:T(8,128)(2,1)S(1)}, u32[]{:S(2)}, u32[]{:S(2)}) collective-permute-start(bf16[14,32,128]{2,1,0:T(8,128)(2,1)} %get-tuple-element.145), channel_id=1, source_target_pairs={{0,7},{1,6},{2,5},{3,4},{4,3},{5,2},{6,1},{7,0},{8,15},{9,14},{10,... | collective-permute-start | bytes 344072 | tf_op jit(solution)/shard_map/ppermute | solution.py:284
  463.6 17.3 %collective-permute-start.33 = (bf16[14,32,128]{2,1,0:T(8,128)(2,1)}, bf16[14,32,128]{2,1,0:T(8,128)(2,1)S(1)}, u32[]{:S(2)}, u32[]{:S(2)}) collective-permute-start(bf16[14,32,128]{2,1,0:T(8,128)(2,1)} %get-tuple-element.146), channel_id=1, source_target_pairs={{0,3},{1,2},{2,1},{3,0},{4,7},{5,6},{6,5},{7,4},{8,11},{9,10},{10,... | collective-permute-start | bytes 344072 | tf_op jit(solution)/shard_map/ppermute | solution.py:284
  464.3 18.3 %collective-permute-start.34 = (bf16[14,32,128]{2,1,0:T(8,128)(2,1)}, bf16[14,32,128]{2,1,0:T(8,128)(2,1)S(1)}, u32[]{:S(2)}, u32[]{:S(2)}) collective-permute-start(bf16[14,32,128]{2,1,0:T(8,128)(2,1)} %get-tuple-element.147), channel_id=1, source_target_pairs={{0,2},{1,3},{2,0},{3,1},{4,6},{5,7},{6,4},{7,5},{8,10},{9,11},{10,... | collective-permute-start | bytes 344072 | tf_op jit(solution)/shard_map/ppermute | solution.py:284
  476.4 6.1 %collective-permute-start.35 = (bf16[14,32,128]{2,1,0:T(8,128)(2,1)}, bf16[14,32,128]{2,1,0:T(8,128)(2,1)S(1)}, u32[]{:S(2)}, u32[]{:S(2)}) collective-permute-start(bf16[14,32,128]{2,1,0:T(8,128)(2,1)} %get-tuple-element.148), channel_id=1, source_target_pairs={{0,1},{1,0},{2,3},{3,2},{4,5},{5,4},{6,7},{7,6},{8,9},{9,8},{10,11... | collective-permute-start | bytes 344072 | tf_op jit(solution)/shard_map/ppermute | solution.py:284
  479.0 18.0 %collective-permute-start.36 = (bf16[14,64,128]{2,1,0:T(8,128)(2,1)}, bf16[14,64,128]{2,1,0:T(8,128)(2,1)S(1)}, u32[]{:S(2)}, u32[]{:S(2)}) collective-permute-start(bf16[14,64,128]{2,1,0:T(8,128)(2,1)} %get-tuple-element.155), channel_id=1, source_target_pairs={{0,3},{1,2},{2,1},{3,0},{4,7},{5,6},{6,5},{7,4},{8,11},{9,10},{10,... | collective-permute-start | bytes 688136 | tf_op jit(solution)/shard_map/ppermute | solution.py:284
  480.4 8.9 %collective-permute-start.39 = (bf16[14,32,128]{2,1,0:T(8,128)(2,1)}, bf16[14,32,128]{2,1,0:T(8,128)(2,1)S(1)}, u32[]{:S(2)}, u32[]{:S(2)}) collective-permute-start(bf16[14,32,128]{2,1,0:T(8,128)(2,1)} %get-tuple-element.163), channel_id=1, source_target_pairs={{0,3},{1,2},{2,1},{3,0},{4,7},{5,6},{6,5},{7,4},{8,11},{9,10},{10,... | collective-permute-start | bytes 344072 | tf_op jit(solution)/shard_map/ppermute | solution.py:284
  481.0 16.1 %collective-permute-start.37 = (bf16[14,64,128]{2,1,0:T(8,128)(2,1)}, bf16[14,64,128]{2,1,0:T(8,128)(2,1)S(1)}, u32[]{:S(2)}, u32[]{:S(2)}) collective-permute-start(bf16[14,64,128]{2,1,0:T(8,128)(2,1)} %get-tuple-element.156), channel_id=1, source_target_pairs={{0,2},{1,3},{2,0},{3,1},{4,6},{5,7},{6,4},{7,5},{8,10},{9,11},{10,... | collective-permute-start | bytes 688136 | tf_op jit(solution)/shard_map/ppermute | solution.py:284
  482.5 14.5 %collective-permute-start.38 = (bf16[14,64,128]{2,1,0:T(8,128)(2,1)}, bf16[14,64,128]{2,1,0:T(8,128)(2,1)S(1)}, u32[]{:S(2)}, u32[]{:S(2)}) collective-permute-start(bf16[14,64,128]{2,1,0:T(8,128)(2,1)} %get-tuple-element.157), channel_id=1, source_target_pairs={{0,1},{1,0},{2,3},{3,2},{4,5},{5,4},{6,7},{7,6},{8,9},{9,8},{10,11... | collective-permute-start | bytes 688136 | tf_op jit(solution)/shard_map/ppermute | solution.py:284
  482.6 14.4 %collective-permute-start.40 = (bf16[14,32,128]{2,1,0:T(8,128)(2,1)}, bf16[14,32,128]{2,1,0:T(8,128)(2,1)S(1)}, u32[]{:S(2)}, u32[]{:S(2)}) collective-permute-start(bf16[14,32,128]{2,1,0:T(8,128)(2,1)} %get-tuple-element.164), channel_id=1, source_target_pairs={{0,2},{1,3},{2,0},{3,1},{4,6},{5,7},{6,4},{7,5},{8,10},{9,11},{10,... | collective-permute-start | bytes 344072 | tf_op jit(solution)/shard_map/ppermute | solution.py:284
  489.3 7.7 %collective-permute-start.41 = (bf16[14,32,128]{2,1,0:T(8,128)(2,1)}, bf16[14,32,128]{2,1,0:T(8,128)(2,1)S(1)}, u32[]{:S(2)}, u32[]{:S(2)}) collective-permute-start(bf16[14,32,128]{2,1,0:T(8,128)(2,1)} %get-tuple-element.165), channel_id=1, source_target_pairs={{0,1},{1,0},{2,3},{3,2},{4,5},{5,4},{6,7},{7,6},{8,9},{9,8},{10,11... | collective-permute-start | bytes 344072 | tf_op jit(solution)/shard_map/ppermute | solution.py:284
  (28 other events, 528.2 us)
